TPU v7x, 128 devices: a whole 4x4x4 slice. The times are simulated.
128 devices in a mesh: dp: 16 (over y, x_hi, core), tensor: 8 (over x_lo, z).
Axes of the slice: x: 4 (x_hi: 2, x_lo: 2; x = x_hi * 2 + x_lo), y: 4, z: 4, core: 2. Of those that a mesh axis runs over, the one named last changes fastest.
Arguments:
- tokens: bfloat16 [32768, 1024], P(('dp', 'tensor')), may hold values from -6 to 6
- lengths: int32 [16, 3], P('dp'), may hold values from 1 to 1536, 2048 in all within a row
- token_order: int32 [16, 2048], P('dp'), may hold values from 0 to 2047, each once within a row
- routes: int32 [32768, 8], P(('dp', 'tensor')), may hold values from 0 to 31, all different within a row; in each aligned block of 256 rows (0 to 255, 256 to 511, ...) at most 80 rows name the same one
- cotangent: bfloat16 [32768, 1024], P(('dp', 'tensor')), may hold values from -6 to 6
- attn_gain: bfloat16 [1024], P(('dp', 'tensor')), may hold values from 0.099609375 to 1.8984375
- ffn_gain: bfloat16 [1024], P(('dp', 'tensor')), may hold values from 0.099609375 to 1.8984375
- router: bfloat16 [1024, 32], P(('dp', 'tensor')), may hold values from -0.09375 to 0.09375
- w_query: bfloat16 [1024, 1024], P('dp', 'tensor'), may hold values from -0.1875 to 0.1875
- w_key: bfloat16 [1024, 512], P('dp', 'tensor'), may hold values from -0.1875 to 0.1875
- w_value: bfloat16 [1024, 512], P('dp', 'tensor'), may hold values from -0.1875 to 0.1875
- w_output: bfloat16 [1024, 1024], P('tensor', 'dp'), may hold values from -0.75 to 0.75
- query_gain: bfloat16 [16, 64], P('tensor', 'dp'), may hold values from 0.099609375 to 1.8984375
- key_gain: bfloat16 [8, 64], P('tensor', 'dp'), may hold values from 0.099609375 to 1.8984375
- w_gate: bfloat16 [32, 1024, 512], P('tensor', 'dp'), may hold values from -0.1875 to 0.1875
- w_up: bfloat16 [32, 1024, 512], P('tensor', 'dp'), may hold values from -0.1875 to 0.1875
- w_down: bfloat16 [32, 512, 1024], P('tensor', None, 'dp'), may hold values from -0.75 to 0.75
Outputs:
- layer_out: float32 [32768, 1024], P(('dp', 'tensor'))
- grad_tokens: float32 [32768, 1024], P(('dp', 'tensor'))
- grad_attn_gain: float32 [1024], P(('dp', 'tensor'))
- grad_ffn_gain: float32 [1024], P(('dp', 'tensor'))
- grad_router: float32 [1024, 32], P(('dp', 'tensor'))
- grad_w_query: float32 [1024, 1024], P('dp', 'tensor')
- grad_w_key: float32 [1024, 512], P('dp', 'tensor')
- grad_w_value: float32 [1024, 512], P('dp', 'tensor')
- grad_w_output: float32 [1024, 1024], P('tensor', 'dp')
- grad_query_gain: float32 [16, 64], P('tensor', 'dp')
- grad_key_gain: float32 [8, 64], P('tensor', 'dp')
- grad_w_gate: float32 [32, 1024, 512], P('tensor', 'dp')
- grad_w_up: float32 [32, 1024, 512], P('tensor', 'dp')
- grad_w_down: float32 [32, 512, 1024], P('tensor', None, 'dp')
Inputs may be any that keep to these rules, and one draw needn't show every extreme that they name: `token_order`: each row is a permutation: the rows of group g hold the places of its packed stream. Each row holds 3 lengths summing to 2048; the longest is exactly 1536. `routes`: each row names 8 different experts; in the 256 rows of one device no expert is named more than 80 times, a bound that some block reaches.
All inputs are finite; a program needn't handle non-finite values.
Results may differ from a plain program's by a relative error of at most 0.028.
Values may be sent and summed in bfloat16 or wider, within the bound.
A program may use at most 192 MiB of HBM per device.

v0:
```python
import jax
import jax.numpy as jnp
from jax import lax
from jax.sharding import PartitionSpec as P

CAP = 80


epsilon = 1e-06
rotary_base = 10000.0
masked_score = -1e30


def in_one_piece(arrays, axis, dim, along):
    widths = [a.shape[along] for a in arrays]
    both = jnp.concatenate(arrays, axis=along)
    whole = lax.all_gather(both, axis, axis=dim, tiled=True)
    return tuple(jnp.split(whole, [sum(widths[:k]) for k in range(1, len(widths))], axis=along))


def split_up(value, dim, size):
    before, after = (value.shape[:dim], value.shape[dim + 1 :])
    return jnp.moveaxis(value.reshape(*before, size, -1, *after), dim, 0)


def sent_and_summed(value, axis, dim):
    size = lax.axis_size(axis)
    pieces = lax.all_to_all(split_up(value, dim, size), axis, 0, 0, tiled=True)
    return jnp.sum(pieces, axis=0)


def side_by_side(arrays, axis, dim, along):
    both = jnp.concatenate(arrays, axis=along)
    whole, at, done = (lax.psum_scatter(both, axis, scatter_dimension=dim, tiled=True), 0, [])
    for a in arrays:
        done.append(lax.slice_in_dim(whole, at, at + a.shape[along], axis=along))
        at += a.shape[along]
    return tuple(done)


def rms_scale(vector, scales):
    return vector * lax.rsqrt(jnp.mean(vector * vector, axis=-1, keepdims=True) + epsilon) * scales


def rotate(vector, positions):
    half_width = vector.shape[-1] // 2
    frequency = rotary_base ** (-2.0 * jnp.arange(half_width, dtype=jnp.float32) / vector.shape[-1])
    angles = positions.astype(jnp.float32)[:, None, None] * frequency[None, None, :]
    cosine_part = jnp.cos(angles)
    sine_part = jnp.sin(angles)
    first_half = vector[..., :half_width]
    second_half = vector[..., half_width:]
    return jnp.concatenate(
        [
            first_half * cosine_part - second_half * sine_part,
            second_half * cosine_part + first_half * sine_part,
        ],
        axis=-1,
    )


def places(stream, seq_lengths):
    seq_ends = jnp.cumsum(seq_lengths)
    segment = jnp.sum((stream[:, None] >= seq_ends[None, :]).astype(jnp.int32), axis=1)
    owner_table = segment[:, None] == jnp.arange(seq_lengths.shape[0], dtype=jnp.int32)[None, :]
    seq_start = jnp.sum(jnp.where(owner_table, (seq_ends - seq_lengths)[None, :], 0), axis=1)
    return (segment, stream - seq_start)


def per_device(
    tokens,
    lengths,
    token_order,
    routes,
    cotangent,
    attn_gain,
    ffn_gain,
    router,
    w_query,
    w_key,
    w_value,
    w_output,
    query_gain,
    key_gain,
    w_gate,
    w_up,
    w_down,
):
    local_rows, model_width = tokens.shape
    group_rows = local_rows * lax.axis_size("tensor")
    experts = router.shape[1]
    top_count = routes.shape[1]
    capacity = CAP
    gains_attn, gains_ffn, router_full = (
        lax.all_gather(attn_gain, ("dp", "tensor"), axis=0, tiled=True),
        lax.all_gather(ffn_gain, ("dp", "tensor"), axis=0, tiled=True),
        lax.all_gather(router, ("dp", "tensor"), axis=0, tiled=True),
    )
    (
        query_full,
        key_full,
        value_full,
        output_full,
        qgain_full,
        kgain_full,
        gate_full,
        up_full,
        down_full,
    ) = (
        *in_one_piece((w_query, w_key, w_value), "dp", 0, 1),
        lax.all_gather(w_output, "dp", axis=1, tiled=True),
        *in_one_piece((query_gain, key_gain), "dp", 1, 0),
        *in_one_piece((w_gate, w_up), "dp", 1, 0),
        lax.all_gather(w_down, "dp", axis=2, tiled=True),
    )
    stream = token_order[0]
    segment, positions = places(stream, lengths[0])
    head_local = query_gain.shape[0]
    kv_local = key_gain.shape[0]
    repeat = head_local // kv_local
    head_dim = qgain_full.shape[1]
    scale_factor = head_dim ** (-0.5)
    inputs = tokens.astype(jnp.float32)
    normed, attn_norm_pull = jax.vjp(rms_scale, inputs, gains_attn.astype(jnp.float32))
    gathered = lax.all_gather(normed.astype(jnp.bfloat16), "tensor", axis=0, tiled=True)
    query_proj = jnp.dot(gathered, query_full, preferred_element_type=jnp.float32)
    key_proj = jnp.dot(gathered, key_full, preferred_element_type=jnp.float32)
    value_proj = jnp.dot(gathered, value_full, preferred_element_type=jnp.float32)

    def prepare(query_in, key_in, query_scales, key_scales):
        query_shaped = query_in.reshape(group_rows, head_local, head_dim)
        key_shaped = key_in.reshape(group_rows, kv_local, head_dim)
        return (
            rotate(rms_scale(query_shaped, query_scales), positions),
            rotate(rms_scale(key_shaped, key_scales), positions),
        )

    (query_rot, key_rot), prepare_pull = jax.vjp(
        prepare,
        query_proj,
        key_proj,
        qgain_full.astype(jnp.float32),
        kgain_full.astype(jnp.float32),
    )
    query_low = query_rot.astype(jnp.bfloat16).reshape(group_rows, kv_local, repeat, head_dim)
    key_low = key_rot.astype(jnp.bfloat16)
    value_low = value_proj.astype(jnp.bfloat16).reshape(group_rows, kv_local, head_dim)
    block_len = min(512, group_rows)
    start_rows = jnp.arange(group_rows // block_len, dtype=jnp.int32) * block_len

    def scores_for(start_row):
        query_block = lax.dynamic_slice_in_dim(query_low, start_row, block_len, 0)
        seg_block = lax.dynamic_slice_in_dim(segment, start_row, block_len, 0)
        place_block = lax.dynamic_slice_in_dim(stream, start_row, block_len, 0)
        raw_scores = (
            jnp.einsum("qkrd,skd->krqs", query_block, key_low, preferred_element_type=jnp.float32)
            * scale_factor
        )
        allowed = (seg_block[:, None] == segment[None, :]) & (
            stream[None, :] <= place_block[:, None]
        )
        return (jnp.where(allowed[None, None], raw_scores, masked_score), query_block)

    def forward_block(start_row):
        scores, _ = scores_for(start_row)
        row_peak = jnp.max(scores, axis=-1, keepdims=True)
        exponent = jnp.exp(scores - row_peak)
        row_total = jnp.sum(exponent, axis=-1, keepdims=True)
        prob_low = (exponent / row_total).astype(jnp.bfloat16)
        mixed_block = jnp.einsum(
            "krqs,skd->qkrd", prob_low, value_low, preferred_element_type=jnp.float32
        )
        return (
            mixed_block.reshape(block_len, head_local * head_dim).astype(jnp.bfloat16),
            row_peak + jnp.log(row_total),
        )

    mixed_blocks, log_totals = lax.map(forward_block, start_rows)
    mixed_low = mixed_blocks.reshape(group_rows, head_local * head_dim)
    hidden = inputs + sent_and_summed(
        jnp.dot(mixed_low, output_full, preferred_element_type=jnp.float32), "tensor", 0
    )
    normed2, ffn_norm_pull = jax.vjp(rms_scale, hidden, gains_ffn.astype(jnp.float32))
    normed2_low = normed2.astype(jnp.bfloat16)
    logits = jnp.dot(normed2_low, router_full, preferred_element_type=jnp.float32)
    choose = routes[:, :, None] == jnp.arange(experts, dtype=jnp.int32)[None, None, :]
    choose_float = choose.astype(jnp.float32)
    chosen = jnp.sum(choose_float * logits[:, None, :], axis=2)
    gate_probs, gate_pull = jax.vjp(lambda chosen_in: jax.nn.softmax(chosen_in, axis=-1), chosen)
    flat_choose = choose.reshape(local_rows * top_count, experts).astype(jnp.int32)
    slot_rank = jnp.sum(flat_choose * (jnp.cumsum(flat_choose, axis=0) - 1), axis=1)
    slot_of = routes.reshape(-1) * capacity + slot_rank
    pick_table = jnp.arange(experts * capacity, dtype=jnp.int32)[:, None] == slot_of[None, :]
    dispatch_table = jnp.any(
        pick_table.reshape(experts * capacity, local_rows, top_count), axis=2
    ).astype(jnp.bfloat16)
    assignment_ids = jnp.arange(local_rows * top_count, dtype=jnp.int32) + 1
    slot_source = jnp.sum(jnp.where(pick_table, assignment_ids[None, :], 0), axis=1)
    send_rows = jnp.dot(dispatch_table, normed2_low, preferred_element_type=jnp.bfloat16)
    received = lax.all_to_all(
        send_rows.reshape(experts, capacity, model_width),
        "tensor",
        split_axis=0,
        concat_axis=1,
        tiled=True,
    )
    gate_act = jnp.einsum("erd,edf->erf", received, gate_full, preferred_element_type=jnp.float32)
    up_act = jnp.einsum("erd,edf->erf", received, up_full, preferred_element_type=jnp.float32)
    inner_act, inner_pull = jax.vjp(
        lambda gate_in, up_in: jax.nn.silu(gate_in) * up_in, gate_act, up_act
    )
    inner_low = inner_act.astype(jnp.bfloat16)
    result_low = jnp.einsum(
        "erf,efd->erd", inner_low, down_full, preferred_element_type=jnp.float32
    ).astype(jnp.bfloat16)
    returned = lax.all_to_all(result_low, "tensor", split_axis=1, concat_axis=0, tiled=True)
    picked = jnp.take(returned.reshape(experts * capacity, model_width), slot_of, axis=0).astype(
        jnp.float32
    )
    picked = picked.reshape(local_rows, top_count, model_width)
    layer_out = hidden + jnp.sum(gate_probs[:, :, None] * picked, axis=1)
    upstream = cotangent.astype(jnp.float32)
    gate_grad = jnp.sum(upstream[:, None, :] * picked, axis=2)
    (chosen_grad,) = gate_pull(gate_grad)
    slot_grad = (
        (gate_probs[:, :, None] * upstream[:, None, :])
        .astype(jnp.bfloat16)
        .reshape(local_rows * top_count, model_width)
    )
    padded = jnp.concatenate([jnp.zeros((1, model_width), jnp.bfloat16), slot_grad], axis=0)
    back_send = jnp.take(padded, slot_source, axis=0).reshape(experts, capacity, model_width)
    back_received = lax.all_to_all(back_send, "tensor", split_axis=0, concat_axis=1, tiled=True)
    down_grad_part = jnp.einsum(
        "erf,erd->efd", inner_low, back_received, preferred_element_type=jnp.float32
    )
    inner_grad = jnp.einsum(
        "erd,efd->erf", back_received, down_full, preferred_element_type=jnp.float32
    )
    gate_act_grad, up_act_grad = inner_pull(inner_grad)
    gate_grad_low = gate_act_grad.astype(jnp.bfloat16)
    up_grad_low = up_act_grad.astype(jnp.bfloat16)
    gate_grad_part = jnp.einsum(
        "erd,erf->edf", received, gate_grad_low, preferred_element_type=jnp.float32
    )
    up_grad_part = jnp.einsum(
        "erd,erf->edf", received, up_grad_low, preferred_element_type=jnp.float32
    )
    copy_grad = jnp.einsum(
        "erf,edf->erd", gate_grad_low, gate_full, preferred_element_type=jnp.float32
    )
    copy_grad = copy_grad + jnp.einsum(
        "erf,edf->erd", up_grad_low, up_full, preferred_element_type=jnp.float32
    )
    expert_sums = None
    expert_sums = (
        lax.psum_scatter(gate_grad_part, "dp", scatter_dimension=1, tiled=True),
        lax.psum_scatter(up_grad_part, "dp", scatter_dimension=1, tiled=True),
        lax.psum_scatter(down_grad_part, "dp", scatter_dimension=2, tiled=True),
    )
    back_tokens = lax.all_to_all(
        copy_grad.astype(jnp.bfloat16), "tensor", split_axis=1, concat_axis=0, tiled=True
    )
    normed2_grad = jnp.einsum(
        "sl,sd->ld",
        dispatch_table,
        back_tokens.reshape(experts * capacity, model_width),
        preferred_element_type=jnp.float32,
    )
    logit_grad = jnp.sum(choose_float * chosen_grad[:, :, None], axis=1).astype(jnp.bfloat16)
    normed2_grad = normed2_grad + jnp.einsum(
        "le,de->ld", logit_grad, router_full, preferred_element_type=jnp.float32
    )
    router_grad_part = jnp.einsum(
        "ld,le->de", normed2_low, logit_grad, preferred_element_type=jnp.float32
    )
    hidden_norm_grad, ffn_gain_part = ffn_norm_pull(normed2_grad)
    hidden_grad = upstream + hidden_norm_grad
    branch_all = lax.all_gather(hidden_grad.astype(jnp.bfloat16), "tensor", axis=0, tiled=True)
    mixed_grad = jnp.einsum(
        "gd,hd->gh", branch_all, output_full, preferred_element_type=jnp.float32
    ).astype(jnp.bfloat16)
    output_grad_part = jnp.einsum(
        "gh,gd->hd", mixed_low, branch_all, preferred_element_type=jnp.float32
    )
    mixed_grad_heads = mixed_grad.reshape(group_rows, kv_local, repeat, head_dim)

    def backward_block(totals, block_item):
        key_total, value_total = totals
        start_row, log_total = block_item
        scores, query_block = scores_for(start_row)
        probability = jnp.exp(scores - log_total)
        prob_low = probability.astype(jnp.bfloat16)
        grad_block = lax.dynamic_slice_in_dim(mixed_grad_heads, start_row, block_len, 0)
        value_total = value_total + jnp.einsum(
            "krqs,qkrd->skd", prob_low, grad_block, preferred_element_type=jnp.float32
        )
        prob_grad = jnp.einsum(
            "qkrd,skd->krqs", grad_block, value_low, preferred_element_type=jnp.float32
        )
        inner_sum = jnp.sum(probability * prob_grad, axis=-1, keepdims=True)
        score_grad = (probability * (prob_grad - inner_sum)).astype(jnp.bfloat16)
        key_total = (
            key_total
            + jnp.einsum(
                "krqs,qkrd->skd", score_grad, query_block, preferred_element_type=jnp.float32
            )
            * scale_factor
        )
        query_part = (
            jnp.einsum("krqs,skd->qkrd", score_grad, key_low, preferred_element_type=jnp.float32)
            * scale_factor
        )
        return ((key_total, value_total), query_part)

    zero_heads = jnp.zeros((group_rows, kv_local, head_dim), jnp.float32)
    (key_rot_grad, value_grad), query_parts = lax.scan(
        backward_block, (zero_heads, zero_heads), (start_rows, log_totals)
    )
    query_rot_grad = query_parts.reshape(group_rows, head_local, head_dim)
    query_proj_grad, key_proj_grad, qgain_part, kgain_part = prepare_pull(
        (query_rot_grad, key_rot_grad)
    )
    query_grad_low = query_proj_grad.astype(jnp.bfloat16)
    key_grad_low = key_proj_grad.astype(jnp.bfloat16)
    value_grad_low = value_grad.reshape(group_rows, kv_local * head_dim).astype(jnp.bfloat16)
    query_w_part = jnp.einsum(
        "gd,gh->dh", gathered, query_grad_low, preferred_element_type=jnp.float32
    )
    key_w_part = jnp.einsum("gd,gh->dh", gathered, key_grad_low, preferred_element_type=jnp.float32)
    value_w_part = jnp.einsum(
        "gd,gh->dh", gathered, value_grad_low, preferred_element_type=jnp.float32
    )
    summed = jnp.einsum("gh,dh->gd", query_grad_low, query_full, preferred_element_type=jnp.float32)
    summed = summed + jnp.einsum(
        "gh,dh->gd", key_grad_low, key_full, preferred_element_type=jnp.float32
    )
    normed_grad = sent_and_summed(
        summed
        + jnp.einsum("gh,dh->gd", value_grad_low, value_full, preferred_element_type=jnp.float32),
        "tensor",
        0,
    )
    input_norm_grad, attn_gain_part = attn_norm_pull(normed_grad)
    grad_tokens = hidden_grad + input_norm_grad
    attn_sums = (
        *side_by_side((query_w_part, key_w_part, value_w_part), "dp", 0, 1),
        lax.psum_scatter(output_grad_part, "dp", scatter_dimension=1, tiled=True),
        *side_by_side((qgain_part, kgain_part), "dp", 1, 0),
    )
    weight_sums = tuple(attn_sums) + tuple(expert_sums)
    small_sums = (
        lax.psum_scatter(attn_gain_part, ("dp", "tensor"), scatter_dimension=0, tiled=True),
        lax.psum_scatter(ffn_gain_part, ("dp", "tensor"), scatter_dimension=0, tiled=True),
        lax.psum_scatter(router_grad_part, ("dp", "tensor"), scatter_dimension=0, tiled=True),
    )
    return (layer_out, grad_tokens) + tuple(small_sums) + weight_sums


def solution(mesh):
    return jax.shard_map(
        per_device,
        mesh=mesh,
        in_specs=(
            P(("dp", "tensor"), None),
            P("dp", None),
            P("dp", None),
            P(("dp", "tensor"), None),
            P(("dp", "tensor"), None),
            P(("dp", "tensor")),
            P(("dp", "tensor")),
            P(("dp", "tensor"), None),
            P("dp", "tensor"),
            P("dp", "tensor"),
            P("dp", "tensor"),
            P("tensor", "dp"),
            P("tensor", "dp"),
            P("tensor", "dp"),
            P("tensor", "dp", None),
            P("tensor", "dp", None),
            P("tensor", None, "dp"),
        ),
        out_specs=(
            P(("dp", "tensor"), None),
            P(("dp", "tensor"), None),
            P(("dp", "tensor")),
            P(("dp", "tensor")),
            P(("dp", "tensor"), None),
            P("dp", "tensor"),
            P("dp", "tensor"),
            P("dp", "tensor"),
            P("tensor", "dp"),
            P("tensor", "dp"),
            P("tensor", "dp"),
            P("tensor", "dp", None),
            P("tensor", "dp", None),
            P("tensor", None, "dp"),
        ),
        check_vma=False,
    )
```

profile of v0, /device:TPU:0, one launch (start us, length us, event | category | flops | bytes accessed | tf_op | source)
XLA Modules:
  0.0 1639.5 jit_solution(1906649411254221383)
XLA Ops:
  10.7 68.2 %all-reduce.12 = (bf16[1024]{0:T(1024)(128)(2,1)S(1)}, bf16[1024]{0:T(1024)(128)(2,1)S(1)}) all-reduce(bf16[1024]{0:T(1024)(128)(2,1)S(1)} %dynamic-update-slice, bf16[1024]{0:T(1024)(128)(2,1)S(1)} %dynamic-update-slice.1), channel_id=1, replica_groups=mesh['dp'=16,'tensor'=8] {'dp','tensor'}, use_global_device_ids=true, to_apply=%add.5 | all-reduce | flops 2048 | bytes 8192
  83.1 21.6 %all-gather = bf16[16,4,3]{2,1,0:T(4,128)(2,1)S(1)} all-gather(bf16[1,4,3]{2,1,0:T(4,128)(2,1)S(1)} %bitcast.409), channel_id=1, replica_groups=mesh['dp'=16,'tensor'=8] {'dp'}, dimensions={0}, use_global_device_ids=true | all-gather | bytes 408 | tf_op jit(solution)/shard_map/all_gather | solution.py:17
  107.9 22.8 %all_gather.34 = bf16[128,1024]{0,1:T(8,128)(2,1)S(1)} all-gather(bf16[128,64]{0,1:T(8,128)(2,1)} %param.32), channel_id=1, replica_groups=mesh['dp'=16,'tensor'=8] {'dp'}, dimensions={1}, use_global_device_ids=true | all-gather | bytes 278528 | tf_op jit(solution)/shard_map/all_gather | solution.py:111
  131.7 25.1 %all_gather.32 = bf16[1024,256]{1,0:T(8,128)(2,1)S(1)} all-gather(bf16[64,256]{1,0:T(8,128)(2,1)S(1)} %pad_maximum_fusion.4), channel_id=1, replica_groups=mesh['dp'=16,'tensor'=8] {'dp'}, dimensions={0}, use_global_device_ids=true | all-gather | bytes 557056 | tf_op jit(solution)/shard_map/all_gather | solution.py:17
  167.3 46.2 %while.27 = (s32[]{:T(128)}, bf16[4,512,128]{2,1,0:T(8,128)(2,1)S(1)}, f32[4,1,2,512,1]{3,2,4,1,0:T(2,128)}, s32[4]{0:T(128)S(1)}, s32[2048]{0:T(1024)S(1)}, /*i...) while((s32[]{:T(128)}, ...), condition=%wide.region_9.10_spmd, body=%wide.region_6.9_spmd.sunk | while | flops 565246976 | bytes 30732488 | solution.py:178
  225.0 9.1 reduce-window.11
  237.3 407.3 %all_gather.36 = bf16[1024,32]{1,0:T(8,128)(2,1)S(1)} all-gather(bf16[8,32]{1,0:T(8,128)(2,1)S(1)} %copy-done.81), channel_id=1, replica_groups=mesh['dp'=16,'tensor'=8] {'dp','tensor'}, dimensions={0}, use_global_device_ids=true | all-gather | bytes 66048 | tf_op jit(solution)/shard_map/all_gather | solution.py:97
  657.2 14.8 gather_fusion.1
  683.3 13.7 fusion.55
  701.7 25.6 %all-to-all-done.3 = bf16[32,80,1024]{2,1,0:T(8,128)(2,1)} async-done(((bf16[32,80,1024]{2,1,0:T(8,128)(2,1)}), bf16[32,80,1024]{2,1,0:T(8,128)(2,1)}, u32[]{:S(2)}, u32[]{:S(2)}) %all-to-all-start.3) | async-done | bytes 5242912 | tf_op jit(solution)/shard_map/all_to_all | solution.py:232
  737.7 53.0 %all-to-all-done.1 = bf16[32,80,1024]{2,1,0:T(8,128)(2,1)} async-done(((bf16[32,80,1024]{2,1,0:T(8,128)(2,1)}), bf16[32,80,1024]{2,1,0:T(8,128)(2,1)}, u32[]{:S(2)}, u32[]{:S(2)}) %all-to-all-start.1) | async-done | bytes 5242912 | tf_op jit(solution)/shard_map/all_to_all | solution.py:200
  814.7 10.1 fusion.60
  864.6 37.1 %all-to-all-done.2 = bf16[4,640,1024]{2,0,1:T(4,128)(2,1)} async-done(((bf16[4,640,1024]{2,0,1:T(4,128)(2,1)}), bf16[4,640,1024]{2,0,1:T(4,128)(2,1)}, u32[]{:S(2)}, u32[]{:S(2)}) %all-to-all-start.2) | async-done | bytes 5242912 | tf_op jit(solution)/shard_map/all_to_all | solution.py:216
  913.5 14.6 gather_fusion
  931.6 34.8 %all-to-all-done.4 = bf16[4,640,1024]{2,0,1:T(4,128)(2,1)} async-done(((bf16[4,640,1024]{2,0,1:T(4,128)(2,1)}), bf16[4,640,1024]{2,0,1:T(4,128)(2,1)}, u32[]{:S(2)}, u32[]{:S(2)}) %all-to-all-start.4) | async-done | bytes 5242912 | tf_op jit(solution)/shard_map/all_to_all | solution.py:260
  976.9 47.2 %all-gather.12.cloned.1.call-done = bf16[2048,1024]{1,0:T(8,128)(2,1)} async-done(((bf16[256,1024]{1,0:T(8,128)(2,1)}), bf16[2048,1024]{1,0:T(8,128)(2,1)}) %all-gather.12.cloned.1.call-update) | async-done | bytes 4194320 | tf_op jit(solution)/shard_map/all_gather | solution.py:278
  1028.0 96.9 %while.28 = (s32[]{:T(128)}, f32[2048,1,64]{0,2,1:T(8,128)S(1)}, f32[2048,1,64]{0,2,1:T(8,128)}, f32[4,512,1,2,64]{1,0,4,3,2:T(4,128)}, s32[4]{0:T(128)S(1)}, /*...) while((s32[]{:T(128)}, f32[2048,1,64]{0,2,1:T(8,128)S(1)}, ...), condition=%wide.region_27.28_spmd.clone, body=%wide.region_25.27_spmd.clone.sunk | while | flops 1377500160 | bytes 71885048 | solution.py:316
  1139.0 9.1 fusion.145
  1160.6 9.4 fusion.144
  1193.3 116.2 %all-reduce.10 = f32[3,64]{1,0:T(4,128)S(1)} all-reduce(f32[3,64]{1,0:T(4,128)S(1)} %pad_maximum_fusion.5), channel_id=7, replica_groups=mesh['dp'=16,'tensor'=8] {'dp'}, use_global_device_ids=true, to_apply=%region_41.42.clone | all-reduce | flops 192 | bytes 1536
  1325.8 67.0 %all-reduce.11 = (f32[1024]{0:T(1024)S(1)}, f32[1024]{0:T(1024)S(1)}) all-reduce(f32[1024]{0:T(1024)S(1)} %get-tuple-element.255, f32[1024]{0:T(1024)S(1)} %copy-done.64), channel_id=2, replica_groups=mesh['dp'=16,'tensor'=8] {'dp','tensor'}, use_global_device_ids=true, to_apply=%region_33.34.clone | all-reduce | flops 2048 | bytes 16384
  1397.4 60.4 %reduce-scatter.11.cloned.1.call-done = f32[4,64,512]{2,1,0:T(8,128)} async-done(((f32[4,1024,512]{2,1,0:T(8,128)}), f32[4,64,512]{2,1,0:T(8,128)}) %reduce-scatter.11.cloned.1.call-update) | async-done | bytes 524304 | tf_op jit(solution)/shard_map/reduce_scatter | solution.py:256
  1457.9 106.0 %reduce-scatter.13.cloned.1.call-done = f32[4,64,512]{2,1,0:T(8,128)} async-done(((f32[4,1024,512]{2,1,0:T(8,128)}), f32[4,64,512]{2,1,0:T(8,128)}) %reduce-scatter.13.cloned.1.call-update) | async-done | bytes 524304 | tf_op jit(solution)/shard_map/reduce_scatter | solution.py:257
  1563.9 68.3 %reduce-scatter.9.cloned.1.call-done = f32[128,64]{0,1:T(8,128)} async-done(((f32[128,1024]{0,1:T(8,128)}), f32[128,64]{0,1:T(8,128)}) %reduce-scatter.9.cloned.1.call-update) | async-done | bytes 32784 | tf_op jit(solution)/shard_map/reduce_scatter | solution.py:347
  (441 shorter events, 364.7 us)
Async XLA Ops:
  7.2 150.7 %all-gather.6.cloned.1.call-start = ((), (), s32[]{:S(2)}) async-start(), calls=%async_computation.11 | async-start | bytes 4718592 | tf_op jit(solution)/shard_map/all_gather | solution.py:125
  81.6 715.0 %all-gather.10.cloned.1.call-start = ((), (), s32[]{:S(2)}) async-start(), calls=%async_computation.13 | async-start | bytes 4456448 | tf_op jit(solution)/shard_map/all_gather | solution.py:114
  218.2 426.5 %all-to-all-start = ((f32[8,256,1024]{2,1,0:T(8,128)}), f32[8,256,1024]{2,1,0:T(8,128)}, u32[]{:S(2)}, u32[]{:S(2)}) async-start(f32[8,256,1024]{2,1,0:T(8,128)} %fusion.109), calls=%async_computation | async-start | bytes 16777216 | tf_op jit(solution)/shard_map/all_to_all | solution.py:28
  223.6 582.0 %all-gather.8.cloned.1.call-start = ((), (), s32[]{:S(2)}) async-start(), calls=%async_computation.12 | async-start | bytes 8912896 | tf_op jit(solution)/shard_map/all_gather | solution.py:17
  224.9 749.5 %copy-start.55 = (f32[1024]{0:T(1024)}, f32[1024]{0:T(1024)S(1)}, u32[]{:S(2)}) copy-start(f32[1024]{0:T(1024)S(1)} %convert_element_type.153) | copy-start | bytes 12292
  237.3 416.1 %copy-start.16 = (f32[256,1024]{1,0:T(8,128)}, f32[256,1024]{1,0:T(8,128)S(1)}, u32[]{:S(2)}) copy-start(f32[256,1024]{1,0:T(8,128)S(1)} %convert_element_type.159) | copy-start | bytes 3145732
  237.3 412.8 %copy-start.9 = (bf16[256,1024]{1,0:T(8,128)(2,1)S(1)}, bf16[256,1024]{1,0:T(8,128)(2,1)}, u32[]{:S(2)}) copy-start(bf16[256,1024]{1,0:T(8,128)(2,1)} %param.21) | copy-start | bytes 1572868
  651.5 322.9 %copy-start.62 = (f32[256]{0:T(256)}, f32[256]{0:T(256)S(1)}, u32[]{:S(2)}) copy-start(f32[256]{0:T(256)S(1)} %fusion.133) | copy-start | bytes 3076
  678.0 49.3 %all-to-all-start.3 = ((bf16[32,80,1024]{2,1,0:T(8,128)(2,1)}), bf16[32,80,1024]{2,1,0:T(8,128)(2,1)}, u32[]{:S(2)}, u32[]{:S(2)}) async-start(bf16[32,80,1024]{2,1,0:T(8,128)(2,1)} %broadcast_select_fusion), calls=%async_computation.3 | async-start | bytes 10485760 | tf_op jit(solution)/shard_map/all_to_all | solution.py:232
  683.2 223.4 %copy-start.43 = (pred[256,8]{1,0:T(8,128)(4,1)}, pred[256,8]{1,0:T(8,128)(4,1)S(1)}, u32[]{:S(2)}) copy-start(pred[256,8]{1,0:T(8,128)(4,1)S(1)} %get-tuple-element.311) | copy-start | bytes 6148
  727.3 63.5 %all-to-all-start.1 = ((bf16[32,80,1024]{2,1,0:T(8,128)(2,1)}), bf16[32,80,1024]{2,1,0:T(8,128)(2,1)}, u32[]{:S(2)}, u32[]{:S(2)}) async-start(bf16[32,80,1024]{2,1,0:T(8,128)(2,1)} %fusion.85), calls=%async_computation.1 | async-start | bytes 10485760 | tf_op jit(solution)/shard_map/all_to_all | solution.py:200
  837.1 64.7 %all-to-all-start.2 = ((bf16[4,640,1024]{2,0,1:T(4,128)(2,1)}), bf16[4,640,1024]{2,0,1:T(4,128)(2,1)}, u32[]{:S(2)}, u32[]{:S(2)}) async-start(bf16[4,640,1024]{2,0,1:T(4,128)(2,1)} %copy.126), calls=%async_computation.2 | async-start | bytes 10485760 | tf_op jit(solution)/shard_map/all_to_all | solution.py:216
  901.8 64.6 %all-to-all-start.4 = ((bf16[4,640,1024]{2,0,1:T(4,128)(2,1)}), bf16[4,640,1024]{2,0,1:T(4,128)(2,1)}, u32[]{:S(2)}, u32[]{:S(2)}) async-start(bf16[4,640,1024]{2,0,1:T(4,128)(2,1)} %copy.130), calls=%async_computation.4 | async-start | bytes 10485760 | tf_op jit(solution)/shard_map/all_to_all | solution.py:260
  906.5 117.7 %all-gather.12.cloned.1.call-start = ((), (), s32[]{:S(2)}) async-start(), calls=%async_computation.14 | async-start | bytes 4718592 | tf_op jit(solution)/shard_map/all_gather | solution.py:278
  975.6 216.4 %all-reduce.15.cloned.1.call-start = ((), (), s32[]{:S(2)}) async-start(), calls=%async_computation.20 | async-start | bytes 1048576
  976.9 338.8 %reduce-scatter.17.cloned.1.call-start = ((), (), s32[]{:S(2)}) async-start(), calls=%async_computation.19 | async-start | bytes 1114112
  1028.0 101.5 %copy-start.46 = (f32[2048,2]{0,1:T(2,128)S(1)}, f32[2048,2]{0,1:T(2,128)}, u32[]{:S(2)}) copy-start(f32[2048,2]{0,1:T(2,128)} %copy-done.45) | copy-start | bytes 49156
  1028.0 101.5 %copy-start.70 = (f32[2,64]{1,0:T(2,128)S(1)}, f32[2,64]{1,0:T(2,128)}, u32[]{:S(2)}) copy-start(f32[2,64]{1,0:T(2,128)} %copy-done.69) | copy-start | bytes 1540
  1138.9 258.5 %reduce-scatter.15.cloned.1.call-start = ((), (), s32[]{:S(2)}) async-start(), calls=%async_computation.18 | async-start | bytes 8912896 | tf_op jit(solution)/shard_map/reduce_scatter | solution.py:258
  1148.1 309.7 %reduce-scatter.11.cloned.1.call-start = ((), (), s32[]{:S(2)}) async-start(), calls=%async_computation.16 | async-start | bytes 8912896 | tf_op jit(solution)/shard_map/reduce_scatter | solution.py:256
  1158.9 405.0 %reduce-scatter.13.cloned.1.call-start = ((), (), s32[]{:S(2)}) async-start(), calls=%async_computation.17 | async-start | bytes 8912896 | tf_op jit(solution)/shard_map/reduce_scatter | solution.py:257
  1179.3 139.4 %all-to-all-start.5 = ((f32[8,256,1024]{2,1,0:T(8,128)}), f32[8,256,1024]{2,1,0:T(8,128)}, u32[]{:S(2)}, u32[]{:S(2)}) async-start(f32[8,256,1024]{2,1,0:T(8,128)} %bitcast.383), calls=%async_computation.5 | async-start | bytes 16777216 | tf_op jit(solution)/shard_map/all_to_all | solution.py:28
  1184.4 126.3 %copy-start.39 = (bf16[4,512,128]{2,1,0:T(8,128)(2,1)S(1)}, bf16[4,512,128]{2,1,0:T(8,128)(2,1)}, u32[]{:S(2)}) copy-start(bf16[4,512,128]{2,1,0:T(8,128)(2,1)} %copy-done.38) | copy-start | bytes 1572868
  1184.4 447.8 %reduce-scatter.9.cloned.1.call-start = ((), (), s32[]{:S(2)}) async-start(), calls=%async_computation.15 | async-start | bytes 557056 | tf_op jit(solution)/shard_map/reduce_scatter | solution.py:347
  (79 other events, 1731.0 us)
Sparse Core Ops, SparseCore 0:
  81.7 51.5 all-gather.5
  135.7 53.6 all-gather.9
  227.5 98.9 all-gather.7
  975.8 48.3 all-gather.11
  1028.8 143.3 all-reduce.14
  1176.3 68.7 reduce-scatter.16
  1250.0 101.9 reduce-scatter.14
  1356.8 101.0 reduce-scatter.10
  1462.7 101.1 reduce-scatter.12
  1568.0 64.1 reduce-scatter.8
where the time goes:
time: 1650 us; the launch traced here: 1640 us
  blocking collectives  728 us (44%)
  waiting for transfers between devices  433 us (26%)
  matrix products  177 us (11%)
  local copies, waits for them, and re-layouts  131 us (8%)
  other arithmetic  107 us (6%)
  starting transfers between devices  30.1 us (2%)
  between operations  16.8 us (1%)
    all_gather x1, blocking collectives, per_device(): lax.all_gather(router, ('dp', 'tensor'), axis=0, tiled=True)  407 us
    unnamed x3, blocking collectives  251 us
    reduce_scatter x1, waiting for transfers between devices, per_device(): lax.psum_scatter(up_grad_part, 'dp', scatter_dimension=1, tiled=True)  106 us
    reduce_scatter x1, waiting for transfers between devices, per_device(): lax.psum_scatter(output_grad_part, 'dp', scatter_dimension=1, tiled=True)  68.3 us
    reduce_scatter x1, waiting for transfers between devices, per_device(): lax.psum_scatter(gate_grad_part, 'dp', scatter_dimension=1, tiled=True)  60.4 us
    all_to_all x1, waiting for transfers between devices, per_device(): lax.all_to_all(send_rows.reshape(experts, capacity, model_width), 'tensor...  53 us
    all_gather x1, waiting for transfers between devices, per_device(): lax.all_gather(hidden_grad.astype(jnp.bfloat16), 'tensor', axis=0, tiled=...  47.2 us
    all_gather x2, blocking collectives, in_one_piece(): whole = lax.all_gather(both, axis, axis=dim, tiled=True)  46.7 us
  transfers between devices with their start and end apart: 16, of which 8 were waited for; matrix products, arithmetic and copies ran while one was open for 22% of the time, Pallas kernels for 0%

commit v1 on v0

v1 whole, which is shorter than its diff:
```python
import functools

import jax
import jax.numpy as jnp
from jax import lax
from jax.experimental import pallas as pl
from jax.experimental.pallas import tpu as pltpu
from jax.sharding import PartitionSpec as P

CAP = 80
EPS = 1e-06
ROTARY_BASE = 10000.0
MASKED = -1e30
MESH = pl.DeviceIdType.MESH
bf16 = jnp.bfloat16
f32 = jnp.float32


def tiny_gather_kernel(n, x, o, send_sem, recv_sem, local_sem):
    me = lax.axis_index("tensor")
    barrier = pltpu.get_barrier_semaphore()
    for k in range(1, n):
        pl.semaphore_signal(
            barrier, inc=1, device_id={"tensor": lax.rem(me + k, n)}, device_id_type=MESH
        )
    pl.semaphore_wait(barrier, n - 1)
    own = pltpu.make_async_copy(x, o.at[me], local_sem)
    own.start()
    copies = []
    for k in range(1, n):
        copy = pltpu.make_async_remote_copy(
            src_ref=x,
            dst_ref=o.at[me],
            send_sem=send_sem.at[k],
            recv_sem=recv_sem.at[k],
            device_id={"tensor": lax.rem(me + k, n)},
            device_id_type=MESH,
        )
        copy.start()
        copies.append(copy)
    for copy in copies:
        copy.wait()
    own.wait()


def tiny_gather(x, collective_id):
    n = 8
    return pl.pallas_call(
        functools.partial(tiny_gather_kernel, n),
        out_shape=jax.ShapeDtypeStruct((n,) + x.shape, x.dtype),
        in_specs=[pl.BlockSpec(memory_space=pl.ANY)],
        out_specs=pl.BlockSpec(memory_space=pl.ANY),
        scratch_shapes=[
            pltpu.SemaphoreType.DMA((n,)),
            pltpu.SemaphoreType.DMA((n,)),
            pltpu.SemaphoreType.DMA,
        ],
        compiler_params=pltpu.CompilerParams(collective_id=collective_id, has_side_effects=True),
        name="tiny_gather",
    )(x)


def row_gather_kernel(count, *refs):
    xs, outs = refs[:count], refs[count : 2 * count]
    send_sem, recv_sem, local_sem = refs[2 * count :]
    me = lax.axis_index("tensor")
    z = lax.rem(me, 4)
    side = me // 4
    right, left = lax.rem(z + 1, 4), lax.rem(z + 3, 4)
    here, there = side * 4, (1 - side) * 4
    partner = there + z
    barrier = pltpu.get_barrier_semaphore()
    for peer in (partner, here + right, here + left):
        pl.semaphore_signal(barrier, inc=1, device_id={"tensor": peer}, device_id_type=MESH)
    pl.semaphore_wait(barrier, 3)

    def send(index, a, src, dst, peer):
        copy = pltpu.make_async_remote_copy(
            src_ref=src,
            dst_ref=dst,
            send_sem=send_sem.at[a, index],
            recv_sem=recv_sem.at[a, index],
            device_id={"tensor": peer},
            device_id_type=MESH,
        )
        copy.start()
        return copy

    owns, done = [], []
    first = []
    for a in range(count):
        x, o = xs[a], outs[a]
        own = pltpu.make_async_copy(x, o.at[me], local_sem.at[a])
        own.start()
        owns.append(own)
        first.append(
            (
                send(0, a, x, o.at[me], partner),
                send(1, a, x, o.at[me], here + right),
                send(2, a, x, o.at[me], here + left),
            )
        )
    for a in range(count):
        o = outs[a]
        half = o.shape[1] // 2
        low, high = pl.ds(0, half), pl.ds(half, half)
        to_partner, to_right, to_left = first[a]
        to_partner.wait_recv()
        pass_right = send(3, a, o.at[partner], o.at[partner], here + right)
        pass_left = send(4, a, o.at[partner], o.at[partner], here + left)
        to_right.wait_recv()
        far = [send(5, a, o.at[here + left, low], o.at[here + left, low], here + right)]
        to_left.wait_recv()
        far += [send(6, a, o.at[here + right, high], o.at[here + right, high], here + left)]
        pass_right.wait_recv()
        far += [send(7, a, o.at[there + left, low], o.at[there + left, low], here + right)]
        pass_left.wait_recv()
        far += [send(8, a, o.at[there + right, high], o.at[there + right, high], here + left)]
        done.append((far, (to_partner, to_right, to_left, pass_right, pass_left)))
    for far, near in done:
        for copy in far:
            copy.wait()
        for copy in near:
            copy.wait_send()
    for own in owns:
        own.wait()


def row_gather(arrays, collective_id):
    count = len(arrays)
    out = pl.pallas_call(
        functools.partial(row_gather_kernel, count),
        out_shape=[jax.ShapeDtypeStruct((8,) + x.shape, x.dtype) for x in arrays],
        in_specs=[pl.BlockSpec(memory_space=pl.ANY)] * count,
        out_specs=[pl.BlockSpec(memory_space=pl.ANY)] * count,
        scratch_shapes=[
            pltpu.SemaphoreType.DMA((count, 9)),
            pltpu.SemaphoreType.DMA((count, 9)),
            pltpu.SemaphoreType.DMA((count,)),
        ],
        compiler_params=pltpu.CompilerParams(collective_id=collective_id, has_side_effects=True),
        name="row_gather",
    )(*arrays)
    return out


def exchange(x):
    return lax.all_to_all(x, "tensor", 0, 0, tiled=False)


def dot(a, b, dims=((1,), (0,)), out=f32):
    return lax.dot_general(a, b, (dims, ((), ())), preferred_element_type=out)


def rms_scale(vector, scales):
    return vector * lax.rsqrt(jnp.mean(vector * vector, axis=-1, keepdims=True) + EPS) * scales


def rotate(vector, positions):
    half_width = vector.shape[-1] // 2
    frequency = ROTARY_BASE ** (-2.0 * jnp.arange(half_width, dtype=f32) / vector.shape[-1])
    angles = positions.astype(f32)[:, None, None] * frequency[None, None, :]
    cosine_part = jnp.cos(angles)
    sine_part = jnp.sin(angles)
    first_half = vector[..., :half_width]
    second_half = vector[..., half_width:]
    return jnp.concatenate(
        [
            first_half * cosine_part - second_half * sine_part,
            second_half * cosine_part + first_half * sine_part,
        ],
        axis=-1,
    )


def places(stream, seq_lengths):
    seq_ends = jnp.cumsum(seq_lengths)
    segment = jnp.sum((stream[:, None] >= seq_ends[None, :]).astype(jnp.int32), axis=1)
    owner_table = segment[:, None] == jnp.arange(seq_lengths.shape[0], dtype=jnp.int32)[None, :]
    seq_start = jnp.sum(jnp.where(owner_table, (seq_ends - seq_lengths)[None, :], 0), axis=1)
    return (segment, stream - seq_start)


def attend(query_low, key_low, value_low, segment, stream, scale):
    group_rows = query_low.shape[0]
    block_len = 512
    start_rows = jnp.arange(group_rows // block_len, dtype=jnp.int32) * block_len

    def forward_block(start_row):
        scores, _ = scores_for(query_low, key_low, segment, stream, scale, start_row, block_len)
        row_peak = jnp.max(scores, axis=-1, keepdims=True)
        exponent = jnp.exp(scores - row_peak)
        row_total = jnp.sum(exponent, axis=-1, keepdims=True)
        prob_low = (exponent / row_total).astype(bf16)
        mixed_block = jnp.einsum("rqs,sd->qrd", prob_low, value_low, preferred_element_type=f32)
        return (mixed_block.reshape(block_len, -1).astype(bf16), row_peak + jnp.log(row_total))

    mixed_blocks, log_totals = lax.map(forward_block, start_rows)
    return mixed_blocks.reshape(group_rows, -1), log_totals


def scores_for(query_low, key_low, segment, stream, scale, start_row, block_len):
    query_block = lax.dynamic_slice_in_dim(query_low, start_row, block_len, 0)
    seg_block = lax.dynamic_slice_in_dim(segment, start_row, block_len, 0)
    place_block = lax.dynamic_slice_in_dim(stream, start_row, block_len, 0)
    raw = jnp.einsum("qrd,sd->rqs", query_block, key_low, preferred_element_type=f32) * scale
    allowed = (seg_block[:, None] == segment[None, :]) & (stream[None, :] <= place_block[:, None])
    return (jnp.where(allowed[None], raw, MASKED), query_block)


def attend_back(query_low, key_low, value_low, segment, stream, scale, log_totals, mixed_grad):
    group_rows, heads, head_dim = query_low.shape
    block_len = 512
    start_rows = jnp.arange(group_rows // block_len, dtype=jnp.int32) * block_len

    def backward_block(totals, block_item):
        key_total, value_total = totals
        start_row, log_total = block_item
        scores, query_block = scores_for(
            query_low, key_low, segment, stream, scale, start_row, block_len
        )
        probability = jnp.exp(scores - log_total)
        prob_low = probability.astype(bf16)
        grad_block = lax.dynamic_slice_in_dim(mixed_grad, start_row, block_len, 0)
        value_total = value_total + jnp.einsum(
            "rqs,qrd->sd", prob_low, grad_block, preferred_element_type=f32
        )
        prob_grad = jnp.einsum("qrd,sd->rqs", grad_block, value_low, preferred_element_type=f32)
        inner_sum = jnp.sum(probability * prob_grad, axis=-1, keepdims=True)
        score_grad = (probability * (prob_grad - inner_sum)).astype(bf16)
        key_total = (
            key_total
            + jnp.einsum("rqs,qrd->sd", score_grad, query_block, preferred_element_type=f32)
            * scale
        )
        query_part = (
            jnp.einsum("rqs,sd->qrd", score_grad, key_low, preferred_element_type=f32) * scale
        )
        return ((key_total, value_total), query_part)

    zero = jnp.zeros((group_rows, head_dim), f32)
    (key_grad, value_grad), query_parts = lax.scan(
        backward_block, (zero, zero), (start_rows, log_totals)
    )
    return query_parts.reshape(group_rows, heads, head_dim), key_grad, value_grad


def per_device(
    tokens,
    lengths,
    token_order,
    routes,
    cotangent,
    attn_gain,
    ffn_gain,
    router,
    w_query,
    w_key,
    w_value,
    w_output,
    query_gain,
    key_gain,
    w_gate,
    w_up,
    w_down,
):
    rows, width = tokens.shape
    ranks = 8
    group_rows = rows * ranks
    experts, top_count = router.shape[1], routes.shape[1]
    local_experts, _, hidden_width = w_gate.shape
    head_local, kv_local, head_dim = query_gain.shape[0], key_gain.shape[0], 64
    dp_rows = w_query.shape[0]
    qkv_width = (head_local + 2 * kv_local) * head_dim
    scale = head_dim ** (-0.5)
    rank = lax.axis_index("tensor")

    wkv = jnp.concatenate([w_key, w_value], axis=1)
    small_own = jnp.concatenate([attn_gain[:, None], ffn_gain[:, None], router], axis=1)
    small_own = jnp.pad(small_own, ((0, 16 - small_own.shape[0]), (0, 128 - small_own.shape[1])))
    route_rows = routes.astype(bf16).reshape(-1, 128)
    payload = jnp.concatenate([w_query, wkv, w_output.T, small_own, route_rows], axis=0)
    gathered = tiny_gather(payload, 1)
    qkv_parts = gathered[:, : 2 * dp_rows].reshape(ranks, 2, dp_rows, 128)
    wqkv_cols = qkv_parts.transpose(2, 0, 1, 3).reshape(dp_rows, ranks * 256)
    wo_cols = gathered[:, 2 * dp_rows : 3 * dp_rows].transpose(1, 0, 2).reshape(dp_rows, -1)
    small_rows = gathered[:, 3 * dp_rows : 3 * dp_rows + 8].reshape(dp_rows, 128)
    routes_all = (
        gathered[:, 3 * dp_rows + 16 :].reshape(group_rows, top_count).astype(jnp.int32)
    )
    head_gains = jnp.concatenate([query_gain, key_gain], axis=0)
    head_gains = jnp.pad(head_gains, ((0, dp_rows - 3), (64, 60)))
    first_payload = jnp.concatenate([w_query, wkv, small_rows + head_gains], axis=1)
    first_full = lax.all_gather(first_payload, "dp", axis=0, tiled=False)
    wqkv = first_full[:, :, :256].reshape(width, 256)
    small_full = first_full[:, :, 256:].reshape(width, 128)
    gain1 = small_full[:, 0].astype(f32)
    gain2 = small_full[:, 1].astype(f32)
    router_full = small_full[:, 2 : 2 + experts]
    hg = first_full[:, :3, 256 + 64 : 256 + 68].transpose(1, 0, 2).reshape(3, head_dim)
    qgain, kgain = hg[:2].astype(f32), hg[2:].astype(f32)
    wo_t = lax.all_gather(wo_cols, "dp", axis=0, tiled=True)
    own_experts = jnp.concatenate([w_gate, w_up, w_down.transpose(0, 2, 1)], axis=0)
    expert_full = lax.all_gather(own_experts, "dp", axis=1, tiled=True)
    gate_w = expert_full[:local_experts]
    up_w = expert_full[local_experts : 2 * local_experts]
    down_t = expert_full[2 * local_experts :]

    tokens_all, cot_all = row_gather([tokens, cotangent], 2)
    inputs_all = tokens_all.reshape(group_rows, width).astype(f32)
    cot_all = cot_all.reshape(group_rows, width)
    scaled_all = inputs_all * lax.rsqrt(
        jnp.mean(inputs_all * inputs_all, axis=-1, keepdims=True) + EPS
    )
    normed_all = (scaled_all * gain1).astype(bf16)
    proj = dot(normed_all, wqkv)
    stream = token_order[0]
    segment, positions = places(stream, lengths[0])

    def prepare(query_in, key_in, query_scales, key_scales):
        return (
            rotate(
                rms_scale(query_in.reshape(group_rows, head_local, head_dim), query_scales),
                positions,
            ),
            rotate(
                rms_scale(key_in.reshape(group_rows, kv_local, head_dim), key_scales), positions
            ),
        )

    (query_rot, key_rot), prepare_pull = jax.vjp(
        prepare, proj[:, :128], proj[:, 128:192], qgain, kgain
    )
    query_low = query_rot.astype(bf16)
    key_low = key_rot.astype(bf16)[:, 0]
    value_low = proj[:, 192:].astype(bf16)
    mixed_low, log_totals = attend(query_low, key_low, value_low, segment, stream, scale)
    mixed_own = exchange(mixed_low.reshape(ranks, rows, 128)).transpose(1, 0, 2).reshape(rows, -1)
    hidden = tokens.astype(f32) + dot(mixed_own, wo_t, ((1,), (1,)))
    r2 = lax.rsqrt(jnp.mean(hidden * hidden, axis=-1, keepdims=True) + EPS)
    normed2 = (hidden * r2 * gain2).astype(bf16)

    (normed2_all,) = row_gather([normed2], 3)
    normed2_all = normed2_all.reshape(group_rows, width)
    logits = dot(normed2_all, router_full)
    named = jnp.any(routes_all[:, :, None] == jnp.arange(experts, dtype=jnp.int32), axis=1)
    gates_all = jax.nn.softmax(jnp.where(named, logits, MASKED), axis=-1)
    blocks = ranks
    own_named = lax.dynamic_slice_in_dim(named, rank * local_experts, local_experts, 1)
    own_gates = lax.dynamic_slice_in_dim(gates_all, rank * local_experts, local_experts, 1)
    own_named = own_named.reshape(blocks, rows, local_experts)
    slot_rank = jnp.cumsum(own_named.astype(jnp.int32), axis=1) - 1
    slot_rank = jnp.where(own_named, slot_rank, -1)
    table = (
        slot_rank.transpose(0, 2, 1)[:, :, None, :]
        == jnp.arange(CAP, dtype=jnp.int32)[None, None, :, None]
    )
    table_low = table.astype(bf16)
    slots = blocks * CAP
    x_slots = jnp.einsum(
        "besl,bld->ebsd",
        table_low,
        normed2_all.reshape(blocks, rows, width),
        preferred_element_type=bf16,
    ).reshape(local_experts, slots, width)
    u_slots = jnp.einsum(
        "besl,bld->ebsd",
        table_low,
        cot_all.reshape(blocks, rows, width),
        preferred_element_type=bf16,
    ).reshape(local_experts, slots, width)
    gate_slot = jnp.sum(
        jnp.where(
            table, own_gates.reshape(blocks, rows, -1).transpose(0, 2, 1)[:, :, None, :], 0.0
        ),
        axis=3,
    )
    gate_slot = gate_slot.transpose(1, 0, 2).reshape(local_experts, slots, 1)
    gate_act = jnp.einsum("erd,edf->erf", x_slots, gate_w, preferred_element_type=f32)
    up_act = jnp.einsum("erd,edf->erf", x_slots, up_w, preferred_element_type=f32)
    sig = 1.0 / (1.0 + jnp.exp(-gate_act))
    silu = gate_act * sig
    inner_low = (silu * up_act).astype(bf16)
    expert_out = jnp.einsum("erf,edf->erd", inner_low, down_t, preferred_element_type=f32)
    u_float = u_slots.astype(f32)
    gate_grad_slot = jnp.sum(u_float * expert_out, axis=2)
    weighted = (gate_slot * expert_out).astype(bf16).reshape(local_experts, blocks, CAP, width)
    out_part = jnp.einsum("besl,ebsd->bld", table_low, weighted, preferred_element_type=bf16)
    out_grad = (gate_slot * u_float).astype(bf16)
    inner_grad = jnp.einsum("erd,edf->erf", out_grad, down_t, preferred_element_type=f32)
    gate_act_grad = (inner_grad * up_act * sig * (1.0 + gate_act * (1.0 - sig))).astype(bf16)
    up_act_grad = (inner_grad * silu).astype(bf16)
    down_grad = jnp.einsum("erd,erf->edf", out_grad, inner_low, preferred_element_type=bf16)
    gate_w_grad = jnp.einsum("erd,erf->edf", x_slots, gate_act_grad, preferred_element_type=bf16)
    up_w_grad = jnp.einsum("erd,erf->edf", x_slots, up_act_grad, preferred_element_type=bf16)
    copy_grad = jnp.einsum("erf,edf->erd", gate_act_grad, gate_w, preferred_element_type=f32)
    copy_grad += jnp.einsum("erf,edf->erd", up_act_grad, up_w, preferred_element_type=f32)
    copy_low = copy_grad.astype(bf16).reshape(local_experts, blocks, CAP, width)
    copy_part = jnp.einsum("besl,ebsd->bld", table_low, copy_low, preferred_element_type=bf16)
    gate_grad_rows = jnp.sum(
        jnp.where(
            table,
            gate_grad_slot.reshape(local_experts, blocks, CAP).transpose(1, 0, 2)[..., None],
            0.0,
        ),
        axis=2,
    ).transpose(0, 2, 1)
    grad_hi = gate_grad_rows.astype(bf16)
    grad_lo = (gate_grad_rows - grad_hi.astype(f32)).astype(bf16)
    extra = jnp.concatenate([grad_hi, grad_lo], axis=2)
    extra = jnp.pad(extra, ((0, 0), (0, 0), (0, 128 - 2 * local_experts)))
    back = exchange(jnp.concatenate([copy_part, extra], axis=2))
    expert_sums = lax.psum_scatter(
        jnp.concatenate([gate_w_grad, up_w_grad, down_grad], axis=0),
        "dp",
        scatter_dimension=1,
        tiled=True,
    ).astype(f32)
    out_sum = jnp.sum(exchange(out_part).astype(f32), axis=0)
    layer_out = hidden + out_sum

    normed2_grad = jnp.sum(back[:, :, :width].astype(f32), axis=0)
    grad_pieces = back[:, :, width : width + local_experts].astype(f32)
    grad_pieces += back[:, :, width + local_experts : width + 2 * local_experts].astype(f32)
    gate_grad_own = grad_pieces.transpose(1, 0, 2).reshape(rows, experts)
    gates_own = lax.dynamic_slice_in_dim(gates_all, rank * rows, rows, 0)
    inner_sum = jnp.sum(gates_own * gate_grad_own, axis=1, keepdims=True)
    logit_grad = (gates_own * (gate_grad_own - inner_sum)).astype(bf16)
    normed2_grad = normed2_grad + dot(logit_grad, router_full, ((1,), (1,)))
    router_grad = dot(normed2, logit_grad, ((0,), (0,)))
    scaled2 = hidden * r2
    ffn_gain_grad = jnp.sum(normed2_grad * scaled2, axis=0)
    weighted_grad = normed2_grad * gain2
    upstream = cotangent.astype(f32)
    hidden_grad = upstream + r2 * (
        weighted_grad - scaled2 * jnp.mean(weighted_grad * scaled2, axis=-1, keepdims=True)
    )
    branch = hidden_grad.astype(bf16)
    mixed_grad_own = dot(branch, wo_t).astype(bf16)
    wo_grad = dot(branch, mixed_own, ((0,), (0,)), bf16)
    mixed_grad = exchange(mixed_grad_own.reshape(rows, ranks, 128).transpose(1, 0, 2))
    mixed_grad = mixed_grad.reshape(group_rows, head_local, head_dim)

    query_rot_grad, key_rot_grad, value_grad = attend_back(
        query_low, key_low, value_low, segment, stream, scale, log_totals, mixed_grad
    )
    query_grad, key_grad, qgain_grad, kgain_grad = prepare_pull(
        (query_rot_grad, key_rot_grad[:, None])
    )
    proj_grad = jnp.concatenate([query_grad, key_grad, value_grad], axis=1).astype(bf16)
    proj_grad_own = exchange(proj_grad.reshape(ranks, rows, qkv_width))
    wqkv_all = lax.all_gather(wqkv_cols, "dp", axis=0, tiled=True)
    normed_grad = dot(
        proj_grad_own.transpose(1, 0, 2).reshape(rows, -1), wqkv_all, ((1,), (1,))
    )
    wqkv_grad = dot(normed_all, proj_grad, ((0,), (0,)))
    inputs = tokens.astype(f32)
    r1 = lax.rsqrt(jnp.mean(inputs * inputs, axis=-1, keepdims=True) + EPS)
    scaled1 = inputs * r1
    attn_gain_grad = jnp.sum(normed_grad * scaled1, axis=0)
    weighted_grad = normed_grad * gain1
    grad_tokens = hidden_grad + r1 * (
        weighted_grad - scaled1 * jnp.mean(weighted_grad * scaled1, axis=-1, keepdims=True)
    )

    small_grad = jnp.concatenate(
        [attn_gain_grad[:, None], ffn_gain_grad[:, None], router_grad], axis=1
    )
    small_grad = jnp.pad(small_grad, ((0, 0), (0, 64 - small_grad.shape[1])))
    head_grads = jnp.concatenate([qgain_grad, kgain_grad], axis=0)
    head_grads = head_grads.reshape(3, 16, head_dim // 16).transpose(1, 0, 2)
    head_grads = jnp.pad(head_grads, ((0, 0), (0, dp_rows - 3), (0, 60))).reshape(width, 64)
    first_sums = lax.psum_scatter(
        jnp.concatenate([wqkv_grad, small_grad, head_grads], axis=1),
        "dp",
        scatter_dimension=0,
        tiled=True,
    )
    wo_sums = lax.psum_scatter(wo_grad, "dp", scatter_dimension=0, tiled=True)
    wo_pieces = exchange(wo_sums.reshape(dp_rows, ranks, 128).transpose(1, 0, 2))
    small_pieces = exchange(first_sums[:, 256:].reshape(ranks, 8, 128))
    grad_w_output = jnp.sum(wo_pieces.astype(f32), axis=0).T
    small_sums = jnp.sum(small_pieces[:, :, :64], axis=0)
    head_sums = first_sums[:3, 320:324]
    return (
        layer_out,
        grad_tokens,
        small_sums[:, 0],
        small_sums[:, 1],
        small_sums[:, 2 : 2 + experts],
        first_sums[:, :128],
        first_sums[:, 128:192],
        first_sums[:, 192:256],
        grad_w_output,
        head_sums[:2],
        head_sums[2:],
        expert_sums[:local_experts],
        expert_sums[local_experts : 2 * local_experts],
        expert_sums[2 * local_experts :].transpose(0, 2, 1),
    )


def solution(mesh):
    both = ("dp", "tensor")
    return jax.shard_map(
        per_device,
        mesh=mesh,
        in_specs=(
            P(both, None),
            P("dp", None),
            P("dp", None),
            P(both, None),
            P(both, None),
            P(both),
            P(both),
            P(both, None),
            P("dp", "tensor"),
            P("dp", "tensor"),
            P("dp", "tensor"),
            P("tensor", "dp"),
            P("tensor", "dp"),
            P("tensor", "dp"),
            P("tensor", "dp", None),
            P("tensor", "dp", None),
            P("tensor", None, "dp"),
        ),
        out_specs=(
            P(both, None),
            P(both, None),
            P(both),
            P(both),
            P(both, None),
            P("dp", "tensor"),
            P("dp", "tensor"),
            P("dp", "tensor"),
            P("tensor", "dp"),
            P("tensor", "dp"),
            P("tensor", "dp"),
            P("tensor", "dp", None),
            P("tensor", "dp", None),
            P("tensor", None, "dp"),
        ),
        check_vma=False,
    )
```

time: 1650 us -> 814 us (0.49)
  blocking collectives: 728 us -> 27.4 us
  waiting for transfers between devices: 433 us -> 220 us
  Pallas kernels: 0 us -> 124 us
  local copies, waits for them, and re-layouts: 131 us -> 81.5 us
    all_gather x4 -> x1, blocking collectives: 477 us -> 27.4 us  [per_device(): first_full = lax.all_gather(first_payload, 'dp', axis=0, tiled=False)]
    unnamed x3 -> x0, blocking collectives: 251 us -> none
    pallas_call x0 -> x3, Pallas kernels: none -> 124 us  [the longest x2 112 us: row_gather(): pl.pallas_call(functools.partial(row_gather_kernel, count), out_shape=[ja...]
    reduce_scatter x4 -> x3, waiting for transfers between devices: 235 us -> 138 us  [the longest x1 112 us: per_device(): lax.psum_scatter(jnp.concatenate([gate_w_grad, up_w_grad, down_grad], axi...]
    all_to_all x6 -> x7, waiting for transfers between devices: 151 us -> 81.9 us  [exchange(): return lax.all_to_all(x, 'tensor', 0, 0, tiled=False)]
    all_gather x4 -> x3, waiting for transfers between devices: 47.3 us -> 0.02 us  [the longest x1 0.02 us: per_device(): wo_t = lax.all_gather(wo_cols, 'dp', axis=0, tiled=True)]
    gather x2 -> x0, local copies, waits for them, and re-layouts: 29.4 us -> none  [the longest x1 14.8 us: per_device(): jnp.take(padded, slot_source, axis=0)]
    convert_element_type x12 -> x17, other arithmetic: 5.2 us -> 29.7 us  [the longest x4 10.2 us: backward_block(): score_grad = (probability * (prob_grad - inner_sum)).astype(bf16)]
  transfers between devices with their start and end apart: 16 -> 13, of which waited for: 8 -> 8; matrix products, arithmetic and copies ran while one was open for 22% -> 43% of each run, Pallas kernels for 0% -> 14%
where the time goes in v1:
time: 814 us; the launch traced here: 802 us
  waiting for transfers between devices  220 us (27%)
  matrix products  192 us (24%)
  Pallas kernels  124 us (15%)
  other arithmetic  95.9 us (12%)
  local copies, waits for them, and re-layouts  81.5 us (10%)
  starting transfers between devices  29.9 us (4%)
  blocking collectives  27.4 us (3%)
  loops' own time  16.4 us (2%)
  between operations  15.7 us (2%)
    pallas_call x2, Pallas kernels, row_gather(): pl.pallas_call(functools.partial(row_gather_kernel, count), out_shape=[ja...  112 us
    reduce_scatter x1, waiting for transfers between devices, per_device(): lax.psum_scatter(jnp.concatenate([gate_w_grad, up_w_grad, down_grad], axi...  112 us
    all_to_all x7, waiting for transfers between devices, exchange(): return lax.all_to_all(x, 'tensor', 0, 0, tiled=False)  81.9 us
    all_to_all x7, starting transfers between devices, exchange(): return lax.all_to_all(x, 'tensor', 0, 0, tiled=False)  29.4 us
    all_gather x1, blocking collectives, per_device(): first_full = lax.all_gather(first_payload, 'dp', axis=0, tiled=False)  27.4 us
    reduce_scatter x1, waiting for transfers between devices, per_device(): lax.psum_scatter(jnp.concatenate([wqkv_grad, small_grad, head_grads], axi...  25.8 us
    dynamic_update_slice x8, local copies, waits for them, and re-layouts, attend_back(): lax.scan(backward_block, (zero, zero), (start_rows, log_totals))  25.6 us
    dot_general x4, matrix products, backward_block(): jnp.einsum('rqs,qrd->sd', prob_low, grad_block, preferred_element_type=f32)  22.9 us
  transfers between devices with their start and end apart: 13, of which 8 were waited for; matrix products, arithmetic and copies ran while one was open for 43% of the time, Pallas kernels for 14%

profile of v1, /device:TPU:0, one launch (start us, length us, event | category | flops | bytes accessed | tf_op | source)
XLA Modules:
  0.0 802.0 jit_solution(14063957744729966192)
XLA Ops:
  13.3 11.7 %tiny_gather.1 = bf16[8,224,128]{2,1,0:T(8,128)(2,1)} custom-call(bf16[224,128]{1,0:T(8,128)(2,1)} %copy-done.46), custom_call_target="tpu_custom_call" | custom-call | tf_op jit(solution)/shard_map/tiny_gather/pallas_call | solution.py:48
  30.5 27.4 %all-gather = bf16[1024,384]{1,0:T(8,128)(2,1)S(1)} all-gather(bf16[64,384]{1,0:T(8,128)(2,1)S(1)} %pad_maximum_fusion.6), channel_id=2, replica_groups=mesh['dp'=16,'tensor'=8] {'dp'}, dimensions={0}, use_global_device_ids=true | all-gather | bytes 835584 | tf_op jit(solution)/shard_map/all_gather | solution.py:294
  58.7 73.6 %row_gather.2 = (bf16[8,256,1024]{2,1,0:T(8,128)(2,1)}, bf16[8,256,1024]{2,1,0:T(8,128)(2,1)}) custom-call(bf16[256,1024]{1,0:T(8,128)(2,1)} %refs_0_.1, bf16[256,1024]{1,0:T(8,128)(2,1)} %refs_1_.1), custom_call_target="tpu_custom_call" | custom-call | tf_op jit(solution)/shard_map/row_gather/pallas_call | solution.py:131
  142.8 43.9 %while.27 = (s32[]{:T(128)}, bf16[4,512,128]{2,1,0:T(8,128)(2,1)S(1)}, f32[4,2,512,1]{2,1,3,0:T(2,128)S(1)}, s32[4]{0:T(128)S(1)}, s32[2048]{0:T(1024)S(1)}, /*i...) while((s32[]{:T(128)}, ...), condition=%wide.region_9.10_spmd, body=%wide.region_6.9_spmd.sunk | while | flops 565246976 | bytes 30732480 | solution.py:198
  210.5 38.5 %row_gather.3 = bf16[8,256,1024]{2,1,0:T(8,128)(2,1)} custom-call(bf16[256,1024]{1,0:T(8,128)(2,1)} %multiply_convert_fusion.5.refs_0_), custom_call_target="tpu_custom_call" | custom-call | tf_op jit(solution)/shard_map/row_gather/pallas_call | solution.py:131
  258.1 9.1 %fusion.68 = f32[4,640,512]{2,1,0:T(8,128)} fusion(bf16[4,640,1024]{2,1,0:T(8,128)(2,1)} %bitcast.359, bf16[12,1024,512]{2,1,0:T(8,128)(2,1)} %all-gather.7.cloned.1.call-done), kind=kOutput, calls=%fused_computation.93 | convolution fusion | flops 2684354560 | bytes 14680064 | tf_op jit(solution)/shard_map/erd,edf->erf/dot_general | solution.py:379
  267.2 8.6 %multiply_convert_fusion.4 = (bf16[4,640,512]{2,1,0:T(8,128)(2,1)S(1)}, f32[4,640,512]{2,1,0:T(8,128)}) fusion(f32[4,640,512]{2,1,0:T(8,128)} %fusion.68, bf16[4,640,1024]{2,1,0:T(8,128)(2,1)S(1)} %bitcast.361, bf16[12,1024,512]{2,1,0:T(8,128)(2,1)} %all-gather.7.cloned.1.call-done), kind=kOutput, calls=%fused_computation.75 | convolution fusion | flops 2692218880 | bytes 22544384 | tf_op jit(solution)/shard_map/erd,edf->erf/dot_general | solution.py:380
  275.9 10.0 %fusion.44 = (f32[4,640]{1,0:T(4,128)S(1)}, f32[4,640,1024]{2,1,0:T(8,128)}) fusion(f32[4,8,80,1024]{3,2,1,0:T(8,128)S(1)} %bitcast.353, bf16[4,640,512]{2,1,0:T(8,128)(2,1)S(1)} %get-tuple-element.404, bf16[12,1024,512]{2,1,0:T(8,128)(2,1)} %all-gather.7.cloned.1.call-done), kind=kOutput, calls=%fused_computation.56 | convolution fusion | flops 2689594880 | bytes 27797504 | tf_op jit(solution)/shard_map/erf,edf->erd/dot_general | solution.py:384
  287.7 10.1 %fusion.43 = (bf16[4,640,1024]{2,1,0:T(8,128)(2,1)}, bf16[4,640,1024]{2,1,0:T(8,128)(2,1)S(1)}) fusion(f32[4,8,80,1024]{3,2,1,0:T(8,128)} %copy.284, f32[4,640]{1,0:T(4,128)S(1)} %mul.486, f32[4,640,1024]{2,1,0:T(8,128)} %get-tuple-element.407), kind=kLoop, calls=%fused_computation.55 | loop fusion | flops 10485760 | bytes 31467520 | tf_op jit(solution)/shard_map/convert_element_type | solution.py:389
  306.9 10.9 %multiply_convert_fusion.3 = (bf16[4,640,512]{2,1,0:T(8,128)(2,1)}, bf16[4,640,512]{2,1,0:T(8,128)(2,1)}) fusion(f32[4,640,512]{2,1,0:T(8,128)} %fusion.68, f32[4,640,512]{2,1,0:T(8,128)} %get-tuple-element.405, bf16[4,640,1024]{2,1,0:T(8,128)(2,1)} %get-tuple-element.396, bf16[12,1024,512]{2,1,0:T(8,128)(2,1)} %all-gather.7.cloned.1.call-done), kind=kOutput, calls=%fused_computation.74 | convolution fusion | flops 2701393920 | bytes 25165824 | tf_op jit(solution)/shard_map/erd,edf->erf/dot_general | solution.py:390
  324.4 8.3 %add_convert_fusion = bf16[4,640,1024]{2,1,0:T(8,128)(2,1)} fusion(f32[4,640,1024]{2,1,0:T(8,128)S(1)} %fusion.62, bf16[4,640,512]{2,1,0:T(8,128)(2,1)} %get-tuple-element.378, bf16[12,1024,512]{2,1,0:T(8,128)(2,1)} %all-gather.7.cloned.1.call-done), kind=kOutput, calls=%fused_computation.58 | convolution fusion | flops 2689597440 | bytes 22544384 | tf_op jit(solution)/shard_map/erf,edf->erd/dot_general | solution.py:396
  340.4 12.9 %all-to-all-done.1 = bf16[8,256,1024]{2,1,0:T(8,128)(2,1)} async-done(((bf16[8,256,1024]{2,1,0:T(8,128)(2,1)}), bf16[8,256,1024]{2,1,0:T(8,128)(2,1)}, u32[]{:S(2)}, u32[]{:S(2)}) %all-to-all-start.1) | async-done | bytes 4194336 | tf_op jit(solution)/shard_map/all_to_all | solution.py:148
  366.5 45.8 %all-to-all-done.2 = bf16[8,256,1152]{2,1,0:T(8,128)(2,1)} async-done(((bf16[8,256,1152]{2,1,0:T(8,128)(2,1)}), bf16[8,256,1152]{2,1,0:T(8,128)(2,1)}, u32[]{:S(2)}, u32[]{:S(2)}) %all-to-all-start.2) | async-done | bytes 4718624 | tf_op jit(solution)/shard_map/all_to_all | solution.py:148
  431.0 7.2 all-to-all-done.3
  440.0 125.5 %while.28 = (s32[]{:T(128)}, f32[2048,64]{0,1:T(8,128)}, f32[2048,64]{0,1:T(8,128)}, f32[4,512,2,64]{1,0,3,2:T(4,128)}, s32[4]{0:T(128)S(1)}, /*index=5*/s32[204...) while((s32[]{:T(128)}, f32[2048,64]{0,1:T(8,128)}, ...), condition=%wide.region_26.27_spmd.clone, body=%wide.region_24.26_spmd.clone.sunk | while | flops 1377500160 | bytes 122216744 | solution.py:242
  455.7 6.1 dynamic_update_slice.20
  518.2 6.1 dynamic_update_slice.20
  549.5 6.1 dynamic_update_slice.20
  585.2 8.4 %all-to-all-done.4 = bf16[8,256,256]{1,2,0:T(8,128)(2,1)S(1)} async-done(((bf16[8,256,256]{1,2,0:T(8,128)(2,1)}), bf16[8,256,256]{1,2,0:T(8,128)(2,1)S(1)}, u32[]{:S(2)}, u32[]{:S(2)}) %all-to-all-start.4) | async-done | bytes 1048608 | tf_op jit(solution)/shard_map/all_to_all | solution.py:148
  600.1 6.9 fusion.164
  607.1 7.1 fusion.162
  619.4 8.0 %pad_maximum_fusion = bf16[12,1024,512]{2,1,0:T(8,128)(2,1)} fusion(bf16[4,1024,512]{2,1,0:T(8,128)(2,1)S(1)} %fusion.164, bf16[4,1024,512]{2,1,0:T(8,128)(2,1)} %fusion.163, bf16[4,1024,512]{2,1,0:T(8,128)(2,1)S(1)} %fusion.162), kind=kLoop, calls=%fused_computation.52 | loop fusion | flops 12582912 | bytes 25165824 | tf_op jit(solution)/shard_map/concatenate | solution.py:414
  640.1 25.8 %reduce-scatter.10.cloned.1.call-done = f32[64,384]{1,0:T(8,128)} async-done(((f32[1024,384]{1,0:T(8,128)}), f32[64,384]{1,0:T(8,128)}) %reduce-scatter.10.cloned.1.call-update) | async-done | bytes 98320 | tf_op jit(solution)/shard_map/reduce_scatter | solution.py:473
  679.6 111.8 %reduce-scatter.8.cloned.1.call-done = bf16[12,64,512]{2,1,0:T(8,128)(2,1)} async-done(((bf16[12,1024,512]{2,1,0:T(8,128)(2,1)}), bf16[12,64,512]{2,1,0:T(8,128)(2,1)}) %reduce-scatter.8.cloned.1.call-update) | async-done | bytes 786448 | tf_op jit(solution)/shard_map/reduce_scatter | solution.py:413
  (421 shorter events, 309.2 us)
Async XLA Ops:
  7.2 51.2 %copy-start.61 = (s32[1,3]{1,0:T(1,128)S(1)}, s32[1,3]{1,0:T(1,128)}, u32[]{:S(2)}) copy-start(s32[1,3]{1,0:T(1,128)} %param.22) | copy-start | bytes 40
  7.2 198.8 %all-gather.5.cloned.1.call-start = ((), (), s32[]{:S(2)}) async-start(), calls=%async_computation.10 | async-start | bytes 2228224 | tf_op jit(solution)/shard_map/all_gather | solution.py:302
  26.6 231.5 %all-gather.7.cloned.1.call-start = ((), (), s32[]{:S(2)}) async-start(), calls=%async_computation.11 | async-start | bytes 13369344 | tf_op jit(solution)/shard_map/all_gather | solution.py:304
  58.3 83.6 %copy-start.53 = (f32[2,64]{1,0:T(2,128)}, f32[2,64]{1,0:T(2,128)S(1)}, u32[]{:S(2)}) copy-start(f32[2,64]{1,0:T(2,128)S(1)} %reshape.628) | copy-start | bytes 1540
  58.7 80.8 %copy-start.56 = (f32[64]{0:T(128)}, f32[64]{0:T(128)S(1)}, u32[]{:S(2)}) copy-start(f32[64]{0:T(128)S(1)} %reshape.629) | copy-start | bytes 772
  142.8 49.0 %slice-start.6 = ((bf16[8,224,128]{2,1,0:T(8,128)(2,1)}), bf16[8,128,128]{2,1,0:T(8,128)(2,1)S(1)}, s32[]{:S(2)}) async-start(bf16[8,224,128]{2,1,0:T(8,128)(2,1)} %tiny_gather.1), calls=%async_computation.22 | async-start | bytes 524288 | tf_op jit(solution)/shard_map/slice | solution.py:284
  142.8 50.2 %copy-start.27 = (bf16[8,224,128]{2,1,0:T(8,128)(2,1)S(1)}, bf16[8,224,128]{2,1,0:T(8,128)(2,1)}, u32[]{:S(2)}) copy-start(bf16[8,224,128]{2,1,0:T(8,128)(2,1)} %tiny_gather.1) | copy-start | bytes 1376260
  187.5 18.2 %all-to-all-start = ((bf16[8,256,128]{2,1,0:T(8,128)(2,1)}), bf16[8,256,128]{2,1,0:T(8,128)(2,1)S(1)}, u32[]{:S(2)}, u32[]{:S(2)}) async-start(bf16[8,256,128]{2,1,0:T(8,128)(2,1)} %bitcast.393), calls=%async_computation | async-start | bytes 1048576 | tf_op jit(solution)/shard_map/all_to_all | solution.py:148
  191.5 393.7 %all-gather.9.cloned.1.call-start = ((), (), s32[]{:S(2)}) async-start(), calls=%async_computation.12 | async-start | bytes 4456448 | tf_op jit(solution)/shard_map/all_gather | solution.py:452
  205.9 43.1 %copy-start.17 = (bf16[256,8,128]{0,2,1:T(8,128)(2,1)}, bf16[256,8,128]{0,2,1:T(8,128)(2,1)S(1)}, u32[]{:S(2)}) copy-start(bf16[256,8,128]{0,2,1:T(8,128)(2,1)S(1)} %copy.275) | copy-start | bytes 1572868
  302.2 51.1 %all-to-all-start.1 = ((bf16[8,256,1024]{2,1,0:T(8,128)(2,1)}), bf16[8,256,1024]{2,1,0:T(8,128)(2,1)}, u32[]{:S(2)}, u32[]{:S(2)}) async-start(bf16[8,256,1024]{2,1,0:T(8,128)(2,1)} %fusion.77), calls=%async_computation.1 | async-start | bytes 8388608 | tf_op jit(solution)/shard_map/all_to_all | solution.py:148
  340.4 17.7 %copy-start.50 = (f32[1024]{0:T(1024)S(1)}, f32[1024]{0:T(1024)}, u32[]{:S(2)}) copy-start(f32[1024]{0:T(1024)} %copy-done.49) | copy-start | bytes 12292
  353.3 59.1 %all-to-all-start.2 = ((bf16[8,256,1152]{2,1,0:T(8,128)(2,1)}), bf16[8,256,1152]{2,1,0:T(8,128)(2,1)}, u32[]{:S(2)}, u32[]{:S(2)}) async-start(bf16[8,256,1152]{2,1,0:T(8,128)(2,1)} %fusion.53), calls=%async_computation.2 | async-start | bytes 9437184 | tf_op jit(solution)/shard_map/all_to_all | solution.py:148
  366.5 52.4 %copy-start.7 = (f32[256,1024]{1,0:T(8,128)S(1)}, f32[256,1024]{1,0:T(8,128)}, u32[]{:S(2)}) copy-start(f32[256,1024]{1,0:T(8,128)} %copy-done.6) | copy-start | bytes 3145732
  424.5 13.7 %all-to-all-start.3 = ((bf16[8,256,128]{2,1,0:T(8,128)(2,1)}), bf16[8,256,128]{2,1,0:T(8,128)(2,1)}, u32[]{:S(2)}, u32[]{:S(2)}) async-start(bf16[8,256,128]{2,1,0:T(8,128)(2,1)} %bitcast.377), calls=%async_computation.3 | async-start | bytes 1048576 | tf_op jit(solution)/shard_map/all_to_all | solution.py:148
  428.6 198.9 %reduce-scatter.6.cloned.1.call-start = ((), (), s32[]{:S(2)}) async-start(), calls=%async_computation.13 | async-start | bytes 2228224 | tf_op jit(solution)/shard_map/reduce_scatter | solution.py:479
  439.9 128.6 %copy-start.22 = (f32[2048,32]{0,1:T(8,128)S(1)}, f32[2048,32]{0,1:T(8,128)}, u32[]{:S(2)}) copy-start(f32[2048,32]{0,1:T(8,128)} %copy-done.21) | copy-start | bytes 786436
  439.9 130.1 %copy-start.39 = (f32[2048,2]{0,1:T(2,128)S(1)}, f32[2048,2]{0,1:T(2,128)}, u32[]{:S(2)}) copy-start(f32[2048,2]{0,1:T(2,128)} %copy-done.38) | copy-start | bytes 49156
  439.9 130.1 %copy-start.54 = (f32[2,64]{1,0:T(2,128)S(1)}, f32[2,64]{1,0:T(2,128)}, u32[]{:S(2)}) copy-start(f32[2,64]{1,0:T(2,128)} %copy-done.53) | copy-start | bytes 1540
  575.6 18.1 %all-to-all-start.4 = ((bf16[8,256,256]{1,2,0:T(8,128)(2,1)}), bf16[8,256,256]{1,2,0:T(8,128)(2,1)S(1)}, u32[]{:S(2)}, u32[]{:S(2)}) async-start(bf16[8,256,256]{1,2,0:T(8,128)(2,1)} %pad_maximum_fusion.2), calls=%async_computation.4 | async-start | bytes 2097152 | tf_op jit(solution)/shard_map/all_to_all | solution.py:148
  579.2 86.7 %reduce-scatter.10.cloned.1.call-start = ((), (), s32[]{:S(2)}) async-start(), calls=%async_computation.15 | async-start | bytes 1671168 | tf_op jit(solution)/shard_map/reduce_scatter | solution.py:473
  600.1 191.3 %reduce-scatter.8.cloned.1.call-start = ((), (), s32[]{:S(2)}) async-start(), calls=%async_computation.14 | async-start | bytes 13369344 | tf_op jit(solution)/shard_map/reduce_scatter | solution.py:413
  629.3 10.2 %all-to-all-start.6 = ((bf16[8,64,128]{2,1,0:T(8,128)(2,1)}), bf16[8,64,128]{2,1,0:T(8,128)(2,1)S(1)}, u32[]{:S(2)}, u32[]{:S(2)}) async-start(bf16[8,64,128]{2,1,0:T(8,128)(2,1)} %bitcast_bitcast_fusion.1), calls=%async_computation.7 | async-start | bytes 262144 | tf_op jit(solution)/shard_map/all_to_all | solution.py:148
  667.3 10.9 %all-to-all-start.5 = ((f32[8,8,128]{2,1,0:T(8,128)}), f32[8,8,128]{2,1,0:T(8,128)S(1)}, u32[]{:S(2)}, u32[]{:S(2)}) async-start(f32[8,8,128]{2,1,0:T(8,128)} %get-tuple-element.395), calls=%async_computation.5 | async-start | bytes 65536 | tf_op jit(solution)/shard_map/all_to_all | solution.py:148
  (64 other events, 347.3 us)
Sparse Core Ops, SparseCore 0:
  26.8 54.4 all-gather.4
  84.3 88.5 all-gather.6
  194.8 52.8 all-gather.8
  433.0 68.4 reduce-scatter.5
  600.2 65.6 reduce-scatter.9
  670.1 121.2 reduce-scatter.7

commit v2 on v0

v2 whole, which is shorter than its diff:
```python
import functools

import jax
import jax.numpy as jnp
from jax import lax
from jax.experimental import pallas as pl
from jax.experimental.pallas import tpu as pltpu
from jax.sharding import PartitionSpec as P

CAP = 80
EPS = 1e-06
ROTARY_BASE = 10000.0
MASKED = -1e30
ROW = 256
CHUNK = 512
RANKS = 8
GROUPS = 16
MESH = pl.DeviceIdType.MESH
bf16 = jnp.bfloat16
f32 = jnp.float32


def dot(a, b, dims=((1,), (0,)), out=f32):
    return lax.dot_general(a, b, (dims, ((), ())), preferred_element_type=out)


def lane(shape):
    return lax.broadcasted_iota(jnp.int32, shape, len(shape) - 1)


def sublane(shape):
    return lax.broadcasted_iota(jnp.int32, shape, len(shape) - 2)


def whole(n):
    return [pl.BlockSpec(memory_space=pltpu.VMEM) for _ in range(n)]


def anywhere(n):
    return [pl.BlockSpec(memory_space=pl.ANY) for _ in range(n)]


def meet(ranks, groups):
    barrier = pltpu.get_barrier_semaphore()
    for peer in ranks:
        pl.semaphore_signal(barrier, inc=1, device_id={"tensor": peer}, device_id_type=MESH)
    for peer in groups:
        pl.semaphore_signal(barrier, inc=1, device_id={"dp": peer}, device_id_type=MESH)
    pl.semaphore_wait(barrier, len(ranks) + len(groups))


def push(src, dst, sems, index, peer):
    copy = pltpu.make_async_remote_copy(
        src_ref=src,
        dst_ref=dst,
        send_sem=sems[0].at[index],
        recv_sem=sems[1].at[index],
        device_id=peer,
        device_id_type=MESH,
    )
    copy.start()
    return copy


def keep(src, dst, sem):
    copy = pltpu.make_async_copy(src, dst, sem)
    copy.start()
    return copy


def others(name, size):
    me = lax.axis_index(name)
    return [lax.rem(me + k, size) for k in range(1, size)]


def neighbours():
    me = lax.axis_index("tensor")
    z = lax.rem(me, 4)
    here = me - z
    there = 4 - here
    right, left = lax.rem(z + 1, 4), lax.rem(z + 3, 4)
    return me, here, there, there + z, right, left


def start_rows(x, o, sems):
    me, here, _, partner, right, left = neighbours()
    return (
        push(x, o.at[me], sems, 0, {"tensor": partner}),
        push(x, o.at[me], sems, 1, {"tensor": here + right}),
        push(x, o.at[me], sems, 2, {"tensor": here + left}),
    )


def pass_rows(first, o, sems):
    _, here, there, partner, right, left = neighbours()
    to_right, to_left = {"tensor": here + right}, {"tensor": here + left}
    half = o.shape[1] // 2
    low, high = pl.ds(0, half), pl.ds(half, half)
    to_partner, own_right, own_left = first

    def on(index, block, part, peer):
        return push(o.at[block, part], o.at[block, part], sems, index, peer)

    both = pl.ds(0, 2 * half)
    to_partner.wait_recv()
    pass_right = on(3, partner, both, to_right)
    pass_left = on(4, partner, both, to_left)
    own_right.wait_recv()
    far = [on(5, here + left, low, to_right)]
    own_left.wait_recv()
    far += [on(6, here + right, high, to_left)]
    pass_right.wait_recv()
    far += [on(7, there + left, low, to_right)]
    pass_left.wait_recv()
    far += [on(8, there + right, high, to_left)]
    for copy in far:
        copy.wait()
    for copy in (*first, pass_right, pass_left):
        copy.wait_send()


def group_place():
    group = lax.axis_index("dp")
    core, side, y = lax.rem(group, 2), lax.rem(group // 2, 2), group // 4
    across = {"dp": group + 2 - 4 * side}
    other = {"dp": group + 1 - 2 * core}
    column = [(lax.rem(y + k, 4), {"dp": lax.rem(y + k, 4) * 4 + side * 2 + core}) for k in (2, 1, 3)]
    return y, side, core, across, column, other


def gather_first(src, o, sems):
    y, side, core, across, _, _ = group_place()
    return push(src, o.at[y, side, core], sems, 0, across)


def gather_second(first, own, o, sems):
    y, _, core, _, column, _ = group_place()
    first.wait_recv()
    own.wait()
    part = o.at[y, :, core]
    return [push(part, part, sems, 1 + k, peer) for k, (_, peer) in enumerate(column)]


def gather_third(second, o, sems):
    _, _, core, _, _, other = group_place()
    for copy in second:
        copy.wait_recv()
    part = o.at[:, :, core]
    return push(part, part, sems, 4, other)


def opening_kernel(
    tokens, payload,
    tokens_all, tiny_all, first_all, rest_all,
    row_send, row_recv, tiny_send, tiny_recv, first_send, first_recv, rest_send, rest_recv, local,
):
    me = lax.axis_index("tensor")
    y, side, core, across, column, other = group_place()
    ranks = others("tensor", RANKS)
    meet(ranks, [across["dp"], other["dp"]] + [peer["dp"] for _, peer in column])
    tiny = [
        push(payload, tiny_all.at[me], (tiny_send, tiny_recv), k, {"tensor": peer})
        for k, peer in enumerate(ranks)
    ]
    first_sems, rest_sems = (first_send, first_recv), (rest_send, rest_recv)
    own = payload.at[pl.ds(0, 144)]
    first_one = gather_first(own, first_all, first_sems)
    rows = start_rows(tokens, tokens_all, (row_send, row_recv))
    tiny_own = keep(payload, tiny_all.at[me], local.at[0])
    first_own = keep(own, first_all.at[y, side, core], local.at[1])
    tokens_own = keep(tokens, tokens_all.at[me], local.at[2])
    first_two = gather_second(first_one, first_own, first_all, first_sems)
    for copy in tiny:
        copy.wait_recv()
    tiny_own.wait()
    part = tiny_all.at[:, pl.ds(128, 80)]
    rest_one = gather_first(part, rest_all, rest_sems)
    rest_own = keep(part, rest_all.at[y, side, core], local.at[3])
    first_three = gather_third(first_two, first_all, first_sems)
    rest_two = gather_second(rest_one, rest_own, rest_all, rest_sems)
    pass_rows(rows, tokens_all, (row_send, row_recv))
    rest_three = gather_third(rest_two, rest_all, rest_sems)
    first_three.wait()
    rest_three.wait()
    for copy in (*tiny, first_one, rest_one, *first_two, *rest_two):
        copy.wait_send()
    tokens_own.wait()


def opening(tokens, payload):
    dma = pltpu.SemaphoreType.DMA
    return pl.pallas_call(
        opening_kernel,
        out_shape=[
            jax.ShapeDtypeStruct((RANKS,) + tokens.shape, bf16),
            jax.ShapeDtypeStruct((RANKS,) + payload.shape, bf16),
            jax.ShapeDtypeStruct((4, 2, 2, 144, 128), bf16),
            jax.ShapeDtypeStruct((4, 2, 2, RANKS, 80, 128), bf16),
        ],
        in_specs=anywhere(2),
        out_specs=anywhere(4),
        scratch_shapes=[dma((9,)), dma((9,)), dma((7,)), dma((7,))] + [dma((5,))] * 4 + [dma((4,))],
        compiler_params=pltpu.CompilerParams(collective_id=1, has_side_effects=True),
        name="opening",
    )(tokens, payload)


def middle_kernel(
    mixed, rest, tokens, small,
    mixed_own, hidden, normed2_all,
    landed, normed2, mix_send, mix_recv, row_send, row_recv, local,
):
    me, here, _, partner, right, left = neighbours()
    ranks = others("tensor", RANKS)
    meet(ranks, [])
    sent = [
        push(mixed.at[peer], landed.at[me], (mix_send, mix_recv), k, {"tensor": peer})
        for k, peer in enumerate(ranks)
    ]
    own = keep(mixed.at[me], landed.at[me], local.at[0])
    for copy in sent:
        copy.wait_recv()
    own.wait()
    total = tokens[...].astype(f32)
    for s in range(RANKS):
        weight = rest[:, s, 16:80, :].reshape(-1, 128)
        total = total + dot(landed[s], weight, ((1,), (1,)))
    mixed_own[...] = landed[...]
    hidden[...] = total
    scale = lax.rsqrt(jnp.mean(total * total, axis=1, keepdims=True) + EPS)
    normed2[...] = (total * scale * small[1:2, :]).astype(bf16)
    rows = start_rows(normed2, normed2_all, (row_send, row_recv))
    kept = keep(normed2, normed2_all.at[me], local.at[1])
    pass_rows(rows, normed2_all, (row_send, row_recv))
    for copy in sent:
        copy.wait_send()
    kept.wait()


def middle(mixed, rest, tokens, small):
    dma = pltpu.SemaphoreType.DMA
    rows, width = tokens.shape
    return pl.pallas_call(
        middle_kernel,
        out_shape=[
            jax.ShapeDtypeStruct(mixed.shape, bf16),
            jax.ShapeDtypeStruct((rows, width), f32),
            jax.ShapeDtypeStruct((RANKS, rows, width), bf16),
        ],
        in_specs=whole(4),
        out_specs=whole(2) + anywhere(1),
        scratch_shapes=[
            pltpu.VMEM(mixed.shape, bf16),
            pltpu.VMEM((rows, width), bf16),
            dma((7,)),
            dma((7,)),
            dma((9,)),
            dma((9,)),
            dma((2,)),
        ],
        compiler_params=pltpu.CompilerParams(
            collective_id=2, has_side_effects=True, vmem_limit_bytes=40 << 20
        ),
        name="middle",
    )(mixed, rest, tokens, small)


def named_of(routes):
    picks = routes.astype(f32)
    picks = jnp.concatenate([picks[0:8], picks[8:16]], axis=1)
    expert = sublane((32, ROW)).astype(f32)
    found = jnp.zeros((32, ROW), f32)
    for k in range(8):
        found = jnp.where(picks[k : k + 1] == expert, 1.0, found)
    return found


def gates_of(named, logits):
    logits = jnp.where(named > 0.5, logits, MASKED)
    odds = jnp.where(named > 0.5, jnp.exp(logits - jnp.max(logits, axis=0, keepdims=True)), 0.0)
    return odds / jnp.sum(odds, axis=0, keepdims=True)


def norm_back(value, scales, grad):
    scale = lax.rsqrt(jnp.mean(value * value, axis=1, keepdims=True) + EPS)
    scaled = value * scale
    weighted = grad * scales
    moved = scale * (weighted - scaled * jnp.mean(weighted * scaled, axis=1, keepdims=True))
    return moved, scaled


def turn_kernel(
    back, hidden, cotangent, routes, small, mixed_own, rest,
    hidden_grad, mixed_grad, wo_grad, small_grad,
    leaving, landed, mix_send, mix_recv, local,
):
    me = lax.axis_index("tensor")
    ranks = others("tensor", RANKS)
    meet(ranks, [])
    value = hidden[...]
    gain = small[1:2, :]
    router = small[8:40, :].astype(bf16)
    scale = lax.rsqrt(jnp.mean(value * value, axis=1, keepdims=True) + EPS)
    normed2 = (value * scale * gain).astype(bf16)
    gates = gates_of(named_of(routes[...]), dot(router, normed2, ((1,), (1,))))
    pieces = back[:, ROW : ROW + 16, 0 : 2 * ROW].reshape(RANKS * 16, 2 * ROW)
    order = lane((32, RANKS * 16))
    expert = order // 16 * 4 + order % 16
    spread = jnp.where((expert == sublane(order.shape)) & (order % 16 < 4), 1.0, 0.0).astype(bf16)
    pieces = dot(spread, pieces)
    gate_grad = pieces[:, :ROW] + pieces[:, ROW:]
    inner = jnp.sum(gates * gate_grad, axis=0, keepdims=True)
    logit_grad = (gates * (gate_grad - inner)).astype(bf16)
    grad = dot(logit_grad, router, ((0,), (0,)))
    for s in range(RANKS):
        grad = grad + back[s, 0:ROW, :].astype(f32)
    moved, scaled = norm_back(value, gain, grad)
    total = cotangent[...].astype(f32) + moved
    branch = total.astype(bf16)
    for s in range(RANKS):
        weight = rest[:, s, 16:80, :].reshape(-1, 128)
        leaving[s] = dot(branch, weight).astype(bf16)
    sent = [
        push(leaving.at[peer], landed.at[me], (mix_send, mix_recv), k, {"tensor": peer})
        for k, peer in enumerate(ranks)
    ]
    own = keep(leaving.at[me], landed.at[me], local.at[0])
    hidden_grad[...] = total
    small_grad[0:8, :] = jnp.broadcast_to(
        jnp.sum(grad * scaled, axis=0, keepdims=True), (8, grad.shape[1])
    )
    small_grad[8:40, :] = dot(logit_grad, normed2)
    for s in range(RANKS):
        part = dot(branch, mixed_own[s], ((0,), (0,)))
        wo_grad[:, s] = part.astype(bf16).reshape(GROUPS, -1, 128)
    for copy in sent:
        copy.wait()
    own.wait()
    mixed_grad[...] = landed[...]


def turn(back, hidden, cotangent, routes, small, mixed_own, rest):
    dma = pltpu.SemaphoreType.DMA
    rows, width = hidden.shape
    return pl.pallas_call(
        turn_kernel,
        out_shape=[
            jax.ShapeDtypeStruct((rows, width), f32),
            jax.ShapeDtypeStruct(mixed_own.shape, bf16),
            jax.ShapeDtypeStruct((GROUPS, RANKS, width // GROUPS, 128), bf16),
            jax.ShapeDtypeStruct((40, width), f32),
        ],
        in_specs=whole(7),
        out_specs=whole(4),
        scratch_shapes=[
            pltpu.VMEM(mixed_own.shape, bf16),
            pltpu.VMEM(mixed_own.shape, bf16),
            dma((7,)),
            dma((7,)),
            dma((1,)),
        ],
        compiler_params=pltpu.CompilerParams(
            collective_id=3, has_side_effects=True, vmem_limit_bytes=48 << 20
        ),
        name="turn",
    )(back, hidden, cotangent, routes, small, mixed_own, rest)


def closing_kernel(
    proj_grad, wide, small_grad, wqkv_all, tokens, small, hidden_grad,
    grad_tokens, wqkv_sum, wo_sum, small_sum, head_sum,
    proj_in, wide_core, wide_y, wide_x, small_core, small_y, small_x,
    wide_half, wide_pair, small_half, small_pair, wo_out, small_out, wo_last, small_last,
    proj_send, proj_recv, wide_send, wide_recv, small_send, small_recv, last_send, last_recv, local,
):
    me = lax.axis_index("tensor")
    y, side, core, across, column, other = group_place()
    ranks = others("tensor", RANKS)
    meet(ranks, [across["dp"], other["dp"]] + [peer["dp"] for _, peer in column])
    wide_sems, small_sems = (wide_send, wide_recv), (small_send, small_recv)
    away = 1 - core
    first = [
        push(wide.at[:, :, away], wide_core, wide_sems, 0, other),
        push(small_grad.at[:, :, away], small_core, small_sems, 0, other),
    ]
    proj = [
        push(proj_grad.at[peer], proj_in.at[me], (proj_send, proj_recv), k, {"tensor": peer})
        for k, peer in enumerate(ranks)
    ]
    proj_own = keep(proj_grad.at[me], proj_in.at[me], local.at[0])
    for copy in first:
        copy.wait_recv()
    wide_half[...] = (wide[:, :, core].astype(f32) + wide_core[...].astype(f32)).astype(bf16)
    small_half[...] = small_grad[:, :, core] + small_core[...]
    second = []
    for k, (at, peer) in enumerate(column):
        second.append(push(wide_half.at[at], wide_y.at[k], wide_sems, 1 + k, peer))
        second.append(push(small_half.at[at], small_y.at[k], small_sems, 1 + k, peer))
    for copy in second:
        copy.wait_recv()
    total = wide_half[y].astype(f32)
    small_total = small_half[y]
    for k in range(3):
        total = total + wide_y[k].astype(f32)
        small_total = small_total + small_y[k]
    wide_pair[...] = total.astype(bf16)
    small_pair[...] = small_total
    third = [
        push(wide_pair.at[1 - side], wide_x, wide_sems, 4, across),
        push(small_pair.at[1 - side], small_x, small_sems, 4, across),
    ]
    for copy in proj:
        copy.wait_recv()
    proj_own.wait()
    grad = jnp.zeros(grad_tokens.shape, f32)
    for s in range(RANKS):
        query = wqkv_all[:, s, 0:64, :].reshape(-1, 128)
        rest = wqkv_all[:, s, 64:128, :].reshape(-1, 128)
        grad = grad + dot(proj_in[s, :, 0:128], query, ((1,), (1,)))
        grad = grad + dot(proj_in[s, :, 128:256], rest, ((1,), (1,)))
    moved, _ = norm_back(tokens[...].astype(f32), small[0:1, :], grad)
    grad_tokens[...] = hidden_grad[...] + moved
    for copy in third:
        copy.wait_recv()
    total = wide_pair[side].astype(f32) + wide_x[...].astype(f32)
    small_total = small_pair[side] + small_x[...]
    wo_out[...] = total[:RANKS].astype(bf16)
    wqkv_sum[:, 0:128] = total[RANKS]
    wqkv_sum[:, 128:256] = total[RANKS + 1]
    head_sum[...] = small_total[0:8]
    small_out[...] = small_total.reshape(small_out.shape)
    last = []
    for a, (src, dst) in enumerate(((wo_out, wo_last), (small_out, small_last))):
        sems = last_send.at[a], last_recv.at[a]
        last += [
            push(src.at[peer], dst.at[me], sems, k, {"tensor": peer}) for k, peer in enumerate(ranks)
        ]
    kept = [
        keep(wo_out.at[me], wo_last.at[me], local.at[1]),
        keep(small_out.at[me], small_last.at[me], local.at[2]),
    ]
    for copy in last:
        copy.wait_recv()
    for copy in kept:
        copy.wait()
    total = jnp.zeros(wo_sum.shape, f32)
    small_total = jnp.zeros(small_sum.shape, f32)
    for s in range(RANKS):
        total = total + wo_last[s].astype(f32)
        small_total = small_total + small_last[s]
    wo_sum[...] = total
    small_sum[...] = small_total
    for copy in (*proj, *first, *second, *third, *last):
        copy.wait_send()


def closing(proj_grad, wide, small_grad, wqkv_all, tokens, small, hidden_grad):
    dma = pltpu.SemaphoreType.DMA
    block, shard = wide.shape[3:], wide.shape[4]
    rows = shard // RANKS
    return pl.pallas_call(
        closing_kernel,
        out_shape=[
            jax.ShapeDtypeStruct(hidden_grad.shape, f32),
            jax.ShapeDtypeStruct((shard, 256), f32),
            jax.ShapeDtypeStruct((shard, 128), f32),
            jax.ShapeDtypeStruct((rows, 128), f32),
            jax.ShapeDtypeStruct((8, 128), f32),
        ],
        in_specs=whole(7),
        out_specs=whole(5),
        scratch_shapes=[
            pltpu.VMEM(proj_grad.shape, bf16),
            pltpu.VMEM((4, 2) + block, bf16),
            pltpu.VMEM((3, 2) + block, bf16),
            pltpu.VMEM(block, bf16),
            pltpu.VMEM((4, 2, shard, 128), f32),
            pltpu.VMEM((3, 2, shard, 128), f32),
            pltpu.VMEM((shard, 128), f32),
            pltpu.VMEM((4, 2) + block, bf16),
            pltpu.VMEM((2,) + block, bf16),
            pltpu.VMEM((4, 2, shard, 128), f32),
            pltpu.VMEM((2, shard, 128), f32),
            pltpu.VMEM((RANKS, shard, 128), bf16),
            pltpu.VMEM((RANKS, rows, 128), f32),
            pltpu.VMEM((RANKS, shard, 128), bf16),
            pltpu.VMEM((RANKS, rows, 128), f32),
            dma((7,)),
            dma((7,)),
            dma((5,)),
            dma((5,)),
            dma((5,)),
            dma((5,)),
            dma((2, 7)),
            dma((2, 7)),
            dma((3,)),
        ],
        compiler_params=pltpu.CompilerParams(
            collective_id=4, has_side_effects=True, vmem_limit_bytes=48 << 20
        ),
        name="closing",
    )(proj_grad, wide, small_grad, wqkv_all, tokens, small, hidden_grad)


def sequence_start(place, lengths):
    first, second = lengths[0], lengths[0] + lengths[1]
    return jnp.where(place < first, 0, jnp.where(place < second, first, second))


def swap_halves(x):
    return jnp.where(lane(x.shape) % 64 < 32, pltpu.roll(x, 96, 1), pltpu.roll(x, 32, 1))


def head_mean(x, heads):
    low = lane(x.shape) < 64
    first = jnp.sum(jnp.where(low, x, 0.0), axis=1, keepdims=True) / 64
    if heads == 1:
        return jnp.where(low, first, 0.0)
    second = jnp.sum(jnp.where(low, 0.0, x), axis=1, keepdims=True) / 64
    return jnp.where(low, first, second)


def head_gains(first_all):
    total = jnp.zeros((8, 128), f32)
    for g in range(GROUPS):
        piece = first_all[g, 128:144, :].astype(f32)[8:16]
        total = total + pltpu.roll(jnp.where(lane(piece.shape) < 4, piece, 0.0), 4 * g, 1)
    low = lane((1, 128)) < 64
    return jnp.where(low, total[0:1], pltpu.roll(total[1:2], 64, 1)), total[2:3]


def turned(table, block, b):
    within_cos, within_sin = table[0], table[1]
    block_cos, block_sin = block[0, pl.ds(b, 1), :], block[1, pl.ds(b, 1), :]
    cos = within_cos * block_cos - within_sin * block_sin
    sin = within_sin * block_cos + within_cos * block_sin
    return cos, jnp.where(lane(sin.shape) % 64 < 32, -sin, sin)


def attend_kernel(
    lengths, x, small, first_all, table, block, order_row, order_col,
    normed, proj, stream_qkv, mixed_stream, log_total, mixed, wqkv,
    token_qkv, keys, values,
):
    rows = x.shape[0]
    blocks = rows // ROW
    q_gain, k_gain = head_gains(first_all)
    wqkv[:, 0:128] = first_all[:, 0:64, :].reshape(-1, 128)
    wqkv[:, 128:256] = first_all[:, 64:128, :].reshape(-1, 128)

    @pl.loop(0, blocks)
    def _(b):
        at = pl.ds(pl.multiple_of(b * ROW, ROW), ROW)
        v = x[at, :].astype(f32)
        r = lax.rsqrt(jnp.mean(v * v, axis=1, keepdims=True) + EPS)
        n = (v * r * small[0:1, :]).astype(bf16)
        normed[at, :] = n
        p = dot(n, wqkv[...])
        proj[at, :] = p
        q, kv = p[:, :128], p[:, 128:]
        low = lane(kv.shape) < 64
        q = q * lax.rsqrt(head_mean(q * q, 2) + EPS) * q_gain
        k = kv * lax.rsqrt(head_mean(kv * kv, 1) + EPS) * k_gain
        token_qkv[at, 0:128] = q.astype(bf16)
        token_qkv[at, 128:256] = jnp.where(low, k, kv).astype(bf16)

    @pl.loop(0, blocks)
    def _(b):
        at = pl.ds(pl.multiple_of(b * ROW, ROW), ROW)
        place = sublane((ROW, rows)) + b * ROW
        moves = jnp.where(order_row[...] == place, 1.0, 0.0).astype(bf16)
        moved = dot(moves, token_qkv[...])
        cos, sin = turned(table, block, b)
        q, kv = moved[:, :128], moved[:, 128:]
        low = lane(kv.shape) < 64
        q = (q * cos + swap_halves(q) * sin) * 0.125
        kv = jnp.where(low, kv * cos + swap_halves(kv) * sin, kv)
        stream_qkv[at, 0:128] = q.astype(bf16)
        stream_qkv[at, 128:256] = kv.astype(bf16)
        other = pltpu.roll(kv, 64, 1)
        keys[at, :] = jnp.where(low, kv, other).astype(bf16)
        values[at, :] = jnp.where(low, other, 1.0).astype(bf16)

    @pl.loop(0, blocks)
    def _(b):
        at = pl.ds(pl.multiple_of(b * ROW, ROW), ROW)
        q = stream_qkv[at, 0:128]
        low = lane(q.shape) < 64
        zero = jnp.zeros_like(q)
        q0, q1 = jnp.where(low, q, zero), jnp.where(low, zero, q)
        place = sublane((ROW, 1)) + b * ROW
        start = sequence_start(place, lengths)
        first = sequence_start(b * ROW, lengths) // CHUNK
        last = (b * ROW + ROW - 1) // CHUNK + 1

        def step(j, totals):
            t0, t1 = totals
            here = pl.ds(pl.multiple_of(j * CHUNK, CHUNK), CHUNK)
            k, v = keys[here, :], values[here, :]
            key = lane((ROW, CHUNK)) + j * CHUNK
            allowed = (key <= place) & (key >= start)
            e0 = jnp.where(allowed, jnp.exp(dot(q0, k, ((1,), (1,)))), 0.0).astype(bf16)
            e1 = jnp.where(allowed, jnp.exp(dot(q1, k, ((1,), (1,)))), 0.0).astype(bf16)
            return t0 + dot(e0, v), t1 + dot(e1, v)

        none = jnp.zeros((ROW, 128), f32)
        t0, t1 = lax.fori_loop(first, last, step, (none, none))
        low = lane((ROW, 128)) < 64
        other0, other1 = pltpu.roll(t0, 64, 1), pltpu.roll(t1, 64, 1)
        total = jnp.where(low, other0, t1)
        out = jnp.where(low, t0, other1) / total
        log_total[at, :] = jnp.log(total)
        mixed_stream[at, :] = out.astype(bf16)

    @pl.loop(0, blocks)
    def _(b):
        at = pl.ds(pl.multiple_of(b * ROW, ROW), ROW)
        moves = jnp.where(order_col[at, :] == lane((ROW, rows)), 1.0, 0.0).astype(bf16)
        mixed[at, :] = dot(moves, mixed_stream[...]).astype(bf16)


def attend(lengths, x, small, first_all, table, block, order_row, order_col):
    rows, width = x.shape
    return pl.pallas_call(
        attend_kernel,
        out_shape=[
            jax.ShapeDtypeStruct((rows, width), bf16),
            jax.ShapeDtypeStruct((rows, 256), f32),
            jax.ShapeDtypeStruct((rows, 256), bf16),
            jax.ShapeDtypeStruct((rows, 128), bf16),
            jax.ShapeDtypeStruct((rows, 128), f32),
            jax.ShapeDtypeStruct((rows, 128), bf16),
            jax.ShapeDtypeStruct((width, 256), bf16),
        ],
        in_specs=[pl.BlockSpec(memory_space=pltpu.SMEM)] + whole(7),
        out_specs=whole(7),
        scratch_shapes=[
            pltpu.VMEM((rows, 256), bf16),
            pltpu.VMEM((rows, 128), bf16),
            pltpu.VMEM((rows, 128), bf16),
        ],
        compiler_params=pltpu.CompilerParams(vmem_limit_bytes=56 << 20),
        cost_estimate=pl.CostEstimate(flops=1000, bytes_accessed=1000, transcendentals=0),
        name="attend",
    )(lengths, x, small, first_all, table, block, order_row, order_col)


def attend_back_kernel(
    lengths, mixed_grad, stream_qkv, mixed_stream, log_total, proj, first_all, table, block,
    order_row, order_col, normed, wqkv, small, turn_grad,
    proj_grad, wqkv_grad, small_grad,
    gain_grad, keys, values, out_grad, query_grad, key_grad, value_grad, attn_gain,
):
    rows = proj.shape[0]
    blocks = rows // ROW
    q_gain, k_gain = head_gains(first_all)
    key_grad[...] = jnp.zeros_like(key_grad)
    value_grad[...] = jnp.zeros_like(value_grad)

    @pl.loop(0, blocks)
    def _(b):
        at = pl.ds(pl.multiple_of(b * ROW, ROW), ROW)
        place = sublane((ROW, rows)) + b * ROW
        moves = jnp.where(order_row[...] == place, 1.0, 0.0).astype(bf16)
        out_grad[at, :] = dot(moves, mixed_grad[...]).astype(bf16)
        kv = stream_qkv[at, 128:256].astype(f32)
        low = lane(kv.shape) < 64
        other = pltpu.roll(kv, 64, 1)
        keys[at, :] = jnp.where(low, kv, other).astype(bf16)
        values[at, :] = jnp.where(low, other, kv).astype(bf16)

    @pl.loop(0, blocks)
    def _(b):
        at = pl.ds(pl.multiple_of(b * ROW, ROW), ROW)
        q, g = stream_qkv[at, 0:128], out_grad[at, :]
        low = lane(q.shape) < 64
        zero = jnp.zeros_like(q)
        qs = jnp.where(low, q, zero), jnp.where(low, zero, q)
        gs = jnp.where(low, g, zero), jnp.where(low, zero, g)
        product = jnp.transpose(g.astype(f32) * mixed_stream[at, :].astype(f32))
        inner = (
            jnp.sum(product[:64], axis=0, keepdims=True),
            jnp.sum(product[64:], axis=0, keepdims=True),
        )
        logs = jnp.transpose(log_total[at, :])
        logs = logs[0:1], logs[64:65]
        place = lane((1, ROW)) + b * ROW
        start = sequence_start(place, lengths)
        first = sequence_start(b * ROW, lengths) // CHUNK
        last = (b * ROW + ROW - 1) // CHUNK + 1

        def step(j, totals):
            here = pl.ds(pl.multiple_of(j * CHUNK, CHUNK), CHUNK)
            k, v = keys[here, :], values[here, :]
            key = sublane((CHUNK, ROW)) + j * CHUNK
            allowed = (key <= place) & (key >= start)
            done = []
            kt, vt = key_grad[here, :], value_grad[here, :]
            for h in range(2):
                p = jnp.exp(dot(k, qs[h], ((1,), (1,))) - logs[h])
                p = jnp.where(allowed, p, 0.0)
                d = p * (dot(v, gs[h], ((1,), (1,))) - inner[h])
                p, d = p.astype(bf16), d.astype(bf16)
                vt = vt + dot(p, gs[h])
                kt = kt + dot(d, qs[h])
                done.append(totals[h] + dot(k, d, ((0,), (0,))))
            key_grad[here, :] = kt
            value_grad[here, :] = vt
            return tuple(done)

        none = jnp.zeros((128, ROW), f32)
        t0, t1 = lax.fori_loop(first, last, step, (none, none))
        grad = jnp.where(sublane((128, ROW)) < 64, t0, t1) * 0.125
        cos, sin = turned(table, block, b)
        cos, sin = jnp.transpose(cos), jnp.transpose(sin)
        swapped = jnp.concatenate([grad[32:64], grad[0:32], grad[96:128], grad[64:96]], axis=0)
        query_grad[:, at] = (grad * cos - swapped * sin).astype(bf16)

    gain_grad[...] = jnp.zeros_like(gain_grad)
    attn_gain[...] = jnp.zeros_like(attn_gain)

    @pl.loop(0, blocks)
    def _(b):
        at = pl.ds(pl.multiple_of(b * ROW, ROW), ROW)
        key, value = key_grad[at, :], value_grad[at, :]
        low = lane(key.shape) < 64
        key = key + pltpu.roll(key, 64, 1)
        cos, sin = turned(table, block, b)
        key = key * cos - swap_halves(key) * sin
        keys[at, :] = jnp.where(low, key, value + pltpu.roll(value, 64, 1)).astype(bf16)

    @pl.loop(0, blocks)
    def _(b):
        at = pl.ds(pl.multiple_of(b * ROW, ROW), ROW)
        moves = jnp.where(order_col[at, :] == lane((ROW, rows)), 1.0, 0.0).astype(bf16)
        dq = dot(moves, query_grad[...], ((1,), (1,)))
        dkv = dot(moves, keys[...])

        def back(grad, value, scales, heads):
            r = lax.rsqrt(head_mean(value * value, heads) + EPS)
            scaled = value * r
            weighted = grad * scales
            result = r * (weighted - scaled * head_mean(weighted * scaled, heads))
            return result, jnp.sum(grad * scaled, axis=0, keepdims=True)

        q_result, q_sum = back(dq, proj[at, 0:128], q_gain, 2)
        k_result, k_sum = back(dkv, proj[at, 128:256], k_gain, 1)
        q_low = q_result.astype(bf16)
        k_low = jnp.where(lane(dkv.shape) < 64, k_result, dkv).astype(bf16)
        proj_grad[at, 0:128] = q_low
        proj_grad[at, 128:256] = k_low
        gain_grad[0:1, :] += q_sum
        gain_grad[1:2, :] += k_sum
        part = dot(jnp.concatenate([q_low, k_low], axis=1), wqkv[...], ((1,), (1,)))
        part = part * normed[at, :].astype(f32)
        attn_gain[0:1, :] += jnp.sum(part, axis=0, keepdims=True)

    @pl.loop(0, normed.shape[1] // 256)
    def _(c):
        at = pl.ds(pl.multiple_of(c * 256, 256), 256)
        part = dot(normed[:, at], proj_grad[...], ((0,), (0,))).astype(bf16)
        own = pl.ds(c * 4, 4)
        wqkv_grad[own, 0] = part[:, 0:128].reshape(4, 64, 128)
        wqkv_grad[own, 1] = part[:, 128:256].reshape(4, 64, 128)

    heads = gain_grad[...]
    low = lane(heads.shape) < 64
    heads = jnp.concatenate(
        [
            jnp.where(low[0:1], heads[0:1], 0.0),
            jnp.where(low[0:1], pltpu.roll(heads[0:1], 64, 1), 0.0),
            jnp.where(low[0:1], heads[1:2], 0.0),
            jnp.zeros((5, 128), f32),
        ],
        axis=0,
    )
    spots = []
    for pair in range(GROUPS // 2):
        even = pltpu.roll(heads, (128 - 8 * pair) % 128, 1)
        odd = pltpu.roll(heads, (188 - 8 * pair) % 128, 1)
        at = lane(heads.shape)
        spots.append(jnp.where(at < 4, even, jnp.where((at >= 64) & (at < 68), odd, 0.0)))
    lines = [turn_grad[...], attn_gain[...] / small[0:1, :], jnp.concatenate(spots, axis=1)]
    lines.append(jnp.zeros((128 - 56, small.shape[1]), f32))
    small_grad[...] = jnp.transpose(jnp.concatenate(lines, axis=0))


def attend_back(
    lengths, mixed_grad, stream_qkv, mixed_stream, log_total, proj, first_all, table, block,
    order_row, order_col, normed, wqkv, small, turn_grad,
):
    rows, width = normed.shape
    return pl.pallas_call(
        attend_back_kernel,
        out_shape=[
            jax.ShapeDtypeStruct((rows, 256), bf16),
            jax.ShapeDtypeStruct((GROUPS, 2, width // GROUPS, 128), bf16),
            jax.ShapeDtypeStruct((width, 128), f32),
        ],
        in_specs=[pl.BlockSpec(memory_space=pltpu.SMEM)] + whole(14),
        out_specs=whole(3),
        scratch_shapes=[
            pltpu.VMEM((8, 128), f32),
            pltpu.VMEM((rows, 128), bf16),
            pltpu.VMEM((rows, 128), bf16),
            pltpu.VMEM((rows, 128), bf16),
            pltpu.VMEM((128, rows), bf16),
            pltpu.VMEM((rows, 128), f32),
            pltpu.VMEM((rows, 128), f32),
            pltpu.VMEM((8, width), f32),
        ],
        compiler_params=pltpu.CompilerParams(vmem_limit_bytes=56 << 20),
        cost_estimate=pl.CostEstimate(flops=1000, bytes_accessed=1000, transcendentals=0),
        name="attend_back",
    )(
        lengths, mixed_grad, stream_qkv, mixed_stream, log_total, proj, first_all, table, block,
        order_row, order_col, normed, wqkv, small, turn_grad,
    )


def experts_kernel(
    rank, rows_in, cot_in, routes, small, w,
    out_part, copy_part, wg,
    xs, us, weights, grads, x_buf, u_buf, og_s, inner_s, dgu_s, ranks, sem,
):
    e = pl.program_id(0)
    experts = pl.num_programs(0)
    blocks, held, width = xs.shape
    hidden = inner_s.shape[1]
    local = held // CAP

    def fetch(b, slot):
        return (
            pltpu.make_async_copy(rows_in.at[b], x_buf.at[slot], sem.at[0, slot]),
            pltpu.make_async_copy(cot_in.at[b], u_buf.at[slot], sem.at[1, slot]),
        )

    def table_of(b, i):
        slot = sublane((CAP, ROW))
        return ranks[b, pl.ds(i, 1), :] == slot

    @pl.when(e == 0)
    def _():
        for copy in fetch(0, 0):
            copy.start()
        pick = sublane((8, 32)) + rank[0] * local == lane((8, 32))
        pick = jnp.where(pick & (sublane((8, 32)) < local), 1.0, 0.0)
        before = jnp.where(sublane((ROW, ROW)) < lane((ROW, ROW)), 1.0, 0.0).astype(bf16)
        router = small[8:40, :].astype(bf16)

        @pl.loop(0, blocks)
        def _(b):
            slot = lax.rem(b, 2)

            @pl.when(b + 1 < blocks)
            def _():
                for copy in fetch(b + 1, 1 - slot):
                    copy.start()

            for copy in fetch(b, slot):
                copy.wait()
            x = x_buf[slot]
            named = named_of(routes[b])
            gates = gates_of(named, dot(router, x, ((1,), (1,))))
            own = lax.dot_general(
                pick,
                gates,
                (((1,), (0,)), ((), ())),
                precision=lax.Precision.HIGHEST,
                preferred_element_type=f32,
            )
            place = jnp.where(named > 0.5, dot(named.astype(bf16), before), -1.0)
            place = dot(pick.astype(bf16), place.astype(bf16))
            ranks[b] = place.astype(jnp.int32)
            u = u_buf[slot]
            for i in range(local):
                hit = table_of(b, i)
                table = jnp.where(hit, 1.0, 0.0).astype(bf16)
                here = pl.ds(i * CAP, CAP)
                xs[b, here, :] = dot(table, x).astype(bf16)
                us[b, here, :] = dot(table, u).astype(bf16)
                gate = jnp.sum(jnp.where(hit, own[i : i + 1], 0.0), axis=1, keepdims=True)
                weights[b, here, :] = jnp.broadcast_to(gate, (CAP, 128))

    group = blocks // 2
    tile = group * CAP

    @pl.loop(0, 2)
    def _(t):
        part = pl.ds(t * group, group)
        here = pl.ds(pl.multiple_of(e * CAP, CAP), CAP)
        flat = pl.ds(pl.multiple_of(t * tile, tile), tile)
        x = xs[part, here, :].reshape(tile, width)
        u = us[part, here, :].reshape(tile, width).astype(f32)
        gate = weights[part, here, :].reshape(tile, 128)[:, 0:1]
        gate_act = dot(x, w[0, 0])
        up_act = dot(x, w[0, 1])
        sig = 1.0 / (1.0 + jnp.exp(-gate_act))
        silu = gate_act * sig
        inner = (silu * up_act).astype(bf16)
        inner_s[flat, :] = inner
        result = dot(inner, w[0, 2], ((1,), (1,)))
        grad = jnp.sum(u * result, axis=1, keepdims=True)
        grads[part, here, :] = jnp.broadcast_to(grad, (tile, 128)).reshape(group, CAP, 128)
        us[part, here, :] = (gate * result).astype(bf16).reshape(group, CAP, width)
        og = (gate * u).astype(bf16)
        og_s[flat, :] = og
        inner_grad = dot(og, w[0, 2])
        dg = (inner_grad * up_act * (sig * (1.0 + gate_act * (1.0 - sig)))).astype(bf16)
        du = (inner_grad * silu).astype(bf16)
        dgu_s[flat, 0:hidden] = dg
        dgu_s[flat, hidden : 2 * hidden] = du

    col = 256

    @pl.loop(0, width // col)
    def _(c):
        at = pl.ds(pl.multiple_of(c * col, col), col)
        here = pl.ds(pl.multiple_of(e * CAP, CAP), CAP)
        x = xs[:, here, at].reshape(blocks * CAP, col)
        both = dot(x, dgu_s[...], ((0,), (0,)))
        wg[0, 0, at, :] = both[:, :hidden].astype(bf16)
        wg[0, 1, at, :] = both[:, hidden:].astype(bf16)
        wg[0, 2, at, :] = dot(og_s[:, at], inner_s[...], ((0,), (0,))).astype(bf16)

    @pl.loop(0, 2)
    def _(t):
        part = pl.ds(t * group, group)
        here = pl.ds(pl.multiple_of(e * CAP, CAP), CAP)
        flat = pl.ds(pl.multiple_of(t * tile, tile), tile)
        copy_grad = dot(dgu_s[flat, 0:hidden], w[0, 0], ((1,), (1,)))
        copy_grad += dot(dgu_s[flat, hidden : 2 * hidden], w[0, 1], ((1,), (1,)))
        xs[part, here, :] = copy_grad.astype(bf16).reshape(group, CAP, width)

    @pl.when(e == experts - 1)
    def _():
        def leave(b, slot):
            return (
                pltpu.make_async_copy(
                    x_buf.at[slot], copy_part.at[b, pl.ds(0, ROW)], sem.at[0, slot]
                ),
                pltpu.make_async_copy(u_buf.at[slot], out_part.at[b], sem.at[1, slot]),
            )

        def extra(b, slot):
            return pltpu.make_async_copy(
                og_s.at[pl.ds(slot * 16, 16)], copy_part.at[b, pl.ds(ROW, 16)], sem.at[2, slot]
            )

        @pl.loop(0, blocks)
        def _(b):
            slot = lax.rem(b, 2)

            @pl.when(b >= 2)
            def _():
                for copy in leave(b - 2, slot):
                    copy.wait()
                extra(b - 2, slot).wait()

            tables, lines = [], []
            for i in range(local):
                hit = table_of(b, i)
                tables.append(jnp.where(hit, 1.0, 0.0).astype(bf16))
                column = grads[b, pl.ds(i * CAP, CAP), :][:, 0:1]
                lines.append(jnp.sum(jnp.where(hit, column, 0.0), axis=0, keepdims=True))
            table = jnp.concatenate(tables, axis=0)
            x_buf[slot] = dot(table, xs[b], ((0,), (0,))).astype(bf16)
            u_buf[slot] = dot(table, us[b], ((0,), (0,))).astype(bf16)
            row = sublane((16, ROW))
            line = jnp.zeros((16, ROW), f32)
            for i in range(local):
                line = jnp.where(row == i, lines[i], line)
            high = line.astype(bf16).astype(f32)
            both = jnp.concatenate(
                [high, line - high, jnp.zeros((16, width - 2 * ROW), f32)], axis=1
            )
            og_s[pl.ds(pl.multiple_of(slot * 16, 16), 16), :] = both.astype(bf16)
            for copy in leave(b, slot):
                copy.start()
            extra(b, slot).start()

        for b in (blocks - 2, blocks - 1):
            for copy in leave(b, b % 2):
                copy.wait()
            extra(b, b % 2).wait()


def experts_part(rank, rows_in, cot_in, routes, small, expert_full):
    blocks, rows, width = rows_in.shape
    local, _, _, hidden = expert_full.shape
    slots = blocks * CAP
    any_space = pl.BlockSpec(memory_space=pl.ANY)
    one_expert = pl.BlockSpec((1, 3, width, hidden), lambda e: (e, 0, 0, 0))
    return pl.pallas_call(
        experts_kernel,
        grid=(local,),
        out_shape=[
            jax.ShapeDtypeStruct((blocks, rows, width), bf16),
            jax.ShapeDtypeStruct((blocks, rows + 16, width), bf16),
            jax.ShapeDtypeStruct((local, 3, width, hidden), bf16),
        ],
        in_specs=[pl.BlockSpec(memory_space=pltpu.SMEM), any_space, any_space] + whole(2) + [one_expert],
        out_specs=[any_space, any_space, one_expert],
        scratch_shapes=[
            pltpu.VMEM((blocks, local * CAP, width), bf16),
            pltpu.VMEM((blocks, local * CAP, width), bf16),
            pltpu.VMEM((blocks, local * CAP, 128), f32),
            pltpu.VMEM((blocks, local * CAP, 128), f32),
            pltpu.VMEM((2, rows, width), bf16),
            pltpu.VMEM((2, rows, width), bf16),
            pltpu.VMEM((slots, width), bf16),
            pltpu.VMEM((slots, hidden), bf16),
            pltpu.VMEM((slots, 2 * hidden), bf16),
            pltpu.VMEM((blocks, 8, ROW), jnp.int32),
            pltpu.SemaphoreType.DMA((3, 2)),
        ],
        compiler_params=pltpu.CompilerParams(vmem_limit_bytes=60 << 20),
        cost_estimate=pl.CostEstimate(
            flops=30_000_000_000, bytes_accessed=50 << 20, transcendentals=2_000_000
        ),
        name="experts",
    )(rank, rows_in, cot_in, routes, small, expert_full)


def exchange(x):
    return lax.all_to_all(x, "tensor", 0, 0, tiled=False)


def per_device(
    tokens,
    lengths,
    token_order,
    routes,
    cotangent,
    attn_gain,
    ffn_gain,
    router,
    w_query,
    w_key,
    w_value,
    w_output,
    query_gain,
    key_gain,
    w_gate,
    w_up,
    w_down,
):
    rows, width = tokens.shape
    group_rows = rows * RANKS
    experts = router.shape[1]
    rank = lax.axis_index("tensor")

    wkv = jnp.concatenate([w_key, w_value], axis=1)
    small_own = jnp.concatenate([attn_gain[:, None], ffn_gain[:, None], router], axis=1)
    small_own = jnp.pad(small_own, ((0, 0), (0, 128 - small_own.shape[1])))
    heads_own = jnp.concatenate([query_gain, key_gain], axis=0)
    heads_own = jnp.pad(heads_own, ((0, 5), (0, 124)))
    routes_own = routes.T.reshape(8, 2, 128).transpose(1, 0, 2).reshape(16, 128).astype(bf16)
    payload = jnp.concatenate(
        [w_query, wkv, small_own, heads_own, w_output.T, routes_own], axis=0
    )
    own_experts = jnp.stack([w_gate, w_up, w_down.transpose(0, 2, 1)], axis=1)
    expert_full = lax.all_gather(own_experts, "dp", axis=2, tiled=True)
    tokens_all, tiny_all, first_all, rest_all = opening(tokens, payload)
    first_all = first_all.reshape((GROUPS,) + first_all.shape[3:])
    rest_all = rest_all.reshape((GROUPS,) + rest_all.shape[3:])
    small = rest_all[:, :, 0:8, : 2 + experts].reshape(width, 2 + experts).T.astype(f32)
    small = jnp.concatenate([small[:2], jnp.zeros((6, width), f32), small[2:]], axis=0)
    cot_copies, tokens_all = lax.optimization_barrier((cotangent, tokens_all))
    cot_all = exchange(jnp.broadcast_to(cot_copies, (RANKS,) + cotangent.shape))

    feature = jnp.arange(128, dtype=jnp.int32) % 32
    frequency = ROTARY_BASE ** (-feature.astype(f32) / 32.0)
    within = jnp.arange(ROW, dtype=f32)[:, None] * frequency
    table = jnp.stack([jnp.cos(within), jnp.sin(within)])
    starts = (jnp.arange(8, dtype=f32) * ROW)[:, None] * frequency
    block = jnp.stack([jnp.cos(starts), jnp.sin(starts)])
    order_row, order_col = token_order, token_order.T
    normed_all, proj, stream_qkv, mixed_stream, log_total, mixed, wqkv = attend(
        lengths[0], tokens_all.reshape(group_rows, width), small, first_all, table, block,
        order_row, order_col,
    )
    mixed_own, hidden, normed2_all = middle(
        mixed.reshape(RANKS, rows, 128), rest_all, tokens, small
    )

    wqkv_cols, normed2_all = lax.optimization_barrier((tiny_all[:, :128], normed2_all))
    wqkv_all = lax.all_gather(wqkv_cols, "dp", axis=0, tiled=False)
    routes_all = tiny_all[:, 208:]
    out_part, copy_part, expert_grads = experts_part(
        rank[None], normed2_all, cot_all, routes_all, small, expert_full
    )
    expert_sums = lax.psum_scatter(expert_grads, "dp", scatter_dimension=2, tiled=True).astype(f32)
    back = exchange(copy_part)
    hidden_grad, mixed_grad, wo_grad, turn_grad = turn(
        back, hidden, cotangent, routes_own, small, mixed_own, rest_all
    )
    out_part, mixed_grad = lax.optimization_barrier((out_part, mixed_grad))
    out_pieces = exchange(out_part)

    proj_grad, wqkv_grad, small_grad = attend_back(
        lengths[0], mixed_grad.reshape(group_rows, 128), stream_qkv, mixed_stream, log_total,
        proj, first_all, table, block, order_row, order_col, normed_all, wqkv, small, turn_grad,
    )
    wide = jnp.concatenate([wo_grad, wqkv_grad], axis=1)
    grad_tokens, wqkv_sum, wo_sum, small_sum, head_sum = closing(
        proj_grad.reshape(RANKS, rows, 256), wide.reshape((4, 2, 2) + wide.shape[1:]),
        small_grad.reshape(4, 2, 2, -1, 128), wqkv_all, tokens, small, hidden_grad,
    )
    out_pieces, grad_tokens = lax.optimization_barrier((out_pieces, grad_tokens))
    layer_out = hidden + jnp.sum(out_pieces.astype(f32), axis=0)
    return (
        layer_out,
        grad_tokens,
        small_sum[:, 40],
        small_sum[:, 0],
        small_sum[:, 8:40],
        wqkv_sum[:, :128],
        wqkv_sum[:, 128:192],
        wqkv_sum[:, 192:256],
        wo_sum.T,
        head_sum[:4, 48:50].T,
        head_sum[:4, 50:51].T,
        expert_sums[:, 0],
        expert_sums[:, 1],
        expert_sums[:, 2].transpose(0, 2, 1),
    )


def solution(mesh):
    both = ("dp", "tensor")
    return jax.shard_map(
        per_device,
        mesh=mesh,
        in_specs=(
            P(both, None),
            P("dp", None),
            P("dp", None),
            P(both, None),
            P(both, None),
            P(both),
            P(both),
            P(both, None),
            P("dp", "tensor"),
            P("dp", "tensor"),
            P("dp", "tensor"),
            P("tensor", "dp"),
            P("tensor", "dp"),
            P("tensor", "dp"),
            P("tensor", "dp", None),
            P("tensor", "dp", None),
            P("tensor", None, "dp"),
        ),
        out_specs=(
            P(both, None),
            P(both, None),
            P(both),
            P(both),
            P(both, None),
            P("dp", "tensor"),
            P("dp", "tensor"),
            P("dp", "tensor"),
            P("tensor", "dp"),
            P("tensor", "dp"),
            P("tensor", "dp"),
            P("tensor", "dp", None),
            P("tensor", "dp", None),
            P("tensor", None, "dp"),
        ),
        check_vma=False,
    )
```

time: 1650 us -> 510 us (0.31)
  blocking collectives: 728 us -> 68.4 us
  waiting for transfers between devices: 433 us -> 60.2 us
  Pallas kernels: 0 us -> 312 us
  matrix products: 177 us -> 0 us
  local copies, waits for them, and re-layouts: 131 us -> 29.5 us
  other arithmetic: 107 us -> 16.2 us
  starting transfers between devices: 30.1 us -> 9.67 us
    all_gather x4 -> x0, blocking collectives: 477 us -> none  [the longest x1 407 us: per_device(): lax.all_gather(router, ('dp', 'tensor'), axis=0, tiled=True)]
    pallas_call x0 -> x7, Pallas kernels: none -> 312 us  [the longest x1 66.1 us: opening(): pl.pallas_call(opening_kernel, out_shape=[jax.ShapeDtypeStruct((RANKS,) +...]
    unnamed x3 -> x0, blocking collectives: 251 us -> none
    reduce_scatter x4 -> x1, waiting for transfers between devices: 235 us -> 0.01 us  [per_device(): lax.psum_scatter(expert_grads, 'dp', scatter_dimension=2, tiled=True)]
    dot_general x54 -> x0, matrix products: 177 us -> none  [the longest x4 16.3 us: backward_block(): jnp.einsum('krqs,qkrd->skd', prob_low, grad_block, preferred_element_type...]
    all_to_all x6 -> x2, waiting for transfers between devices: 151 us -> 60.2 us  [exchange(): return lax.all_to_all(x, 'tensor', 0, 0, tiled=False)]
    all_to_all x0 -> x1, blocking collectives: none -> 68.4 us  [exchange(): return lax.all_to_all(x, 'tensor', 0, 0, tiled=False)]
    all_gather x4 -> x2, waiting for transfers between devices: 47.3 us -> 0.01 us  [the longest x1 0.01 us: per_device(): expert_full = lax.all_gather(own_experts, 'dp', axis=2, tiled=True)]
  transfers between devices with their start and end apart: 16 -> 5, of which waited for: 8 -> 1; matrix products, arithmetic and copies ran while one was open for 22% -> 6% of each run, Pallas kernels for 0% -> 61%
where the time goes in v2:
time: 510 us
  Pallas kernels  312 us (61%)
  blocking collectives  68.4 us (13%)
  waiting for transfers between devices  60.2 us (12%)
  local copies, waits for them, and re-layouts  29.5 us (6%)
  other arithmetic  16.2 us (3%)
  between operations  14 us (3%)
  starting transfers between devices  9.67 us (2%)
    all_to_all x1, blocking collectives, exchange(): return lax.all_to_all(x, 'tensor', 0, 0, tiled=False)  68.4 us
    pallas_call x1, Pallas kernels, opening(): pl.pallas_call(opening_kernel, out_shape=[jax.ShapeDtypeStruct((RANKS,) +...  66.1 us
    all_to_all x2, waiting for transfers between devices, exchange(): return lax.all_to_all(x, 'tensor', 0, 0, tiled=False)  60.2 us
    pallas_call x1, Pallas kernels, experts_part(): pl.pallas_call(experts_kernel, grid=(local,), out_shape=[jax.ShapeDtypeSt...  59 us
    pallas_call x1, Pallas kernels, closing(): pl.pallas_call(closing_kernel, out_shape=[jax.ShapeDtypeStruct(hidden_gra...  58.5 us
    pallas_call x1, Pallas kernels, middle(): pl.pallas_call(middle_kernel, out_shape=[jax.ShapeDtypeStruct(mixed.shape...  48.2 us
    pallas_call x1, Pallas kernels, attend_back(): pl.pallas_call(attend_back_kernel, out_shape=[jax.ShapeDtypeStruct((rows,...  37.9 us
    pallas_call x1, Pallas kernels, attend(): pl.pallas_call(attend_kernel, out_shape=[jax.ShapeDtypeStruct((rows, widt...  28.2 us
  transfers between devices with their start and end apart: 5, of which 1 were waited for; matrix products, arithmetic and copies ran while one was open for 6% of the time, Pallas kernels for 61%

profile of v2, /device:TPU:0, one launch (start us, length us, event | category | flops | bytes accessed | tf_op | source)
XLA Modules:
  0.0 509.9 jit_solution(3072003135594752588)
XLA Ops:
  7.2 2.1 pad_maximum_fusion.1
  16.0 66.1 %opening.1 = (bf16[8,256,1024]{2,1,0:T(8,128)(2,1)}, bf16[8,224,128]{2,1,0:T(8,128)(2,1)}, bf16[4,2,2,144,128]{4,3,2,1,0:T(8,128)(2,1)}, bf16[4,2,2,8,80,128]{5,4,3,2,1,0:T(8,128)(2,1)}) custom-call(bf16[256,1024]{1,0:T(8,128)(2,1)} %tokens.5, bf16[224,128]{1,0:T(8,128)(2,1)} %copy-done.20), custom_call_target="tpu_custom_call" | custom-call | tf_op jit(solution)/shard_map/opening/pallas_call | solution.py:192
  83.4 1.3 copy.44.order_col
  87.5 28.2 %attend.1 = (bf16[2048,1024]{1,0:T(8,128)(2,1)}, f32[2048,256]{1,0:T(8,128)}, bf16[2048,256]{1,0:T(8,128)(2,1)}, bf16[2048,128]{1,0:T(8,128)(2,1)}, f32[2048,128...) custom-call(s32[3]{0:T(128)} %bitcast.65, bf16[2048,1024]{1,0:T(8,128)(2,1)} %bitcast.55, ...), custom_call_target="tpu_custom_call" | custom-call | flops 1000 | bytes 1000 | tf_op jit(solution)/shard_map/attend/pallas_call | solution.py:624
  116.8 48.2 %middle.1 = (bf16[8,256,128]{2,1,0:T(8,128)(2,1)S(1)}, f32[256,1024]{1,0:T(8,128)S(1)}, bf16[8,256,1024]{2,1,0:T(8,128)(2,1)S(1)}) custom-call(bf16[8,256,128]{2,1,0:T(8,128)(2,1)S(1)} %bitcast.52, bf16[16,8,80,128]{3,2,1,0:T(8,128)(2,1)S(1)} %bitcast.48, bf16[256,1024]{1,0:T(8,128)(2,1)S(1)} %copy-done.4, f32[40,1024]{1,0:T(8,128)S(1)} %copy-done.1), custom_call_target="tpu_custom_call" | custom-call | tf_op jit(solution)/shard_map/middle/pallas_call | solution.py:243
  166.8 2.0 copy-done.19
  168.8 1.7 slice.51
  170.5 3.6 broadcast_in_dim.23
  174.0 5.0 all-to-all-start
  179.0 1.4 slice.52.routes
  180.4 60.2 %all-to-all-done.cot_in = bf16[8,256,1024]{2,1,0:T(8,128)(2,1)} async-done(((bf16[8,256,1024]{2,1,0:T(8,128)(2,1)}), bf16[8,256,1024]{2,1,0:T(8,128)(2,1)}, u32[]{:S(2)}, u32[]{:S(2)}) %all-to-all-start) | async-done | bytes 4194336 | tf_op jit(solution)/shard_map/all_to_all | solution.py:1026
  240.6 59.0 %experts.1 = (bf16[8,256,1024]{2,1,0:T(8,128)(2,1)}, bf16[8,272,1024]{2,1,0:T(8,128)(2,1)}, bf16[4,3,1024,512]{3,2,1,0:T(8,128)(2,1)}) custom-call(s32[1]{0:T(128)} %bitcast.15.rank, bf16[8,256,1024]{2,1,0:T(8,128)(2,1)} %copy-done.19, bf16[8,256,1024]{2,1,0:T(8,128)(2,1)} %all-to-all-done.cot_in, bf16[8,16,128]{2,1,0:T(8,128)(2,1)} %slice.52.routes, ...), custom_call_target="tpu_custom_call" | custom-call | flops 30000001024 | bytes 52428800 | tf_op jit(solution)/shard_map/experts/pallas_call | solution.py:994
  299.7 68.4 %all_to_all.15.back = bf16[8,272,1024]{2,1,0:T(8,128)(2,1)} all-to-all(bf16[8,272,1024]{2,1,0:T(8,128)(2,1)} %get-tuple-element.62), channel_id=1, replica_groups=mesh['dp'=16,'tensor'=8] {'tensor'}, dimensions={0} | all-to-all | bytes 8912896 | tf_op jit(solution)/shard_map/all_to_all | solution.py:1026
  368.2 13.8 %turn.1 = (f32[256,1024]{1,0:T(8,128)S(1)}, bf16[8,256,128]{2,1,0:T(8,128)(2,1)S(1)}, bf16[16,8,64,128]{3,2,1,0:T(8,128)(2,1)S(1)}, f32[40,1024]{1,0:T(8,128)S(1)}) custom-call(bf16[8,272,1024]{2,1,0:T(8,128)(2,1)} %all_to_all.15.back, f32[256,1024]{1,0:T(8,128)S(1)} %copy-done.6, bf16[256,1024]{1,0:T(8,128)(2,1)S(1)} %copy-done.7, ...), custom_call_target="tpu_custom_call" | custom-call | tf_op jit(solution)/shard_map/turn/pallas_call | solution.py:345
  382.0 1.3 copy-done.8
  384.8 4.6 all-to-all-start.2
  389.4 37.9 %attend_back.1 = (bf16[2048,256]{1,0:T(8,128)(2,1)}, bf16[16,2,64,128]{3,2,1,0:T(8,128)(2,1)}, f32[1024,128]{1,0:T(8,128)}) custom-call(s32[3]{0:T(128)} %bitcast.66, bf16[2048,128]{1,0:T(8,128)(2,1)} %bitcast.51, bf16[2048,256]{1,0:T(8,128)(2,1)} %get-tuple-element.67.stream_qkv, bf16[2048,128]{1,0:T(8,128)(2,1)} %get-tuple-element.68.mixed_stream, ...), custom_call_target="tpu_custom_call" | custom-call | flops 1000 | bytes 1000 | tf_op jit(solution)/shard_map/attend_back/pallas_call | solution.py:793
  427.4 2.8 pad_maximum_fusion
  430.2 1.2 copy-done.10
  431.4 58.5 %closing.1 = (f32[256,1024]{1,0:T(8,128)S(1)}, f32[64,256]{1,0:T(8,128)S(1)}, f32[64,128]{1,0:T(8,128)S(1)}, f32[8,128]{1,0:T(8,128)S(1)}, f32[8,128]{1,0:T(8,128)S(1)}) custom-call(bf16[8,256,256]{2,1,0:T(8,128)(2,1)S(1)} %bitcast.49, bf16[4,2,2,10,64,128]{5,4,3,2,1,0:T(8,128)(2,1)} %bitcast.54, f32[4,2,2,64,128]{4,3,2,1,0:T(8,128)S(1)} %bitcast.50, ...), custom_call_target="tpu_custom_call" | custom-call | tf_op jit(solution)/shard_map/closing/pallas_call | solution.py:461
  494.9 3.2 convert_reduce_fusion
  498.1 1.1 add.26
  499.2 1.3 convert_element_type.53
  500.6 1.2 slice_bitcast_fusion
  (82 shorter events, 21.7 us)
Async XLA Ops:
  7.2 76.1 %copy-start.21 = (s32[1,2048]{1,0:T(1,128)S(1)}, s32[1,2048]{1,0:T(1,128)}, u32[]{:S(2)}) copy-start(s32[1,2048]{1,0:T(1,128)} %order_row.3) | copy-start | bytes 24580
  7.2 233.4 %all-gather.4.cloned.1.call-start = ((), (), s32[]{:S(2)}) async-start(), calls=%async_computation.4 | async-start | bytes 13369344 | tf_op jit(solution)/shard_map/all_gather | solution.py:1063
  9.4 420.8 %all-gather.6.cloned.1.call-start = ((), (), s32[]{:S(2)}) async-start(), calls=%async_computation.6 | async-start | bytes 4456448 | tf_op jit(solution)/shard_map/all_gather | solution.py:1088
  83.3 32.4 %copy-start = (bf16[4,2,2,8,80,128]{5,4,3,2,1,0:T(8,128)(2,1)S(1)}, bf16[4,2,2,8,80,128]{5,4,3,2,1,0:T(8,128)(2,1)}, u32[]{:S(2)}) copy-start(bf16[4,2,2,8,80,128]{5,4,3,2,1,0:T(8,128)(2,1)} %get-tuple-element.53) | copy-start | bytes 7864324
  83.3 32.4 %copy-start.4 = (bf16[256,1024]{1,0:T(8,128)(2,1)S(1)}, bf16[256,1024]{1,0:T(8,128)(2,1)}, u32[]{:S(2)}) copy-start(bf16[256,1024]{1,0:T(8,128)(2,1)} %tokens.5) | copy-start | bytes 1572868
  87.5 28.2 %copy-start.1 = (f32[40,1024]{1,0:T(8,128)S(1)}, f32[40,1024]{1,0:T(8,128)}, u32[]{:S(2)}) copy-start(f32[40,1024]{1,0:T(8,128)} %pad_maximum_fusion.3.small) | copy-start | bytes 491524
  115.7 1.0 copy-start.17
  165.0 1.0 copy-start.5
  166.0 0.8 copy-start.13
  166.8 2.0 copy-start.19
  174.0 66.6 %all-to-all-start = ((bf16[8,256,1024]{2,1,0:T(8,128)(2,1)}), bf16[8,256,1024]{2,1,0:T(8,128)(2,1)}, u32[]{:S(2)}, u32[]{:S(2)}) async-start(bf16[8,256,1024]{2,1,0:T(8,128)(2,1)} %broadcast_in_dim.23), calls=%async_computation | async-start | bytes 8388608 | tf_op jit(solution)/shard_map/all_to_all | solution.py:1026
  179.0 320.2 %reduce-scatter.2.cloned.1.call-start = ((), (), s32[]{:S(2)}) async-start(), calls=%async_computation.5 | async-start | bytes 13369344 | tf_op jit(solution)/shard_map/reduce_scatter | solution.py:1093
  299.7 68.5 %copy-start.2 = (f32[40,1024]{1,0:T(8,128)S(1)}, f32[40,1024]{1,0:T(8,128)}, u32[]{:S(2)}) copy-start(f32[40,1024]{1,0:T(8,128)} %pad_maximum_fusion.3.small) | copy-start | bytes 491524
  299.7 68.5 %copy-start.6 = (f32[256,1024]{1,0:T(8,128)S(1)}, f32[256,1024]{1,0:T(8,128)}, u32[]{:S(2)}) copy-start(f32[256,1024]{1,0:T(8,128)} %copy-done.5) | copy-start | bytes 3145732
  299.7 68.5 %copy-start.7 = (bf16[256,1024]{1,0:T(8,128)(2,1)S(1)}, bf16[256,1024]{1,0:T(8,128)(2,1)}, u32[]{:S(2)}) copy-start(bf16[256,1024]{1,0:T(8,128)(2,1)} %cotangent.1) | copy-start | bytes 1572868
  299.7 68.5 %copy-start.14 = (bf16[8,256,128]{2,1,0:T(8,128)(2,1)S(1)}, bf16[8,256,128]{2,1,0:T(8,128)(2,1)}, u32[]{:S(2)}) copy-start(bf16[8,256,128]{2,1,0:T(8,128)(2,1)} %copy-done.13) | copy-start | bytes 1572868
  382.0 1.4 copy-start.8
  384.8 110.1 %all-to-all-start.2 = ((bf16[8,256,1024]{2,1,0:T(8,128)(2,1)}), bf16[8,256,1024]{2,1,0:T(8,128)(2,1)}, u32[]{:S(2)}, u32[]{:S(2)}) async-start(bf16[8,256,1024]{2,1,0:T(8,128)(2,1)} %get-tuple-element.65), calls=%async_computation.2 | async-start | bytes 8388608 | tf_op jit(solution)/shard_map/all_to_all | solution.py:1026
  389.4 38.0 %copy-start.9 = (bf16[16,8,64,128]{3,2,1,0:T(8,128)(2,1)S(1)}, bf16[16,8,64,128]{3,2,1,0:T(8,128)(2,1)}, u32[]{:S(2)}) copy-start(bf16[16,8,64,128]{3,2,1,0:T(8,128)(2,1)} %copy-done.8) | copy-start | bytes 6291460
  427.3 2.8 copy-start.3
  427.3 2.8 copy-start.15
  430.2 1.2 copy-start.10
  489.9 1.0 copy-start.11
  498.1 3.7 copy-start.12
  (3 other events, 2.1 us)
Sparse Core Ops, SparseCore 0:
  10.5 101.6 all-gather.3
  170.6 69.1 all-gather.5
  299.8 168.6 reduce-scatter.1

commit v3 on v2

--- a/solution.py
+++ b/solution.py
@@ -2,6 +2,7 @@
 
 import jax
 import jax.numpy as jnp
+import numpy as np
 from jax import lax
 from jax.experimental import pallas as pl
 from jax.experimental.pallas import tpu as pltpu
@@ -32,6 +33,12 @@
     return lax.broadcasted_iota(jnp.int32, shape, len(shape) - 2)
 
 
+def cost_of(microseconds):
+    return pl.CostEstimate(
+        flops=microseconds * 1_100_000_000, bytes_accessed=1 << 20, transcendentals=0
+    )
+
+
 def whole(n):
     return [pl.BlockSpec(memory_space=pltpu.VMEM) for _ in range(n)]
 
@@ -82,41 +89,139 @@
     return me, here, there, there + z, right, left
 
 
-def start_rows(x, o, sems):
-    me, here, _, partner, right, left = neighbours()
-    return (
-        push(x, o.at[me], sems, 0, {"tensor": partner}),
-        push(x, o.at[me], sems, 1, {"tensor": here + right}),
-        push(x, o.at[me], sems, 2, {"tensor": here + left}),
-    )
-
-
-def pass_rows(first, o, sems):
-    _, here, there, partner, right, left = neighbours()
-    to_right, to_left = {"tensor": here + right}, {"tensor": here + left}
+def row_copy(index, x, o, sems):
+    me, here, there, partner, right, left = neighbours()
     half = o.shape[1] // 2
     low, high = pl.ds(0, half), pl.ds(half, half)
-    to_partner, own_right, own_left = first
-
-    def on(index, block, part, peer):
-        return push(o.at[block, part], o.at[block, part], sems, index, peer)
-
     both = pl.ds(0, 2 * half)
-    to_partner.wait_recv()
-    pass_right = on(3, partner, both, to_right)
-    pass_left = on(4, partner, both, to_left)
-    own_right.wait_recv()
-    far = [on(5, here + left, low, to_right)]
-    own_left.wait_recv()
-    far += [on(6, here + right, high, to_left)]
-    pass_right.wait_recv()
-    far += [on(7, there + left, low, to_right)]
-    pass_left.wait_recv()
-    far += [on(8, there + right, high, to_left)]
-    for copy in far:
-        copy.wait()
-    for copy in (*first, pass_right, pass_left):
-        copy.wait_send()
+    to_right, to_left = {"tensor": here + right}, {"tensor": here + left}
+    block, part, peer = (
+        (me, both, {"tensor": partner}),
+        (me, both, to_right),
+        (me, both, to_left),
+        (partner, both, to_right),
+        (partner, both, to_left),
+        (here + left, low, to_right),
+        (here + right, high, to_left),
+        (there + left, low, to_right),
+        (there + right, high, to_left),
+    )[index]
+    return pltpu.make_async_remote_copy(
+        src_ref=x if index < 3 else o.at[block, part],
+        dst_ref=o.at[block, part],
+        send_sem=sems[0].at[index],
+        recv_sem=sems[1].at[index],
+        device_id=peer,
+        device_id_type=MESH,
+    )
+
+
+def rows_begin(x, o, sems):
+    for index in range(3):
+        row_copy(index, x, o, sems).start()
+
+
+def rows_on(x, o, sems, arrived, leaving):
+    for index, later in zip(arrived, leaving):
+        row_copy(index, x, o, sems).wait_recv()
+        for other in later:
+            row_copy(other, x, o, sems).start()
+
+
+def rows_near(x, o, sems):
+    rows_on(x, o, sems, (1, 2, 0), ((5,), (6,), (3, 4)))
+
+
+def rows_far(x, o, sems):
+    rows_on(x, o, sems, (3, 4), ((7,), (8,)))
+
+
+def rows_end(x, o, sems):
+    for index in range(5, 9):
+        row_copy(index, x, o, sems).wait_recv()
+    for index in range(9):
+        row_copy(index, x, o, sems).wait_send()
+
+
+class RowSums:
+    def __init__(self, blocks, far, near, leaving, landed, sems):
+        self.blocks, self.far, self.near = blocks, far, near
+        self.leaving, self.landed, self.sems = leaving, landed, sems
+        self.me, here, there, self.partner, self.right, self.left = neighbours()
+        self.here, self.z, self.bases = here, self.me - here, (there, here)
+        self.half = blocks.shape[1] // 2
+        self.parts = pl.ds(0, self.half), pl.ds(self.half, self.half)
+
+    def copy(self, src, dst, index, peer):
+        return pltpu.make_async_remote_copy(
+            src_ref=src,
+            dst_ref=dst,
+            send_sem=self.sems[0].at[index],
+            recv_sem=self.sems[1].at[index],
+            device_id={"tensor": peer},
+            device_id_type=MESH,
+        )
+
+    def far_copy(self, side, way):
+        block = self.bases[side] + lax.rem(self.z + 2, 4)
+        peer = self.here + (self.right, self.left)[way]
+        src = self.blocks.at[block, self.parts[way]]
+        return self.copy(src, self.far.at[side, way], side * 4 + way, peer)
+
+    def near_copy(self, side, way):
+        step = (self.right, self.left)[way]
+        src = self.blocks.at[self.bases[side] + step]
+        return self.copy(src, self.near.at[side, way], side * 4 + 2 + way, self.here + step)
+
+    def cross_copy(self):
+        return self.copy(self.leaving, self.landed, 8, self.partner)
+
+    def begin(self, side):
+        for way in range(2):
+            self.far_copy(side, way).start()
+
+    def go_on(self, side):
+        for way in range(2):
+            self.far_copy(side, way).wait_recv()
+            at = self.bases[side] + (self.right, self.left)[way]
+            total = self.blocks[at, self.parts[way], :].astype(f32)
+            total = total + self.far[side, way].astype(f32)
+            self.blocks[at, self.parts[way], :] = total.astype(bf16)
+            self.near_copy(side, way).start()
+
+    def total(self, side):
+        total = self.blocks[self.bases[side] + self.z].astype(f32)
+        for way in range(2):
+            self.near_copy(side, way).wait_recv()
+            total = total + self.near[side, way].astype(f32)
+        return total
+
+    def cross(self):
+        self.leaving[...] = self.total(0).astype(bf16)
+        self.cross_copy().start()
+
+    def finish(self):
+        total = self.total(1)
+        self.cross_copy().wait_recv()
+        total = total + self.landed[...].astype(f32)
+        for side in range(2):
+            for way in range(2):
+                self.far_copy(side, way).wait_send()
+                self.near_copy(side, way).wait_send()
+        self.cross_copy().wait_send()
+        return total
+
+
+def row_sum_scratch(rows, width):
+    dma = pltpu.SemaphoreType.DMA
+    return [
+        pltpu.VMEM((2, 2, rows // 2, width), bf16),
+        pltpu.VMEM((2, 2, rows, width), bf16),
+        pltpu.VMEM((rows, width), bf16),
+        pltpu.VMEM((rows, width), bf16),
+        dma((9,)),
+        dma((9,)),
+    ]
 
 
 def group_place():
@@ -150,64 +255,118 @@
 
 
 def opening_kernel(
-    tokens, payload,
-    tokens_all, tiny_all, first_all, rest_all,
-    row_send, row_recv, tiny_send, tiny_recv, first_send, first_recv, rest_send, rest_recv, local,
+    tokens, w_query, w_key, w_value, w_output, attn_gain, ffn_gain, router, query_gain, key_gain, routes,
+    tokens_all, qkv_all, tiny_all, first_all, rest_all, small, routes_own,
+    payload, lines, small_rows,
+    row_send, row_recv, qkv_send, qkv_recv, tiny_send, tiny_recv, first_send, first_recv,
+    rest_send, rest_recv, local,
 ):
     me = lax.axis_index("tensor")
     y, side, core, across, column, other = group_place()
     ranks = others("tensor", RANKS)
+    lines[...] = jnp.zeros_like(lines)
+    lines[0, 0:1, 0:8] = attn_gain[...].astype(f32)
+    lines[0, 1:2, 0:8] = ffn_gain[...].astype(f32)
+    lines[1, :, 0:32] = router[...].astype(f32)
+    lines[2, 0:2, 0:4] = query_gain[...].astype(f32)
+    lines[2, 2:3, 0:4] = key_gain[...].astype(f32)
+    lines[3, :, 0:8] = jnp.transpose(lines[0])[0:8]
+    block = lines[3] + pltpu.roll(lines[1], 2, 1)
+    payload[0:64] = w_query[...]
+    payload[64:128, 0:64] = w_key[...]
+    payload[64:128, 64:128] = w_value[...]
+    payload[128:144] = jnp.concatenate([block, lines[2]], axis=0).astype(bf16)
+    payload[144:208] = jnp.transpose(w_output[...].astype(f32)).astype(bf16)
+    picks = routes[...].astype(f32)
+    picks = jnp.concatenate([picks[:, 0:128], picks[:, 128:256]], axis=0).astype(bf16)
+    payload[208:224] = picks
+    routes_own[...] = picks
     meet(ranks, [across["dp"], other["dp"]] + [peer["dp"] for _, peer in column])
+    own, qkv, rest = payload.at[0:144], payload.at[0:128], payload.at[128:224]
     tiny = [
-        push(payload, tiny_all.at[me], (tiny_send, tiny_recv), k, {"tensor": peer})
+        push(rest, tiny_all.at[me], (tiny_send, tiny_recv), k, {"tensor": peer})
         for k, peer in enumerate(ranks)
     ]
     first_sems, rest_sems = (first_send, first_recv), (rest_send, rest_recv)
-    own = payload.at[pl.ds(0, 144)]
     first_one = gather_first(own, first_all, first_sems)
-    rows = start_rows(tokens, tokens_all, (row_send, row_recv))
-    tiny_own = keep(payload, tiny_all.at[me], local.at[0])
+    row_sems = row_send, row_recv
+    rows_begin(tokens, tokens_all, row_sems)
+    tiny_own = keep(rest, tiny_all.at[me], local.at[0])
     first_own = keep(own, first_all.at[y, side, core], local.at[1])
-    tokens_own = keep(tokens, tokens_all.at[me], local.at[2])
-    first_two = gather_second(first_one, first_own, first_all, first_sems)
+    kept = [
+        keep(tokens, tokens_all.at[me], local.at[2]),
+        keep(qkv, qkv_all.at[me], local.at[3]),
+    ]
     for copy in tiny:
         copy.wait_recv()
     tiny_own.wait()
-    part = tiny_all.at[:, pl.ds(128, 80)]
+    part = tiny_all.at[:, pl.ds(0, 80)]
     rest_one = gather_first(part, rest_all, rest_sems)
-    rest_own = keep(part, rest_all.at[y, side, core], local.at[3])
+    rest_own = keep(part, rest_all.at[y, side, core], local.at[4])
+    first_two = gather_second(first_one, first_own, first_all, first_sems)
+    rows_near(tokens, tokens_all, row_sems)
+    rest_two = gather_second(rest_one, rest_own, rest_all, rest_sems)
     first_three = gather_third(first_two, first_all, first_sems)
-    rest_two = gather_second(rest_one, rest_own, rest_all, rest_sems)
-    pass_rows(rows, tokens_all, (row_send, row_recv))
+    qkv_sent = [
+        push(qkv, qkv_all.at[me], (qkv_send, qkv_recv), k, {"tensor": peer})
+        for k, peer in enumerate(ranks)
+    ]
+    rows_far(tokens, tokens_all, row_sems)
     rest_three = gather_third(rest_two, rest_all, rest_sems)
+    rest_three.wait_recv()
+    gathered = keep(rest_all.at[:, :, :, :, pl.ds(0, 16)], small_rows, local.at[5])
+    gathered.wait()
+    turned_rows = jnp.transpose(small_rows[:, :, :, :, 0:8, :].astype(f32).reshape(-1, 128))
+    small[0:8] = turned_rows[0:8]
+    small[8:40] = turned_rows[2:34]
+    rows_end(tokens, tokens_all, row_sems)
     first_three.wait()
-    rest_three.wait()
+    rest_three.wait_send()
+    for copy in qkv_sent:
+        copy.wait()
     for copy in (*tiny, first_one, rest_one, *first_two, *rest_two):
         copy.wait_send()
-    tokens_own.wait()
-
-
-def opening(tokens, payload):
+    for copy in kept:
+        copy.wait()
+
+
+def opening(tokens, *weights):
     dma = pltpu.SemaphoreType.DMA
+    like = jax.ShapeDtypeStruct
     return pl.pallas_call(
         opening_kernel,
         out_shape=[
-            jax.ShapeDtypeStruct((RANKS,) + tokens.shape, bf16),
-            jax.ShapeDtypeStruct((RANKS,) + payload.shape, bf16),
-            jax.ShapeDtypeStruct((4, 2, 2, 144, 128), bf16),
-            jax.ShapeDtypeStruct((4, 2, 2, RANKS, 80, 128), bf16),
-        ],
-        in_specs=anywhere(2),
-        out_specs=anywhere(4),
-        scratch_shapes=[dma((9,)), dma((9,)), dma((7,)), dma((7,))] + [dma((5,))] * 4 + [dma((4,))],
-        compiler_params=pltpu.CompilerParams(collective_id=1, has_side_effects=True),
+            like((RANKS,) + tokens.shape, bf16),
+            like((RANKS, 128, 128), bf16),
+            like((RANKS, 96, 128), bf16),
+            like((4, 2, 2, 144, 128), bf16),
+            like((4, 2, 2, RANKS, 80, 128), bf16),
+            like((40, tokens.shape[1]), f32),
+            like((16, 128), bf16),
+        ],
+        in_specs=anywhere(1) + whole(10),
+        out_specs=anywhere(5) + whole(2),
+        scratch_shapes=[
+            pltpu.VMEM((224, 128), bf16),
+            pltpu.VMEM((4, 8, 128), f32),
+            pltpu.VMEM((4, 2, 2, RANKS, 16, 128), bf16),
+            dma((9,)),
+            dma((9,)),
+        ]
+        + [dma((7,))] * 4
+        + [dma((5,))] * 4
+        + [dma((6,))],
+        compiler_params=pltpu.CompilerParams(
+            collective_id=1, has_side_effects=True, vmem_limit_bytes=40 << 20
+        ),
+        cost_estimate=cost_of(50),
         name="opening",
-    )(tokens, payload)
+    )(tokens, *weights)
 
 
 def middle_kernel(
     mixed, rest, tokens, small,
-    mixed_own, hidden, normed2_all,
+    mixed_own, hidden, normed2_all, done,
     landed, normed2, mix_send, mix_recv, row_send, row_recv, local,
 ):
     me, here, _, partner, right, left = neighbours()
@@ -229,12 +388,16 @@
     hidden[...] = total
     scale = lax.rsqrt(jnp.mean(total * total, axis=1, keepdims=True) + EPS)
     normed2[...] = (total * scale * small[1:2, :]).astype(bf16)
-    rows = start_rows(normed2, normed2_all, (row_send, row_recv))
+    row_sems = row_send, row_recv
+    rows_begin(normed2, normed2_all, row_sems)
     kept = keep(normed2, normed2_all.at[me], local.at[1])
-    pass_rows(rows, normed2_all, (row_send, row_recv))
+    rows_near(normed2, normed2_all, row_sems)
+    rows_far(normed2, normed2_all, row_sems)
+    rows_end(normed2, normed2_all, row_sems)
     for copy in sent:
         copy.wait_send()
     kept.wait()
+    done[...] = jnp.zeros_like(done)
 
 
 def middle(mixed, rest, tokens, small):
@@ -246,9 +409,10 @@
             jax.ShapeDtypeStruct(mixed.shape, bf16),
             jax.ShapeDtypeStruct((rows, width), f32),
             jax.ShapeDtypeStruct((RANKS, rows, width), bf16),
-        ],
-        in_specs=whole(4),
-        out_specs=whole(2) + anywhere(1),
+            jax.ShapeDtypeStruct((8, 128), f32),
+        ],
+        in_specs=anywhere(1) + whole(3),
+        out_specs=whole(2) + anywhere(1) + whole(1),
         scratch_shapes=[
             pltpu.VMEM(mixed.shape, bf16),
             pltpu.VMEM((rows, width), bf16),
@@ -261,6 +425,7 @@
         compiler_params=pltpu.CompilerParams(
             collective_id=2, has_side_effects=True, vmem_limit_bytes=40 << 20
         ),
+        cost_estimate=cost_of(40),
         name="middle",
     )(mixed, rest, tokens, small)
 
@@ -303,17 +468,12 @@
     scale = lax.rsqrt(jnp.mean(value * value, axis=1, keepdims=True) + EPS)
     normed2 = (value * scale * gain).astype(bf16)
     gates = gates_of(named_of(routes[...]), dot(router, normed2, ((1,), (1,))))
-    pieces = back[:, ROW : ROW + 16, 0 : 2 * ROW].reshape(RANKS * 16, 2 * ROW)
-    order = lane((32, RANKS * 16))
-    expert = order // 16 * 4 + order % 16
-    spread = jnp.where((expert == sublane(order.shape)) & (order % 16 < 4), 1.0, 0.0).astype(bf16)
-    pieces = dot(spread, pieces)
+    pieces = back[ROW:, 0 : 2 * ROW]
     gate_grad = pieces[:, :ROW] + pieces[:, ROW:]
     inner = jnp.sum(gates * gate_grad, axis=0, keepdims=True)
     logit_grad = (gates * (gate_grad - inner)).astype(bf16)
     grad = dot(logit_grad, router, ((0,), (0,)))
-    for s in range(RANKS):
-        grad = grad + back[s, 0:ROW, :].astype(f32)
+    grad = grad + back[0:ROW, :]
     moved, scaled = norm_back(value, gain, grad)
     total = cotangent[...].astype(f32) + moved
     branch = total.astype(bf16)
@@ -362,53 +522,57 @@
         compiler_params=pltpu.CompilerParams(
             collective_id=3, has_side_effects=True, vmem_limit_bytes=48 << 20
         ),
+        cost_estimate=cost_of(15),
         name="turn",
     )(back, hidden, cotangent, routes, small, mixed_own, rest)
 
 
 def closing_kernel(
-    proj_grad, wide, small_grad, wqkv_all, tokens, small, hidden_grad,
+    proj_grad, wo_grad, wqkv_grad, small_grad, wqkv_all, tokens, small, hidden_grad,
     grad_tokens, wqkv_sum, wo_sum, small_sum, head_sum,
-    proj_in, wide_core, wide_y, wide_x, small_core, small_y, small_x,
-    wide_half, wide_pair, small_half, small_pair, wo_out, small_out, wo_last, small_last,
-    proj_send, proj_recv, wide_send, wide_recv, small_send, small_recv, last_send, last_recv, local,
+    proj_in,
+    wo_core, wo_y, wo_x, wo_half, wo_pair,
+    wqkv_core, wqkv_y, wqkv_x, wqkv_half, wqkv_pair,
+    small_core, small_y, small_x, small_half, small_pair,
+    wo_out, small_out, wo_last, small_last,
+    proj_send, proj_recv, group_send, group_recv, last_send, last_recv, local,
 ):
     me = lax.axis_index("tensor")
     y, side, core, across, column, other = group_place()
     ranks = others("tensor", RANKS)
     meet(ranks, [across["dp"], other["dp"]] + [peer["dp"] for _, peer in column])
-    wide_sems, small_sems = (wide_send, wide_recv), (small_send, small_recv)
     away = 1 - core
+    arrays = (
+        (wo_grad, wo_core, wo_half, wo_y, wo_pair, wo_x),
+        (wqkv_grad, wqkv_core, wqkv_half, wqkv_y, wqkv_pair, wqkv_x),
+        (small_grad, small_core, small_half, small_y, small_pair, small_x),
+    )
+    sems = [(group_send.at[a], group_recv.at[a]) for a in range(3)]
     first = [
-        push(wide.at[:, :, away], wide_core, wide_sems, 0, other),
-        push(small_grad.at[:, :, away], small_core, small_sems, 0, other),
+        push(array[0].at[:, :, away], array[1], sems[a], 0, other) for a, array in enumerate(arrays)
     ]
     proj = [
         push(proj_grad.at[peer], proj_in.at[me], (proj_send, proj_recv), k, {"tensor": peer})
         for k, peer in enumerate(ranks)
     ]
     proj_own = keep(proj_grad.at[me], proj_in.at[me], local.at[0])
-    for copy in first:
-        copy.wait_recv()
-    wide_half[...] = (wide[:, :, core].astype(f32) + wide_core[...].astype(f32)).astype(bf16)
-    small_half[...] = small_grad[:, :, core] + small_core[...]
     second = []
-    for k, (at, peer) in enumerate(column):
-        second.append(push(wide_half.at[at], wide_y.at[k], wide_sems, 1 + k, peer))
-        second.append(push(small_half.at[at], small_y.at[k], small_sems, 1 + k, peer))
-    for copy in second:
-        copy.wait_recv()
-    total = wide_half[y].astype(f32)
-    small_total = small_half[y]
-    for k in range(3):
-        total = total + wide_y[k].astype(f32)
-        small_total = small_total + small_y[k]
-    wide_pair[...] = total.astype(bf16)
-    small_pair[...] = small_total
-    third = [
-        push(wide_pair.at[1 - side], wide_x, wide_sems, 4, across),
-        push(small_pair.at[1 - side], small_x, small_sems, 4, across),
-    ]
+    for a, (whole_grad, landed, half, down, _, _) in enumerate(arrays):
+        first[a].wait_recv()
+        total = whole_grad[:, :, core].astype(f32) + landed[...].astype(f32)
+        half[...] = total.astype(half.dtype)
+        second.append(
+            [push(half.at[at], down.at[k], sems[a], 1 + k, peer) for k, (at, peer) in enumerate(column)]
+        )
+    third = []
+    for a, (_, _, half, down, pair, far) in enumerate(arrays):
+        for copy in second[a]:
+            copy.wait_recv()
+        total = half[y].astype(f32)
+        for k in range(3):
+            total = total + down[k].astype(f32)
+        pair[...] = total.astype(pair.dtype)
+        third.append(push(pair.at[1 - side], far, sems[a], 4, across))
     for copy in proj:
         copy.wait_recv()
     proj_own.wait()
@@ -420,25 +584,25 @@
         grad = grad + dot(proj_in[s, :, 128:256], rest, ((1,), (1,)))
     moved, _ = norm_back(tokens[...].astype(f32), small[0:1, :], grad)
     grad_tokens[...] = hidden_grad[...] + moved
-    for copy in third:
-        copy.wait_recv()
-    total = wide_pair[side].astype(f32) + wide_x[...].astype(f32)
-    small_total = small_pair[side] + small_x[...]
-    wo_out[...] = total[:RANKS].astype(bf16)
-    wqkv_sum[:, 0:128] = total[RANKS]
-    wqkv_sum[:, 128:256] = total[RANKS + 1]
-    head_sum[...] = small_total[0:8]
-    small_out[...] = small_total.reshape(small_out.shape)
+    sums = []
+    for a, (_, _, _, _, pair, far) in enumerate(arrays):
+        third[a].wait_recv()
+        sums.append(pair[side].astype(f32) + far[...].astype(f32))
+    wo_out[...] = sums[0].astype(bf16)
+    head_sum[...] = sums[2][0:8]
+    small_out[...] = sums[2].reshape(small_out.shape)
     last = []
     for a, (src, dst) in enumerate(((wo_out, wo_last), (small_out, small_last))):
-        sems = last_send.at[a], last_recv.at[a]
+        pair = last_send.at[a], last_recv.at[a]
         last += [
-            push(src.at[peer], dst.at[me], sems, k, {"tensor": peer}) for k, peer in enumerate(ranks)
+            push(src.at[peer], dst.at[me], pair, k, {"tensor": peer}) for k, peer in enumerate(ranks)
         ]
     kept = [
         keep(wo_out.at[me], wo_last.at[me], local.at[1]),
         keep(small_out.at[me], small_last.at[me], local.at[2]),
     ]
+    wqkv_sum[:, 0:128] = sums[1][0]
+    wqkv_sum[:, 128:256] = sums[1][1]
     for copy in last:
         copy.wait_recv()
     for copy in kept:
@@ -450,14 +614,22 @@
         small_total = small_total + small_last[s]
     wo_sum[...] = total
     small_sum[...] = small_total
-    for copy in (*proj, *first, *second, *third, *last):
+    for copy in (*proj, *first, *third, *last):
         copy.wait_send()
-
-
-def closing(proj_grad, wide, small_grad, wqkv_all, tokens, small, hidden_grad):
+    for copies in second:
+        for copy in copies:
+            copy.wait_send()
+
+
+def closing(proj_grad, wo_grad, wqkv_grad, small_grad, wqkv_all, tokens, small, hidden_grad):
     dma = pltpu.SemaphoreType.DMA
-    block, shard = wide.shape[3:], wide.shape[4]
+    shard = wo_grad.shape[4]
     rows = shard // RANKS
+    steps = []
+    for array in (wo_grad, wqkv_grad, small_grad):
+        block = array.shape[3:]
+        for lead in ((4, 2), (3, 2), (), (4, 2), (2,)):
+            steps.append(pltpu.VMEM(lead + block, array.dtype))
     return pl.pallas_call(
         closing_kernel,
         out_shape=[
@@ -467,39 +639,29 @@
             jax.ShapeDtypeStruct((rows, 128), f32),
             jax.ShapeDtypeStruct((8, 128), f32),
         ],
-        in_specs=whole(7),
+        in_specs=whole(8),
         out_specs=whole(5),
         scratch_shapes=[
             pltpu.VMEM(proj_grad.shape, bf16),
-            pltpu.VMEM((4, 2) + block, bf16),
-            pltpu.VMEM((3, 2) + block, bf16),
-            pltpu.VMEM(block, bf16),
-            pltpu.VMEM((4, 2, shard, 128), f32),
-            pltpu.VMEM((3, 2, shard, 128), f32),
-            pltpu.VMEM((shard, 128), f32),
-            pltpu.VMEM((4, 2) + block, bf16),
-            pltpu.VMEM((2,) + block, bf16),
-            pltpu.VMEM((4, 2, shard, 128), f32),
-            pltpu.VMEM((2, shard, 128), f32),
+            *steps,
             pltpu.VMEM((RANKS, shard, 128), bf16),
             pltpu.VMEM((RANKS, rows, 128), f32),
             pltpu.VMEM((RANKS, shard, 128), bf16),
             pltpu.VMEM((RANKS, rows, 128), f32),
             dma((7,)),
             dma((7,)),
-            dma((5,)),
-            dma((5,)),
-            dma((5,)),
-            dma((5,)),
+            dma((3, 5)),
+            dma((3, 5)),
             dma((2, 7)),
             dma((2, 7)),
             dma((3,)),
         ],
         compiler_params=pltpu.CompilerParams(
-            collective_id=4, has_side_effects=True, vmem_limit_bytes=48 << 20
+            collective_id=4, has_side_effects=True, vmem_limit_bytes=62 << 20
         ),
+        cost_estimate=cost_of(45),
         name="closing",
-    )(proj_grad, wide, small_grad, wqkv_all, tokens, small, hidden_grad)
+    )(proj_grad, wo_grad, wqkv_grad, small_grad, wqkv_all, tokens, small, hidden_grad)
 
 
 def sequence_start(place, lengths):
@@ -640,7 +802,7 @@
             pltpu.VMEM((rows, 128), bf16),
         ],
         compiler_params=pltpu.CompilerParams(vmem_limit_bytes=56 << 20),
-        cost_estimate=pl.CostEstimate(flops=1000, bytes_accessed=1000, transcendentals=0),
+        cost_estimate=cost_of(30),
         name="attend",
     )(lengths, x, small, first_all, table, block, order_row, order_col)
 
@@ -810,7 +972,7 @@
             pltpu.VMEM((8, width), f32),
         ],
         compiler_params=pltpu.CompilerParams(vmem_limit_bytes=56 << 20),
-        cost_estimate=pl.CostEstimate(flops=1000, bytes_accessed=1000, transcendentals=0),
+        cost_estimate=cost_of(40),
         name="attend_back",
     )(
         lengths, mixed_grad, stream_qkv, mixed_stream, log_total, proj, first_all, table, block,
@@ -819,32 +981,66 @@
 
 
 def experts_kernel(
-    rank, rows_in, cot_in, routes, small, w,
-    out_part, copy_part, wg,
-    xs, us, weights, grads, x_buf, u_buf, og_s, inner_s, dgu_s, ranks, sem,
+    rows_in, cotangent, hidden_in, routes, small, w,
+    cot_all, layer_out, copy_part, xs_out, us_out, inner_out, dgu_out,
+    xs, us, ys, weights, grads, acts, inner_s, dgu_s, ranks, x_buf, u_buf,
+    outs, far, near, leaving, landed, sum_send, sum_recv,
+    row_send, row_recv, sem, local_sem, out_sem,
 ):
-    e = pl.program_id(0)
-    experts = pl.num_programs(0)
+    step = pl.program_id(0)
+    me = lax.axis_index("tensor")
     blocks, held, width = xs.shape
+    local = held // CAP
     hidden = inner_s.shape[1]
-    local = held // CAP
-
-    def fetch(b, slot):
+    e = lax.rem(step, local)
+    here = pl.ds(pl.multiple_of(e * CAP, CAP), CAP)
+    slots = blocks * CAP
+    group = blocks // 2
+    tile = group * CAP
+    row_sems = row_send, row_recv
+    long = ROW + 32
+
+    def fetch_rows(b, slot):
+        return pltpu.make_async_copy(rows_in.at[b], x_buf.at[slot], sem.at[0, slot])
+
+    def fetch_cot(b, slot):
+        return pltpu.make_async_copy(cot_all.at[b], u_buf.at[slot], sem.at[1, slot])
+
+    sums = RowSums(outs, far, near, leaving, landed, (sum_send, sum_recv))
+
+    def save_xs(b):
+        return pltpu.make_async_copy(xs.at[b], xs_out.at[b], out_sem.at[0, b])
+
+    def save_us(b):
+        return pltpu.make_async_copy(us.at[b], us_out.at[b], out_sem.at[1, b])
+
+    def save_tile(k):
+        flat = pl.ds(pl.multiple_of(k * tile, tile), tile)
         return (
-            pltpu.make_async_copy(rows_in.at[b], x_buf.at[slot], sem.at[0, slot]),
-            pltpu.make_async_copy(cot_in.at[b], u_buf.at[slot], sem.at[1, slot]),
+            pltpu.make_async_copy(dgu_s.at[flat], dgu_out.at[flat], out_sem.at[2, k]),
+            pltpu.make_async_copy(inner_s.at[flat], inner_out.at[flat], out_sem.at[3, k]),
         )
 
-    def table_of(b, i):
+    def save_back(b):
+        flat = pl.ds(pl.multiple_of(b * long, 32), long)
+        return pltpu.make_async_copy(acts.at[flat], copy_part.at[b], out_sem.at[4, b])
+
+    def hits_of(b):
         slot = sublane((CAP, ROW))
-        return ranks[b, pl.ds(i, 1), :] == slot
-
-    @pl.when(e == 0)
+        return [ranks[b, i : i + 1, :] == slot for i in range(local)]
+
+    def table_of(hits):
+        return jnp.concatenate([jnp.where(hit, 1.0, 0.0).astype(bf16) for hit in hits], axis=0)
+
+    @pl.when(step == 0)
     def _():
-        for copy in fetch(0, 0):
-            copy.start()
-        pick = sublane((8, 32)) + rank[0] * local == lane((8, 32))
-        pick = jnp.where(pick & (sublane((8, 32)) < local), 1.0, 0.0)
+        _, near, _, partner, right, left = neighbours()
+        meet(others("tensor", blocks), [])
+        rows_begin(cotangent, cot_all, row_sems)
+        keep(cotangent, cot_all.at[me], local_sem.at[0])
+        fetch_rows(0, 0).start()
+        pick = (sublane((8, 32)) + me * local == lane((8, 32))) & (sublane((8, 32)) < local)
+        pick = jnp.where(pick, 1.0, 0.0)
         before = jnp.where(sublane((ROW, ROW)) < lane((ROW, ROW)), 1.0, 0.0).astype(bf16)
         router = small[8:40, :].astype(bf16)
 
@@ -854,13 +1050,11 @@
 
             @pl.when(b + 1 < blocks)
             def _():
-                for copy in fetch(b + 1, 1 - slot):
-                    copy.start()
-
-            for copy in fetch(b, slot):
-                copy.wait()
+                fetch_rows(b + 1, 1 - slot).start()
+
+            fetch_rows(b, slot).wait()
             x = x_buf[slot]
-            named = named_of(routes[b])
+            named = named_of(routes[b, 80:96, :])
             gates = gates_of(named, dot(router, x, ((1,), (1,))))
             own = lax.dot_general(
                 pick,
@@ -872,158 +1066,301 @@
             place = jnp.where(named > 0.5, dot(named.astype(bf16), before), -1.0)
             place = dot(pick.astype(bf16), place.astype(bf16))
             ranks[b] = place.astype(jnp.int32)
-            u = u_buf[slot]
+            hits = hits_of(b)
+            xs[b] = dot(table_of(hits), x).astype(bf16)
+            save_xs(b).start()
             for i in range(local):
-                hit = table_of(b, i)
-                table = jnp.where(hit, 1.0, 0.0).astype(bf16)
-                here = pl.ds(i * CAP, CAP)
-                xs[b, here, :] = dot(table, x).astype(bf16)
-                us[b, here, :] = dot(table, u).astype(bf16)
-                gate = jnp.sum(jnp.where(hit, own[i : i + 1], 0.0), axis=1, keepdims=True)
-                weights[b, here, :] = jnp.broadcast_to(gate, (CAP, 128))
-
-    group = blocks // 2
-    tile = group * CAP
-
-    @pl.loop(0, 2)
-    def _(t):
-        part = pl.ds(t * group, group)
-        here = pl.ds(pl.multiple_of(e * CAP, CAP), CAP)
-        flat = pl.ds(pl.multiple_of(t * tile, tile), tile)
-        x = xs[part, here, :].reshape(tile, width)
-        u = us[part, here, :].reshape(tile, width).astype(f32)
-        gate = weights[part, here, :].reshape(tile, 128)[:, 0:1]
-        gate_act = dot(x, w[0, 0])
-        up_act = dot(x, w[0, 1])
-        sig = 1.0 / (1.0 + jnp.exp(-gate_act))
-        silu = gate_act * sig
-        inner = (silu * up_act).astype(bf16)
-        inner_s[flat, :] = inner
-        result = dot(inner, w[0, 2], ((1,), (1,)))
-        grad = jnp.sum(u * result, axis=1, keepdims=True)
-        grads[part, here, :] = jnp.broadcast_to(grad, (tile, 128)).reshape(group, CAP, 128)
-        us[part, here, :] = (gate * result).astype(bf16).reshape(group, CAP, width)
-        og = (gate * u).astype(bf16)
-        og_s[flat, :] = og
-        inner_grad = dot(og, w[0, 2])
-        dg = (inner_grad * up_act * (sig * (1.0 + gate_act * (1.0 - sig)))).astype(bf16)
-        du = (inner_grad * silu).astype(bf16)
-        dgu_s[flat, 0:hidden] = dg
-        dgu_s[flat, hidden : 2 * hidden] = du
-
-    col = 256
-
-    @pl.loop(0, width // col)
-    def _(c):
-        at = pl.ds(pl.multiple_of(c * col, col), col)
-        here = pl.ds(pl.multiple_of(e * CAP, CAP), CAP)
-        x = xs[:, here, at].reshape(blocks * CAP, col)
-        both = dot(x, dgu_s[...], ((0,), (0,)))
-        wg[0, 0, at, :] = both[:, :hidden].astype(bf16)
-        wg[0, 1, at, :] = both[:, hidden:].astype(bf16)
-        wg[0, 2, at, :] = dot(og_s[:, at], inner_s[...], ((0,), (0,))).astype(bf16)
-
-    @pl.loop(0, 2)
-    def _(t):
-        part = pl.ds(t * group, group)
-        here = pl.ds(pl.multiple_of(e * CAP, CAP), CAP)
-        flat = pl.ds(pl.multiple_of(t * tile, tile), tile)
-        copy_grad = dot(dgu_s[flat, 0:hidden], w[0, 0], ((1,), (1,)))
-        copy_grad += dot(dgu_s[flat, hidden : 2 * hidden], w[0, 1], ((1,), (1,)))
-        xs[part, here, :] = copy_grad.astype(bf16).reshape(group, CAP, width)
-
-    @pl.when(e == experts - 1)
+                gate = jnp.sum(jnp.where(hits[i], own[i : i + 1], 0.0), axis=1, keepdims=True)
+                weights[b, pl.ds(i * CAP, CAP), :] = jnp.broadcast_to(gate, (CAP, 128))
+
+    @pl.when(step == 1)
     def _():
-        def leave(b, slot):
-            return (
-                pltpu.make_async_copy(
-                    x_buf.at[slot], copy_part.at[b, pl.ds(0, ROW)], sem.at[0, slot]
-                ),
-                pltpu.make_async_copy(u_buf.at[slot], out_part.at[b], sem.at[1, slot]),
-            )
-
-        def extra(b, slot):
-            return pltpu.make_async_copy(
-                og_s.at[pl.ds(slot * 16, 16)], copy_part.at[b, pl.ds(ROW, 16)], sem.at[2, slot]
-            )
+        rows_near(cotangent, cot_all, row_sems)
+
+    @pl.when(step == 3)
+    def _():
+        rows_far(cotangent, cot_all, row_sems)
+
+    @pl.when(step < local)
+    def _():
+        @pl.loop(0, 2)
+        def _(t):
+            part = pl.ds(t * group, group)
+            flat = pl.ds(pl.multiple_of(e * slots + t * tile, tile), tile)
+            x = xs[part, here, :].reshape(tile, width)
+            gate_act = dot(x, w[0, 0])
+            up_act = dot(x, w[0, 1])
+            acts[flat, 0:hidden] = gate_act.astype(bf16)
+            acts[flat, hidden : 2 * hidden] = up_act.astype(bf16)
+            inner = gate_act / (1.0 + jnp.exp(-gate_act)) * up_act
+            result = dot(inner.astype(bf16), w[0, 2], ((1,), (1,)))
+            gate = weights[part, here, :].reshape(tile, 128)[:, 0:1]
+            ys[part, here, :] = (gate * result).astype(bf16).reshape(group, CAP, width)
+
+    @pl.when(step == local)
+    def _():
+        @pl.loop(0, blocks)
+        def _(b):
+            outs[b] = dot(table_of(hits_of(b)), ys[b], ((0,), (0,))).astype(bf16)
+
+        rows_end(cotangent, cot_all, row_sems)
+        sums.begin(0)
+        sums.begin(1)
+        pltpu.make_async_copy(cotangent, cot_all.at[me], local_sem.at[0]).wait()
+        fetch_cot(0, 0).start()
 
         @pl.loop(0, blocks)
         def _(b):
             slot = lax.rem(b, 2)
 
-            @pl.when(b >= 2)
+            @pl.when(b + 1 < blocks)
             def _():
-                for copy in leave(b - 2, slot):
-                    copy.wait()
-                extra(b - 2, slot).wait()
-
-            tables, lines = [], []
+                fetch_cot(b + 1, 1 - slot).start()
+
+            table = table_of(hits_of(b))
+            fetch_cot(b, slot).wait()
+            us[b] = dot(table, u_buf[slot]).astype(bf16)
+            save_us(b).start()
+
+    @pl.when(step >= local)
+    def _():
+        @pl.loop(0, 2)
+        def _(t):
+            part = pl.ds(t * group, group)
+            flat = pl.ds(pl.multiple_of(e * slots + t * tile, tile), tile)
+            gate_act = acts[flat, 0:hidden].astype(f32)
+            up_act = acts[flat, hidden : 2 * hidden].astype(f32)
+            u = us[part, here, :].reshape(tile, width)
+            gate = weights[part, here, :].reshape(tile, 128)[:, 0:1]
+            pulled = dot(u, w[0, 2])
+            sig = 1.0 / (1.0 + jnp.exp(-gate_act))
+            silu = gate_act * sig
+            inner = silu * up_act
+            grad = jnp.sum(inner * pulled, axis=1, keepdims=True)
+            grads[part, here, :] = jnp.broadcast_to(grad, (tile, 128)).reshape(group, CAP, 128)
+            inner_s[flat, :] = (gate * inner).astype(bf16)
+            pulled = gate * pulled
+            dg = (pulled * up_act * (sig * (1.0 + gate_act * (1.0 - sig)))).astype(bf16)
+            du = (pulled * silu).astype(bf16)
+            dgu_s[flat, 0:hidden] = dg
+            dgu_s[flat, hidden : 2 * hidden] = du
+            for copy in save_tile(e * 2 + t):
+                copy.start()
+            copy_grad = dot(dg, w[0, 0], ((1,), (1,))) + dot(du, w[0, 1], ((1,), (1,)))
+            ys[part, here, :] = copy_grad.astype(bf16).reshape(group, CAP, width)
+
+    @pl.when(step == local)
+    def _():
+        sums.go_on(0)
+
+    @pl.when(step == local + 1)
+    def _():
+        sums.go_on(1)
+
+    @pl.when(step == 2 * local - 1)
+    def _():
+        sums.cross()
+
+        @pl.loop(0, blocks)
+        def _(b):
+            hits = hits_of(b)
+            row = sublane((32, ROW)) - me * local
+            line = jnp.zeros((32, ROW), f32)
             for i in range(local):
-                hit = table_of(b, i)
-                tables.append(jnp.where(hit, 1.0, 0.0).astype(bf16))
                 column = grads[b, pl.ds(i * CAP, CAP), :][:, 0:1]
-                lines.append(jnp.sum(jnp.where(hit, column, 0.0), axis=0, keepdims=True))
-            table = jnp.concatenate(tables, axis=0)
-            x_buf[slot] = dot(table, xs[b], ((0,), (0,))).astype(bf16)
-            u_buf[slot] = dot(table, us[b], ((0,), (0,))).astype(bf16)
-            row = sublane((16, ROW))
-            line = jnp.zeros((16, ROW), f32)
-            for i in range(local):
-                line = jnp.where(row == i, lines[i], line)
+                total = jnp.sum(jnp.where(hits[i], column, 0.0), axis=0, keepdims=True)
+                line = jnp.where(row == i, total, line)
             high = line.astype(bf16).astype(f32)
             both = jnp.concatenate(
-                [high, line - high, jnp.zeros((16, width - 2 * ROW), f32)], axis=1
+                [high, line - high, jnp.zeros((32, width - 2 * ROW), f32)], axis=1
             )
-            og_s[pl.ds(pl.multiple_of(slot * 16, 16), 16), :] = both.astype(bf16)
-            for copy in leave(b, slot):
-                copy.start()
-            extra(b, slot).start()
-
-        for b in (blocks - 2, blocks - 1):
-            for copy in leave(b, b % 2):
+            start = pl.multiple_of(b * long, 32)
+            acts[pl.ds(start, ROW), :] = dot(table_of(hits), ys[b], ((0,), (0,))).astype(bf16)
+            acts[pl.ds(pl.multiple_of(start + ROW, 32), 32), :] = both.astype(bf16)
+            save_back(b).start()
+
+        for b in range(blocks):
+            save_xs(b).wait()
+            save_us(b).wait()
+            for copy in save_tile(b):
                 copy.wait()
-            extra(b, b % 2).wait()
-
-
-def experts_part(rank, rows_in, cot_in, routes, small, expert_full):
+            save_back(b).wait()
+        layer_out[...] = hidden_in[...] + sums.finish()
+
+
+def experts_part(rows_in, cotangent, hidden_in, routes, small, expert_full):
     blocks, rows, width = rows_in.shape
     local, _, _, hidden = expert_full.shape
     slots = blocks * CAP
-    any_space = pl.BlockSpec(memory_space=pl.ANY)
-    one_expert = pl.BlockSpec((1, 3, width, hidden), lambda e: (e, 0, 0, 0))
+    dma = pltpu.SemaphoreType.DMA
+    like = jax.ShapeDtypeStruct
     return pl.pallas_call(
         experts_kernel,
-        grid=(local,),
+        grid=(2 * local,),
         out_shape=[
-            jax.ShapeDtypeStruct((blocks, rows, width), bf16),
-            jax.ShapeDtypeStruct((blocks, rows + 16, width), bf16),
-            jax.ShapeDtypeStruct((local, 3, width, hidden), bf16),
-        ],
-        in_specs=[pl.BlockSpec(memory_space=pltpu.SMEM), any_space, any_space] + whole(2) + [one_expert],
-        out_specs=[any_space, any_space, one_expert],
+            like((blocks, rows, width), bf16),
+            like((rows, width), f32),
+            like((blocks, rows + 32, width), bf16),
+            like((blocks, local * CAP, width), bf16),
+            like((blocks, local * CAP, width), bf16),
+            like((local * slots, hidden), bf16),
+            like((local * slots, 2 * hidden), bf16),
+        ],
+        in_specs=anywhere(2)
+        + [pl.BlockSpec((rows, width), lambda s: (0, 0), pipeline_mode=pl.Buffered(1))]
+        + whole(2)
+        + [pl.BlockSpec((1, 3, width, hidden), lambda s: (lax.rem(s, local), 0, 0, 0))],
+        out_specs=anywhere(1)
+        + [pl.BlockSpec((rows, width), lambda s: (0, 0), pipeline_mode=pl.Buffered(1))]
+        + anywhere(5),
         scratch_shapes=[
+            pltpu.VMEM((blocks, local * CAP, width), bf16),
             pltpu.VMEM((blocks, local * CAP, width), bf16),
             pltpu.VMEM((blocks, local * CAP, width), bf16),
             pltpu.VMEM((blocks, local * CAP, 128), f32),
             pltpu.VMEM((blocks, local * CAP, 128), f32),
+            pltpu.VMEM((local * slots, 2 * hidden), bf16),
+            pltpu.VMEM((local * slots, hidden), bf16),
+            pltpu.VMEM((local * slots, 2 * hidden), bf16),
+            pltpu.VMEM((blocks, 8, ROW), jnp.int32),
             pltpu.VMEM((2, rows, width), bf16),
             pltpu.VMEM((2, rows, width), bf16),
-            pltpu.VMEM((slots, width), bf16),
-            pltpu.VMEM((slots, hidden), bf16),
-            pltpu.VMEM((slots, 2 * hidden), bf16),
-            pltpu.VMEM((blocks, 8, ROW), jnp.int32),
-            pltpu.SemaphoreType.DMA((3, 2)),
-        ],
-        compiler_params=pltpu.CompilerParams(vmem_limit_bytes=60 << 20),
-        cost_estimate=pl.CostEstimate(
-            flops=30_000_000_000, bytes_accessed=50 << 20, transcendentals=2_000_000
+            pltpu.VMEM((blocks, rows, width), bf16),
+            *row_sum_scratch(rows, width),
+            dma((9,)),
+            dma((9,)),
+            dma((2, 2)),
+            dma((1,)),
+            dma((5, blocks)),
+        ],
+        compiler_params=pltpu.CompilerParams(
+            collective_id=5, has_side_effects=True, vmem_limit_bytes=62 << 20
         ),
+        cost_estimate=cost_of(65),
         name="experts",
-    )(rank, rows_in, cot_in, routes, small, expert_full)
-
-
-def exchange(x):
-    return lax.all_to_all(x, "tensor", 0, 0, tiled=False)
+    )(rows_in, cotangent, hidden_in, routes, small, expert_full)[1:]
+
+
+def weight_grads_kernel(
+    x, u, inner, dgu, copy_part,
+    back, out,
+    made, got, rows_s, far, near, leaving, landed, row_send, row_recv,
+    core_send, core_recv, local, out_sem,
+):
+    e, c = pl.program_id(0), pl.program_id(1)
+    experts, parts = pl.num_programs(0), pl.num_programs(1)
+    step = e * parts + c
+    _, here, _, partner, right, left = neighbours()
+    _, _, core, _, _, other = group_place()
+    hidden, rows = inner.shape[1], inner.shape[0]
+    share = made.shape[1] // 2
+    sums = RowSums(rows_s, far, near, leaving, landed, (row_send, row_recv))
+
+    def core_push(e, c):
+        part = pl.ds(c * share, share)
+        return pltpu.make_async_remote_copy(
+            src_ref=made.at[e, part, 1 - core],
+            dst_ref=got.at[e, part],
+            send_sem=core_send.at[e, c],
+            recv_sem=core_recv.at[e, c],
+            device_id=other,
+            device_id_type=MESH,
+        )
+
+    def save(e):
+        return pltpu.make_async_copy(made.at[e, :, core], out.at[:, e], out_sem.at[e])
+
+    def add_core(e):
+        for half in range(2):
+            core_push(e, half).wait_recv()
+
+        @pl.loop(0, 2 * share)
+        def _(k):
+            total = made[e, k, core].astype(f32) + got[e, k].astype(f32)
+            made[e, k, core] = total.astype(bf16)
+
+        save(e).start()
+
+    @pl.when(step == 0)
+    def _():
+        load = pltpu.make_async_copy(copy_part, rows_s, local)
+        load.start()
+        meet([partner, here + right, here + left], [other["dp"]])
+        load.wait()
+        sums.begin(0)
+        sums.begin(1)
+
+    both = dot(x[...].reshape(rows, -1), dgu[...], ((0,), (0,)))
+    part = pl.ds(c * share, share)
+    shape = (share, 2, -1, hidden)
+    made[e, part, :, 0] = both[:, :hidden].astype(bf16).reshape(shape)
+    made[e, part, :, 1] = both[:, hidden:].astype(bf16).reshape(shape)
+    down = dot(u[...].reshape(rows, -1), inner[...], ((0,), (0,)))
+    made[e, part, :, 2] = down.astype(bf16).reshape(shape)
+    core_push(e, c).start()
+
+    @pl.when(step == 3)
+    def _():
+        sums.go_on(0)
+
+    @pl.when(step == 5)
+    def _():
+        sums.go_on(1)
+
+    @pl.when((e > 0) & (c == parts - 1))
+    def _():
+        add_core(e - 1)
+
+    @pl.when(step == experts * parts - 1)
+    def _():
+        add_core(e)
+        sums.cross()
+        back[...] = sums.finish()
+        for k in range(made.shape[0]):
+            for half in range(2):
+                core_push(k, half).wait_send()
+            save(k).wait()
+
+
+def weight_grads(xs, us, inner, dgu, copy_part):
+    blocks, held, width = xs.shape
+    local, hidden, slots = held // CAP, inner.shape[1], blocks * CAP
+    col = width // 2
+    long = copy_part.shape[1]
+    shard = width // GROUPS
+    rows = pl.BlockSpec((blocks, CAP, col), lambda e, c: (0, e, c))
+    dma = pltpu.SemaphoreType.DMA
+    return pl.pallas_call(
+        weight_grads_kernel,
+        grid=(local, width // col),
+        out_shape=[
+            jax.ShapeDtypeStruct((long, width), f32),
+            jax.ShapeDtypeStruct((GROUPS // 2, local, 3, shard, hidden), bf16),
+        ],
+        in_specs=[
+            rows,
+            rows,
+            pl.BlockSpec((slots, hidden), lambda e, c: (e, 0)),
+            pl.BlockSpec((slots, 2 * hidden), lambda e, c: (e, 0)),
+        ]
+        + anywhere(1),
+        out_specs=[pl.BlockSpec((long, width), lambda e, c: (0, 0))] + anywhere(1),
+        scratch_shapes=[
+            pltpu.VMEM((local, GROUPS // 2, 2, 3, shard, hidden), bf16),
+            pltpu.VMEM((local, GROUPS // 2, 3, shard, hidden), bf16),
+            pltpu.VMEM((blocks, long, width), bf16),
+            *row_sum_scratch(long, width),
+            dma((local, 2)),
+            dma((local, 2)),
+            dma,
+            dma((local,)),
+        ],
+        compiler_params=pltpu.CompilerParams(
+            collective_id=6, has_side_effects=True, vmem_limit_bytes=62 << 20
+        ),
+        cost_estimate=cost_of(45),
+        name="weight_grads",
+    )(xs, us, inner, dgu, copy_part)
 
 
 def per_device(
@@ -1047,68 +1384,53 @@
 ):
     rows, width = tokens.shape
     group_rows = rows * RANKS
-    experts = router.shape[1]
-    rank = lax.axis_index("tensor")
-
-    wkv = jnp.concatenate([w_key, w_value], axis=1)
-    small_own = jnp.concatenate([attn_gain[:, None], ffn_gain[:, None], router], axis=1)
-    small_own = jnp.pad(small_own, ((0, 0), (0, 128 - small_own.shape[1])))
-    heads_own = jnp.concatenate([query_gain, key_gain], axis=0)
-    heads_own = jnp.pad(heads_own, ((0, 5), (0, 124)))
-    routes_own = routes.T.reshape(8, 2, 128).transpose(1, 0, 2).reshape(16, 128).astype(bf16)
-    payload = jnp.concatenate(
-        [w_query, wkv, small_own, heads_own, w_output.T, routes_own], axis=0
-    )
+
     own_experts = jnp.stack([w_gate, w_up, w_down.transpose(0, 2, 1)], axis=1)
     expert_full = lax.all_gather(own_experts, "dp", axis=2, tiled=True)
-    tokens_all, tiny_all, first_all, rest_all = opening(tokens, payload)
+    tokens_all, qkv_cols, tiny_all, first_all, rest_all, small, routes_own = opening(
+        tokens, w_query, w_key, w_value, w_output, attn_gain[None], ffn_gain[None], router,
+        query_gain, key_gain, routes.T,
+    )
     first_all = first_all.reshape((GROUPS,) + first_all.shape[3:])
     rest_all = rest_all.reshape((GROUPS,) + rest_all.shape[3:])
-    small = rest_all[:, :, 0:8, : 2 + experts].reshape(width, 2 + experts).T.astype(f32)
-    small = jnp.concatenate([small[:2], jnp.zeros((6, width), f32), small[2:]], axis=0)
-    cot_copies, tokens_all = lax.optimization_barrier((cotangent, tokens_all))
-    cot_all = exchange(jnp.broadcast_to(cot_copies, (RANKS,) + cotangent.shape))
-
-    feature = jnp.arange(128, dtype=jnp.int32) % 32
-    frequency = ROTARY_BASE ** (-feature.astype(f32) / 32.0)
-    within = jnp.arange(ROW, dtype=f32)[:, None] * frequency
-    table = jnp.stack([jnp.cos(within), jnp.sin(within)])
-    starts = (jnp.arange(8, dtype=f32) * ROW)[:, None] * frequency
-    block = jnp.stack([jnp.cos(starts), jnp.sin(starts)])
+
+    frequency = ROTARY_BASE ** (-(np.arange(128) % 32) / 32.0)
+    within = np.arange(ROW)[:, None] * frequency
+    starts = (np.arange(group_rows // ROW) * ROW)[:, None] * frequency
+    table = np.stack([np.cos(within), np.sin(within)]).astype(np.float32)
+    block = np.stack([np.cos(starts), np.sin(starts)]).astype(np.float32)
     order_row, order_col = token_order, token_order.T
     normed_all, proj, stream_qkv, mixed_stream, log_total, mixed, wqkv = attend(
         lengths[0], tokens_all.reshape(group_rows, width), small, first_all, table, block,
         order_row, order_col,
     )
-    mixed_own, hidden, normed2_all = middle(
+    mixed_own, hidden, normed2_all, done = middle(
         mixed.reshape(RANKS, rows, 128), rest_all, tokens, small
     )
 
-    wqkv_cols, normed2_all = lax.optimization_barrier((tiny_all[:, :128], normed2_all))
-    wqkv_all = lax.all_gather(wqkv_cols, "dp", axis=0, tiled=False)
-    routes_all = tiny_all[:, 208:]
-    out_part, copy_part, expert_grads = experts_part(
-        rank[None], normed2_all, cot_all, routes_all, small, expert_full
-    )
-    expert_sums = lax.psum_scatter(expert_grads, "dp", scatter_dimension=2, tiled=True).astype(f32)
-    back = exchange(copy_part)
+    qkv_cols, _ = lax.optimization_barrier((qkv_cols, done))
+    wqkv_all = lax.all_gather(qkv_cols, "dp", axis=0, tiled=False)
+    layer_out, copy_part, xs, us, inner, dgu = experts_part(
+        normed2_all, cotangent, hidden, tiny_all, small, expert_full
+    )
+    back, expert_grads = weight_grads(xs, us, inner, dgu, copy_part)
+    groups = [[core + 2 * k for k in range(GROUPS // 2)] for core in range(2)]
+    expert_sums = lax.psum_scatter(
+        expert_grads, "dp", scatter_dimension=0, axis_index_groups=groups, tiled=False
+    ).astype(f32)
     hidden_grad, mixed_grad, wo_grad, turn_grad = turn(
         back, hidden, cotangent, routes_own, small, mixed_own, rest_all
     )
-    out_part, mixed_grad = lax.optimization_barrier((out_part, mixed_grad))
-    out_pieces = exchange(out_part)
 
     proj_grad, wqkv_grad, small_grad = attend_back(
         lengths[0], mixed_grad.reshape(group_rows, 128), stream_qkv, mixed_stream, log_total,
         proj, first_all, table, block, order_row, order_col, normed_all, wqkv, small, turn_grad,
     )
-    wide = jnp.concatenate([wo_grad, wqkv_grad], axis=1)
     grad_tokens, wqkv_sum, wo_sum, small_sum, head_sum = closing(
-        proj_grad.reshape(RANKS, rows, 256), wide.reshape((4, 2, 2) + wide.shape[1:]),
-        small_grad.reshape(4, 2, 2, -1, 128), wqkv_all, tokens, small, hidden_grad,
-    )
-    out_pieces, grad_tokens = lax.optimization_barrier((out_pieces, grad_tokens))
-    layer_out = hidden + jnp.sum(out_pieces.astype(f32), axis=0)
+        proj_grad.reshape(RANKS, rows, 256), wo_grad.reshape((4, 2, 2) + wo_grad.shape[1:]),
+        wqkv_grad.reshape((4, 2, 2) + wqkv_grad.shape[1:]), small_grad.reshape(4, 2, 2, -1, 128),
+        wqkv_all, tokens, small, hidden_grad,
+    )
     return (
         layer_out,
         grad_tokens,

time: 510 us -> 423 us (0.83); the launches traced: 510 us -> 416 us
  blocking collectives: 68.4 us -> 0 us
  waiting for transfers between devices: 60.2 us -> 0.05 us
  Pallas kernels: 312 us -> 364 us
  other arithmetic: 16.2 us -> 3.42 us
  starting transfers between devices: 9.67 us -> 0.12 us
    all_to_all x1 -> x0, blocking collectives: 68.4 us -> none  [exchange(): return lax.all_to_all(x, 'tensor', 0, 0, tiled=False)]
    all_to_all x2 -> x0, waiting for transfers between devices: 60.2 us -> none  [exchange(): return lax.all_to_all(x, 'tensor', 0, 0, tiled=False)]
    pallas_call x2 -> x3, Pallas kernels: 125 us -> 179 us  [the longest x1 78.8 us: experts_part(): pl.pallas_call(experts_kernel, grid=(2 * local,), out_shape=[like((blocks...]
    pallas_call x1, Pallas kernels: 58.5 us -> 46.5 us  [closing(): pl.pallas_call(closing_kernel, out_shape=[jax.ShapeDtypeStruct(hidden_gra...]
    all_to_all x2 -> x0, starting transfers between devices: 9.55 us -> none  [exchange(): return lax.all_to_all(x, 'tensor', 0, 0, tiled=False)]
    unnamed x49 -> x67, local copies, waits for them, and re-layouts: 14.1 us -> 23.4 us
  transfers between devices with their start and end apart: 5 -> 3, of which waited for: 1 -> 0; matrix products, arithmetic and copies ran while one was open for 6% -> 3% of each run, Pallas kernels for 61% -> 88%
where the time goes in v3:
time: 423 us; the launch traced here: 416 us
  Pallas kernels  364 us (86%)
  local copies, waits for them, and re-layouts  34.2 us (8%)
  between operations  14 us (3%)
    pallas_call x1, Pallas kernels, experts_part(): pl.pallas_call(experts_kernel, grid=(2 * local,), out_shape=[like((blocks...  78.8 us
    pallas_call x1, Pallas kernels, opening(): pl.pallas_call(opening_kernel, out_shape=[like((RANKS,) + tokens.shape, b...  56.5 us
    pallas_call x1, Pallas kernels, middle(): pl.pallas_call(middle_kernel, out_shape=[jax.ShapeDtypeStruct(mixed.shape...  51.9 us
    pallas_call x1, Pallas kernels, closing(): pl.pallas_call(closing_kernel, out_shape=[jax.ShapeDtypeStruct(hidden_gra...  46.5 us
    pallas_call x1, Pallas kernels, weight_grads(): pl.pallas_call(weight_grads_kernel, grid=(local, width // col), out_shape...  44 us
    pallas_call x1, Pallas kernels, attend_back(): pl.pallas_call(attend_back_kernel, out_shape=[jax.ShapeDtypeStruct((rows,...  40.6 us
    pallas_call x1, Pallas kernels, attend(): pl.pallas_call(attend_kernel, out_shape=[jax.ShapeDtypeStruct((rows, widt...  29.9 us
    unnamed x67, local copies, waits for them, and re-layouts  23.4 us
  transfers between devices with their start and end apart: 3, of which 0 were waited for; matrix products, arithmetic and copies ran while one was open for 3% of the time, Pallas kernels for 88%

profile of v3, /device:TPU:0, one launch (start us, length us, event | category | flops | bytes accessed | tf_op | source)
XLA Modules:
  0.0 415.7 jit_solution(8067358637961850965)
XLA Ops:
  7.2 2.1 pad_maximum_fusion
  10.2 1.0 copy-done.1
  17.4 56.5 %opening.1 = (bf16[8,256,1024]{2,1,0:T(8,128)(2,1)S(1)}, bf16[8,128,128]{2,1,0:T(8,128)(2,1)}, bf16[8,96,128]{2,1,0:T(8,128)(2,1)S(1)}, bf16[4,2,2,144,128]{4,3,...) custom-call(bf16[256,1024]{1,0:T(8,128)(2,1)S(1)} %copy-done.1, ...), custom_call_target="tpu_custom_call" | custom-call | flops 54999998464 | bytes 1048576 | tf_op jit(solution)/shard_map/opening/pallas_call | solution.py:336
  73.9 1.9 copy-done.12
  78.1 1.7 copy.40.order_col
  79.7 29.9 %attend.1 = (bf16[2048,1024]{1,0:T(8,128)(2,1)}, f32[2048,256]{1,0:T(8,128)}, bf16[2048,256]{1,0:T(8,128)(2,1)}, bf16[2048,128]{1,0:T(8,128)(2,1)}, f32[2048,128...) custom-call(s32[3]{0:T(128)} %bitcast.52, bf16[2048,1024]{1,0:T(8,128)(2,1)} %bitcast.38, ...), custom_call_target="tpu_custom_call" | custom-call | flops 32999999488 | bytes 1048576 | tf_op jit(solution)/shard_map/attend/pallas_call | solution.py:786
  109.6 1.0 copy-done.16
  110.7 51.9 %middle.1 = (bf16[8,256,128]{2,1,0:T(8,128)(2,1)S(1)}, f32[256,1024]{1,0:T(8,128)S(1)}, bf16[8,256,1024]{2,1,0:T(8,128)(2,1)S(1)}, f32[8,128]{1,0:T(8,128)}) custom-call(bf16[8,256,128]{2,1,0:T(8,128)(2,1)S(1)} %bitcast.44, bf16[16,8,80,128]{3,2,1,0:T(8,128)(2,1)S(1)} %bitcast.39, bf16[256,1024]{1,0:T(8,128)(2,1)S(1)} %copy-done.2, f32[40,1024]{1,0:T(8,128)S(1)} %copy-done.23), custom_call_target="tpu_custom_call" | custom-call | flops 44000002048 | bytes 1048576 | tf_op jit(solution)/shard_map/middle/pallas_call | solution.py:406
  162.6 1.0 copy-done.18
  163.6 1.9 copy-done.21
  165.6 78.8 %experts.1 = (bf16[8,256,1024]{2,1,0:T(8,128)(2,1)}, f32[256,1024]{1,0:T(8,128)}, bf16[8,288,1024]{2,1,0:T(8,128)(2,1)}, bf16[8,320,1024]{2,1,0:T(8,128)(2,1)}, ...) custom-call(bf16[8,256,1024]{2,1,0:T(8,128)(2,1)} %copy-done.21, ...), custom_call_target="tpu_custom_call" | custom-call | flops 71499997184 | bytes 1048576 | tf_op jit(solution)/shard_map/experts/pallas_call | solution.py:1197
  244.3 44.0 %weight_grads.1 = (f32[288,1024]{1,0:T(8,128)}, bf16[8,4,3,64,512]{4,3,2,1,0:T(8,128)(2,1)}) custom-call(bf16[8,320,1024]{2,1,0:T(8,128)(2,1)} %get-tuple-element.60.x, bf16[8,320,1024]{2,1,0:T(8,128)(2,1)} %get-tuple-element.61.u, bf16[2560,512]{1,0:T(8,128)(2,1)} %get-tuple-element.62.inner, bf16[2560,1024]{1,0:T(8,128)(2,1)} %get-tuple-element.63.dgu, ...), custom_call_target="tpu_custom_call" | custom-call | flops 49500000256 | bytes 1048576 | tf_op jit(solution)/shard_map/weight_grads/pallas_call | solution.py:1333
  288.4 1.0 copy-done
  290.1 15.7 %turn.1 = (f32[256,1024]{1,0:T(8,128)S(1)}, bf16[8,256,128]{2,1,0:T(8,128)(2,1)S(1)}, bf16[16,8,64,128]{3,2,1,0:T(8,128)(2,1)}, f32[40,1024]{1,0:T(8,128)S(1)}) custom-call(f32[288,1024]{1,0:T(8,128)S(1)} %copy-done.17, f32[256,1024]{1,0:T(8,128)S(1)} %copy-done.19, bf16[256,1024]{1,0:T(8,128)(2,1)S(1)} %copy-done, ...), custom_call_target="tpu_custom_call" | custom-call | flops 16499999744 | bytes 1048576 | tf_op jit(solution)/shard_map/turn/pallas_call | solution.py:505
  308.2 40.6 %attend_back.1 = (bf16[2048,256]{1,0:T(8,128)(2,1)}, bf16[16,2,64,128]{3,2,1,0:T(8,128)(2,1)}, f32[1024,128]{1,0:T(8,128)}) custom-call(s32[3]{0:T(128)} %bitcast.53, bf16[2048,128]{1,0:T(8,128)(2,1)} %bitcast.43, bf16[2048,256]{1,0:T(8,128)(2,1)} %get-tuple-element.69.stream_qkv, bf16[2048,128]{1,0:T(8,128)(2,1)} %get-tuple-element.70.mixed_stream, ...), custom_call_target="tpu_custom_call" | custom-call | flops 44000002048 | bytes 1048576 | tf_op jit(solution)/shard_map/attend_back/pallas_call | solution.py:955
  348.9 46.5 %closing.1 = (f32[256,1024]{1,0:T(8,128)}, f32[64,256]{1,0:T(8,128)}, f32[64,128]{1,0:T(8,128)}, f32[8,128]{1,0:T(8,128)}, f32[8,128]{1,0:T(8,128)}) custom-call(bf16[8,256,256]{2,1,0:T(8,128)(2,1)} %bitcast.55, bf16[4,2,2,8,64,128]{5,4,3,2,1,0:T(8,128)(2,1)} %bitcast.54, bf16[4,2,2,2,64,128]{5,4,3,2,1,0:T(8,128)(2,1)} %bitcast.56, ...), custom_call_target="tpu_custom_call" | custom-call | flops 49500000256 | bytes 1048576 | tf_op jit(solution)/shard_map/closing/pallas_call | solution.py:633
  395.4 1.5 slice.36
  396.9 1.3 slice.35
  399.7 1.4 slice_reduce_fusion.2
  401.0 1.5 slice_reduce_fusion
  402.5 1.5 fusion
  404.0 1.3 bitcast_convert_fusion
  405.4 1.2 slice_bitcast_fusion
  406.6 1.0 copy.46
  (70 shorter events, 15.4 us)
Async XLA Ops:
  7.2 158.4 %all-gather.4.cloned.1.call-start = ((), (), s32[]{:S(2)}) async-start(), calls=%async_computation.1 | async-start | bytes 13369344 | tf_op jit(solution)/shard_map/all_gather | solution.py:1389
  9.3 339.5 %all-gather.6.cloned.1.call-start = ((), (), s32[]{:S(2)}) async-start(), calls=%async_computation.3 | async-start | bytes 4456448 | tf_op jit(solution)/shard_map/all_gather | solution.py:1412
  10.2 1.1 copy-start.1
  11.3 0.7 copy-start.3
  12.0 0.7 copy-start.4
  17.4 60.6 %copy-start.30 = (s32[1,2048]{1,0:T(1,128)S(1)}, s32[1,2048]{1,0:T(1,128)}, u32[]{:S(2)}) copy-start(s32[1,2048]{1,0:T(1,128)} %order_row.3) | copy-start | bytes 24580
  73.9 1.9 copy-start.12
  75.8 0.8 copy-start.14
  78.0 31.6 %copy-start.13 = (bf16[4,2,2,8,80,128]{5,4,3,2,1,0:T(8,128)(2,1)}, bf16[4,2,2,8,80,128]{5,4,3,2,1,0:T(8,128)(2,1)S(1)}, u32[]{:S(2)}) copy-start(bf16[4,2,2,8,80,128]{5,4,3,2,1,0:T(8,128)(2,1)S(1)} %get-tuple-element.55) | copy-start | bytes 7864324
  78.0 326.0 %reduce-scatter.2.cloned.1.call-start = ((), (), s32[]{:S(2)}) async-start(), calls=%async_computation.2 | async-start | bytes 7077888 | tf_op jit(solution)/shard_map/reduce_scatter | solution.py:1418
  79.7 29.9 %copy-start.2 = (bf16[256,1024]{1,0:T(8,128)(2,1)S(1)}, bf16[256,1024]{1,0:T(8,128)(2,1)}, u32[]{:S(2)}) copy-start(bf16[256,1024]{1,0:T(8,128)(2,1)} %tokens.5) | copy-start | bytes 1572868
  79.7 29.9 %copy-start.23 = (f32[40,1024]{1,0:T(8,128)S(1)}, f32[40,1024]{1,0:T(8,128)}, u32[]{:S(2)}) copy-start(f32[40,1024]{1,0:T(8,128)} %copy-done.22) | copy-start | bytes 491524
  109.6 1.0 copy-start.16
  162.6 1.0 copy-start.18
  163.6 1.9 copy-start.21
  288.4 1.0 copy-start
  288.4 1.4 copy-start.17
  288.4 1.7 copy-start.19
  288.4 1.7 copy-start.24
  305.8 0.8 copy-start.15
  306.6 1.0 copy-start.20
  395.4 11.2 %copy-start.27 = (f32[256,1024]{1,0:T(8,128)S(1)}, f32[256,1024]{1,0:T(8,128)}, u32[]{:S(2)}) copy-start(f32[256,1024]{1,0:T(8,128)} %get-tuple-element.151) | copy-start | bytes 3145732
  395.4 12.2 %copy-start.28 = (f32[256,1024]{1,0:T(8,128)S(1)}, f32[256,1024]{1,0:T(8,128)}, u32[]{:S(2)}) copy-start(f32[256,1024]{1,0:T(8,128)} %get-tuple-element.152) | copy-start | bytes 3145732
  405.4 3.1 copy-start.29
  (10 other events, 6.7 us)
Sparse Core Ops, SparseCore 0:
  10.5 109.2 all-gather.3
  122.2 54.4 all-gather.5
  288.5 113.4 reduce-scatter.1

commit v4 on v3

--- a/solution.py
+++ b/solution.py
@@ -276,7 +276,7 @@
     payload[64:128, 0:64] = w_key[...]
     payload[64:128, 64:128] = w_value[...]
     payload[128:144] = jnp.concatenate([block, lines[2]], axis=0).astype(bf16)
-    payload[144:208] = jnp.transpose(w_output[...].astype(f32)).astype(bf16)
+    payload[144:208] = w_output[...]
     picks = routes[...].astype(f32)
     picks = jnp.concatenate([picks[:, 0:128], picks[:, 128:256]], axis=0).astype(bf16)
     payload[208:224] = picks
@@ -357,7 +357,7 @@
         + [dma((5,))] * 4
         + [dma((6,))],
         compiler_params=pltpu.CompilerParams(
-            collective_id=1, has_side_effects=True, vmem_limit_bytes=40 << 20
+            collective_id=1, has_side_effects=True, vmem_limit_bytes=63 << 20
         ),
         cost_estimate=cost_of(50),
         name="opening",
@@ -423,7 +423,7 @@
             dma((2,)),
         ],
         compiler_params=pltpu.CompilerParams(
-            collective_id=2, has_side_effects=True, vmem_limit_bytes=40 << 20
+            collective_id=2, has_side_effects=True, vmem_limit_bytes=63 << 20
         ),
         cost_estimate=cost_of(40),
         name="middle",
@@ -520,7 +520,7 @@
             dma((1,)),
         ],
         compiler_params=pltpu.CompilerParams(
-            collective_id=3, has_side_effects=True, vmem_limit_bytes=48 << 20
+            collective_id=3, has_side_effects=True, vmem_limit_bytes=63 << 20
         ),
         cost_estimate=cost_of(15),
         name="turn",
@@ -528,19 +528,28 @@
 
 
 def closing_kernel(
-    proj_grad, wo_grad, wqkv_grad, small_grad, wqkv_all, tokens, small, hidden_grad,
-    grad_tokens, wqkv_sum, wo_sum, small_sum, head_sum,
+    proj_grad, wo_grad, wqkv_grad, small_grad, wqkv_all, tokens, small, hidden_grad, expert_pair,
+    grad_tokens, wqkv_sum, wo_sum, small_sum, head_sum, expert_far,
     proj_in,
     wo_core, wo_y, wo_x, wo_half, wo_pair,
     wqkv_core, wqkv_y, wqkv_x, wqkv_half, wqkv_pair,
     small_core, small_y, small_x, small_half, small_pair,
     wo_out, small_out, wo_last, small_last,
-    proj_send, proj_recv, group_send, group_recv, last_send, last_recv, local,
+    proj_send, proj_recv, group_send, group_recv, last_send, last_recv, far_sems, local,
 ):
     me = lax.axis_index("tensor")
     y, side, core, across, column, other = group_place()
     ranks = others("tensor", RANKS)
     meet(ranks, [across["dp"], other["dp"]] + [peer["dp"] for _, peer in column])
+    crossing = pltpu.make_async_remote_copy(
+        src_ref=expert_pair.at[1 - side],
+        dst_ref=expert_far,
+        send_sem=far_sems.at[0],
+        recv_sem=far_sems.at[1],
+        device_id=across,
+        device_id_type=MESH,
+    )
+    crossing.start()
     away = 1 - core
     arrays = (
         (wo_grad, wo_core, wo_half, wo_y, wo_pair, wo_x),
@@ -619,9 +628,12 @@
     for copies in second:
         for copy in copies:
             copy.wait_send()
-
-
-def closing(proj_grad, wo_grad, wqkv_grad, small_grad, wqkv_all, tokens, small, hidden_grad):
+    crossing.wait()
+
+
+def closing(
+    proj_grad, wo_grad, wqkv_grad, small_grad, wqkv_all, tokens, small, hidden_grad, expert_pair
+):
     dma = pltpu.SemaphoreType.DMA
     shard = wo_grad.shape[4]
     rows = shard // RANKS
@@ -638,9 +650,10 @@
             jax.ShapeDtypeStruct((shard, 128), f32),
             jax.ShapeDtypeStruct((rows, 128), f32),
             jax.ShapeDtypeStruct((8, 128), f32),
+            jax.ShapeDtypeStruct(expert_pair.shape[1:], bf16),
         ],
-        in_specs=whole(8),
-        out_specs=whole(5),
+        in_specs=whole(8) + anywhere(1),
+        out_specs=whole(5) + anywhere(1),
         scratch_shapes=[
             pltpu.VMEM(proj_grad.shape, bf16),
             *steps,
@@ -654,14 +667,17 @@
             dma((3, 5)),
             dma((2, 7)),
             dma((2, 7)),
+            dma((2,)),
             dma((3,)),
         ],
         compiler_params=pltpu.CompilerParams(
-            collective_id=4, has_side_effects=True, vmem_limit_bytes=62 << 20
+            collective_id=4, has_side_effects=True, vmem_limit_bytes=63 << 20
         ),
         cost_estimate=cost_of(45),
         name="closing",
-    )(proj_grad, wo_grad, wqkv_grad, small_grad, wqkv_all, tokens, small, hidden_grad)
+    )(
+        proj_grad, wo_grad, wqkv_grad, small_grad, wqkv_all, tokens, small, hidden_grad, expert_pair
+    )
 
 
 def sequence_start(place, lengths):
@@ -699,26 +715,54 @@
     return cos, jnp.where(lane(sin.shape) % 64 < 32, -sin, sin)
 
 
+def columns_of(row):
+    return jnp.transpose(jnp.broadcast_to(row, (128, row.shape[1])))
+
+
 def attend_kernel(
-    lengths, x, small, first_all, table, block, order_row, order_col,
-    normed, proj, stream_qkv, mixed_stream, log_total, mixed, wqkv,
-    token_qkv, keys, values,
+    lengths, x, small, first_all, table, block, order, cotangent,
+    normed, proj, stream_qkv, mixed_stream, log_total, mixed, wqkv, cot_all,
+    x_s, normed_s, proj_s, token_qkv, keys, values,
+    row_send, row_recv, load_sem, save_sem, local,
 ):
     rows = x.shape[0]
     blocks = rows // ROW
+    row_sems = row_send, row_recv
+
+    def load(b):
+        at = pl.ds(pl.multiple_of(b * ROW, ROW), ROW)
+        return pltpu.make_async_copy(x.at[at], x_s.at[at], load_sem.at[b])
+
+    def save(b):
+        at = pl.ds(pl.multiple_of(b * ROW, ROW), ROW)
+        return (
+            pltpu.make_async_copy(normed_s.at[at], normed.at[at], save_sem.at[0, b]),
+            pltpu.make_async_copy(proj_s.at[at], proj.at[at], save_sem.at[1, b]),
+        )
+
+    for b in range(blocks):
+        load(b).start()
+    me, here, _, partner, right, left = neighbours()
+    own = pltpu.make_async_copy(cotangent, cot_all.at[me], local)
+    own.start()
     q_gain, k_gain = head_gains(first_all)
     wqkv[:, 0:128] = first_all[:, 0:64, :].reshape(-1, 128)
     wqkv[:, 128:256] = first_all[:, 64:128, :].reshape(-1, 128)
+    meet([partner, here + right, here + left], [])
+    rows_begin(cotangent, cot_all, row_sems)
 
     @pl.loop(0, blocks)
     def _(b):
         at = pl.ds(pl.multiple_of(b * ROW, ROW), ROW)
-        v = x[at, :].astype(f32)
+        load(b).wait()
+        v = x_s[at, :].astype(f32)
         r = lax.rsqrt(jnp.mean(v * v, axis=1, keepdims=True) + EPS)
         n = (v * r * small[0:1, :]).astype(bf16)
-        normed[at, :] = n
+        normed_s[at, :] = n
         p = dot(n, wqkv[...])
-        proj[at, :] = p
+        proj_s[at, :] = p
+        for copy in save(b):
+            copy.start()
         q, kv = p[:, :128], p[:, 128:]
         low = lane(kv.shape) < 64
         q = q * lax.rsqrt(head_mean(q * q, 2) + EPS) * q_gain
@@ -730,7 +774,7 @@
     def _(b):
         at = pl.ds(pl.multiple_of(b * ROW, ROW), ROW)
         place = sublane((ROW, rows)) + b * ROW
-        moves = jnp.where(order_row[...] == place, 1.0, 0.0).astype(bf16)
+        moves = jnp.where(order[...] == place, 1.0, 0.0).astype(bf16)
         moved = dot(moves, token_qkv[...])
         cos, sin = turned(table, block, b)
         q, kv = moved[:, :128], moved[:, 128:]
@@ -752,21 +796,27 @@
         q0, q1 = jnp.where(low, q, zero), jnp.where(low, zero, q)
         place = sublane((ROW, 1)) + b * ROW
         start = sequence_start(place, lengths)
-        first = sequence_start(b * ROW, lengths) // CHUNK
-        last = (b * ROW + ROW - 1) // CHUNK + 1
-
-        def step(j, totals):
+
+        def step(begin, size, totals, diagonal):
             t0, t1 = totals
-            here = pl.ds(pl.multiple_of(j * CHUNK, CHUNK), CHUNK)
+            here = pl.ds(pl.multiple_of(begin, ROW), size)
             k, v = keys[here, :], values[here, :]
-            key = lane((ROW, CHUNK)) + j * CHUNK
-            allowed = (key <= place) & (key >= start)
+            key = lane((ROW, size)) + begin
+            allowed = key >= start
+            if diagonal:
+                allowed = allowed & (key <= place)
             e0 = jnp.where(allowed, jnp.exp(dot(q0, k, ((1,), (1,)))), 0.0).astype(bf16)
             e1 = jnp.where(allowed, jnp.exp(dot(q1, k, ((1,), (1,)))), 0.0).astype(bf16)
             return t0 + dot(e0, v), t1 + dot(e1, v)
 
         none = jnp.zeros((ROW, 128), f32)
-        t0, t1 = lax.fori_loop(first, last, step, (none, none))
+        totals = step(b * ROW, ROW, (none, none), True)
+        totals = lax.fori_loop(
+            0, b // 2, lambda j, t: step(j * CHUNK, CHUNK, t, False), totals
+        )
+        t0, t1 = lax.fori_loop(
+            0, lax.rem(b, 2), lambda j, t: step((b - 1) * ROW, ROW, t, False), totals
+        )
         low = lane((ROW, 128)) < 64
         other0, other1 = pltpu.roll(t0, 64, 1), pltpu.roll(t1, 64, 1)
         total = jnp.where(low, other0, t1)
@@ -774,15 +824,35 @@
         log_total[at, :] = jnp.log(total)
         mixed_stream[at, :] = out.astype(bf16)
 
+        @pl.when(b == 0)
+        def _():
+            rows_on(cotangent, cot_all, row_sems, (1, 2), ((5,), (6,)))
+
+        @pl.when(b == 2)
+        def _():
+            rows_on(cotangent, cot_all, row_sems, (0,), ((3, 4),))
+
+        @pl.when(b == 6)
+        def _():
+            rows_far(cotangent, cot_all, row_sems)
+
     @pl.loop(0, blocks)
     def _(b):
         at = pl.ds(pl.multiple_of(b * ROW, ROW), ROW)
-        moves = jnp.where(order_col[at, :] == lane((ROW, rows)), 1.0, 0.0).astype(bf16)
+        column = columns_of(order[:, at].astype(f32))[:, 0:1]
+        moves = jnp.where(column == lane((ROW, rows)).astype(f32), 1.0, 0.0).astype(bf16)
         mixed[at, :] = dot(moves, mixed_stream[...]).astype(bf16)
 
-
-def attend(lengths, x, small, first_all, table, block, order_row, order_col):
+    for b in range(blocks):
+        for copy in save(b):
+            copy.wait()
+    rows_end(cotangent, cot_all, row_sems)
+    own.wait()
+
+
+def attend(lengths, x, small, first_all, table, block, order, cotangent):
     rows, width = x.shape
+    dma = pltpu.SemaphoreType.DMA
     return pl.pallas_call(
         attend_kernel,
         out_shape=[
@@ -793,28 +863,79 @@
             jax.ShapeDtypeStruct((rows, 128), f32),
             jax.ShapeDtypeStruct((rows, 128), bf16),
             jax.ShapeDtypeStruct((width, 256), bf16),
+            jax.ShapeDtypeStruct((RANKS,) + cotangent.shape, bf16),
         ],
-        in_specs=[pl.BlockSpec(memory_space=pltpu.SMEM)] + whole(7),
-        out_specs=whole(7),
+        in_specs=[pl.BlockSpec(memory_space=pltpu.SMEM)] + anywhere(1) + whole(5) + anywhere(1),
+        out_specs=anywhere(2) + whole(5) + anywhere(1),
         scratch_shapes=[
+            pltpu.VMEM((rows, width), bf16),
+            pltpu.VMEM((rows, width), bf16),
+            pltpu.VMEM((rows, 256), f32),
             pltpu.VMEM((rows, 256), bf16),
             pltpu.VMEM((rows, 128), bf16),
             pltpu.VMEM((rows, 128), bf16),
+            dma((9,)),
+            dma((9,)),
+            dma((rows // ROW,)),
+            dma((2, rows // ROW)),
+            dma,
         ],
-        compiler_params=pltpu.CompilerParams(vmem_limit_bytes=56 << 20),
+        compiler_params=pltpu.CompilerParams(
+            collective_id=5, has_side_effects=True, vmem_limit_bytes=63 << 20
+        ),
         cost_estimate=cost_of(30),
         name="attend",
-    )(lengths, x, small, first_all, table, block, order_row, order_col)
+    )(lengths, x, small, first_all, table, block, order, cotangent)
 
 
 def attend_back_kernel(
     lengths, mixed_grad, stream_qkv, mixed_stream, log_total, proj, first_all, table, block,
-    order_row, order_col, normed, wqkv, small, turn_grad,
-    proj_grad, wqkv_grad, small_grad,
+    order, normed, wqkv, small, turn_grad, out_part, expert_grads,
+    proj_grad, wqkv_grad, small_grad, out_sum, expert_pair,
     gain_grad, keys, values, out_grad, query_grad, key_grad, value_grad, attn_gain,
+    normed_s, proj_s, outs, far, near, leaving, landed, sum_send, sum_recv, load_sem,
+    far_w, near_w, near_in, own_w, y_send, y_recv,
 ):
     rows = proj.shape[0]
     blocks = rows // ROW
+    sums = RowSums(outs, far, near, leaving, landed, (sum_send, sum_recv))
+    loads = [
+        keep(src, dst, load_sem.at[k])
+        for k, (src, dst) in enumerate(((out_part, outs), (normed, normed_s), (proj, proj_s)))
+    ]
+    _, here, _, partner, right, left = neighbours()
+    y, side, core, _, _, _ = group_place()
+    ways = lax.rem(y + 1, 4), lax.rem(y + 3, 4)
+
+    def y_copy(index, src, dst, way):
+        return pltpu.make_async_remote_copy(
+            src_ref=src,
+            dst_ref=dst,
+            send_sem=y_send.at[index],
+            recv_sem=y_recv.at[index],
+            device_id={"dp": ways[way] * 4 + side * 2 + core},
+            device_id_type=MESH,
+        )
+
+    def far_y(way):
+        opposite = pl.ds(lax.rem(y + 2, 4) * 2, 2)
+        return y_copy(way, expert_grads.at[opposite, pl.ds(2 * way, 2)], far_w.at[way], way)
+
+    def near_y(way):
+        return y_copy(2 + way, near_w.at[way], near_in.at[way], way)
+
+    w_loads = [
+        keep(expert_grads.at[pl.ds(at * 2, 2)], dst, load_sem.at[3 + k])
+        for k, (at, dst) in enumerate(
+            ((ways[0], near_w.at[0]), (ways[1], near_w.at[1]), (y, own_w))
+        )
+    ]
+    meet([partner, here + right, here + left], [at * 4 + side * 2 + core for at in ways])
+    for way in range(2):
+        far_y(way).start()
+    loads[0].wait()
+    sums.begin(0)
+    sums.begin(1)
     q_gain, k_gain = head_gains(first_all)
     key_grad[...] = jnp.zeros_like(key_grad)
     value_grad[...] = jnp.zeros_like(value_grad)
@@ -823,7 +944,7 @@
     def _(b):
         at = pl.ds(pl.multiple_of(b * ROW, ROW), ROW)
         place = sublane((ROW, rows)) + b * ROW
-        moves = jnp.where(order_row[...] == place, 1.0, 0.0).astype(bf16)
+        moves = jnp.where(order[...] == place, 1.0, 0.0).astype(bf16)
         out_grad[at, :] = dot(moves, mixed_grad[...]).astype(bf16)
         kv = stream_qkv[at, 128:256].astype(f32)
         low = lane(kv.shape) < 64
@@ -848,14 +969,14 @@
         logs = logs[0:1], logs[64:65]
         place = lane((1, ROW)) + b * ROW
         start = sequence_start(place, lengths)
-        first = sequence_start(b * ROW, lengths) // CHUNK
-        last = (b * ROW + ROW - 1) // CHUNK + 1
-
-        def step(j, totals):
-            here = pl.ds(pl.multiple_of(j * CHUNK, CHUNK), CHUNK)
+
+        def step(begin, size, totals, diagonal):
+            here = pl.ds(pl.multiple_of(begin, ROW), size)
             k, v = keys[here, :], values[here, :]
-            key = sublane((CHUNK, ROW)) + j * CHUNK
-            allowed = (key <= place) & (key >= start)
+            key = sublane((size, ROW)) + begin
+            allowed = key >= start
+            if diagonal:
+                allowed = allowed & (key <= place)
             done = []
             kt, vt = key_grad[here, :], value_grad[here, :]
             for h in range(2):
@@ -871,12 +992,40 @@
             return tuple(done)
 
         none = jnp.zeros((128, ROW), f32)
-        t0, t1 = lax.fori_loop(first, last, step, (none, none))
+        totals = step(b * ROW, ROW, (none, none), True)
+        totals = lax.fori_loop(
+            0, b // 2, lambda j, t: step(j * CHUNK, CHUNK, t, False), totals
+        )
+        t0, t1 = lax.fori_loop(
+            0, lax.rem(b, 2), lambda j, t: step((b - 1) * ROW, ROW, t, False), totals
+        )
         grad = jnp.where(sublane((128, ROW)) < 64, t0, t1) * 0.125
         cos, sin = turned(table, block, b)
         cos, sin = jnp.transpose(cos), jnp.transpose(sin)
         swapped = jnp.concatenate([grad[32:64], grad[0:32], grad[96:128], grad[64:96]], axis=0)
         query_grad[:, at] = (grad * cos - swapped * sin).astype(bf16)
+
+        @pl.when(b == 2)
+        def _():
+            sums.go_on(0)
+
+        @pl.when(b == 3)
+        def _():
+            sums.go_on(1)
+
+        @pl.when(b == 4)
+        def _():
+            for way in range(2):
+                w_loads[way].wait()
+                far_y(way).wait_recv()
+                part = pl.ds(2 * way, 2)
+                total = near_w[way, :, part].astype(f32) + far_w[way].astype(f32)
+                near_w[way, :, part] = total.astype(bf16)
+                near_y(way).start()
+
+        @pl.when(b == 6)
+        def _():
+            sums.cross()
 
     gain_grad[...] = jnp.zeros_like(gain_grad)
     attn_gain[...] = jnp.zeros_like(attn_gain)
@@ -891,10 +1040,14 @@
         key = key * cos - swap_halves(key) * sin
         keys[at, :] = jnp.where(low, key, value + pltpu.roll(value, 64, 1)).astype(bf16)
 
+    for load in loads[1:]:
+        load.wait()
+
     @pl.loop(0, blocks)
     def _(b):
         at = pl.ds(pl.multiple_of(b * ROW, ROW), ROW)
-        moves = jnp.where(order_col[at, :] == lane((ROW, rows)), 1.0, 0.0).astype(bf16)
+        column = columns_of(order[:, at].astype(f32))[:, 0:1]
+        moves = jnp.where(column == lane((ROW, rows)).astype(f32), 1.0, 0.0).astype(bf16)
         dq = dot(moves, query_grad[...], ((1,), (1,)))
         dkv = dot(moves, keys[...])
 
@@ -905,8 +1058,8 @@
             result = r * (weighted - scaled * head_mean(weighted * scaled, heads))
             return result, jnp.sum(grad * scaled, axis=0, keepdims=True)
 
-        q_result, q_sum = back(dq, proj[at, 0:128], q_gain, 2)
-        k_result, k_sum = back(dkv, proj[at, 128:256], k_gain, 1)
+        q_result, q_sum = back(dq, proj_s[at, 0:128], q_gain, 2)
+        k_result, k_sum = back(dkv, proj_s[at, 128:256], k_gain, 1)
         q_low = q_result.astype(bf16)
         k_low = jnp.where(lane(dkv.shape) < 64, k_result, dkv).astype(bf16)
         proj_grad[at, 0:128] = q_low
@@ -914,13 +1067,13 @@
         gain_grad[0:1, :] += q_sum
         gain_grad[1:2, :] += k_sum
         part = dot(jnp.concatenate([q_low, k_low], axis=1), wqkv[...], ((1,), (1,)))
-        part = part * normed[at, :].astype(f32)
+        part = part * normed_s[at, :].astype(f32)
         attn_gain[0:1, :] += jnp.sum(part, axis=0, keepdims=True)
 
     @pl.loop(0, normed.shape[1] // 256)
     def _(c):
         at = pl.ds(pl.multiple_of(c * 256, 256), 256)
-        part = dot(normed[:, at], proj_grad[...], ((0,), (0,))).astype(bf16)
+        part = dot(normed_s[:, at], proj_grad[...], ((0,), (0,))).astype(bf16)
         own = pl.ds(c * 4, 4)
         wqkv_grad[own, 0] = part[:, 0:128].reshape(4, 64, 128)
         wqkv_grad[own, 1] = part[:, 128:256].reshape(4, 64, 128)
@@ -945,22 +1098,42 @@
     lines = [turn_grad[...], attn_gain[...] / small[0:1, :], jnp.concatenate(spots, axis=1)]
     lines.append(jnp.zeros((128 - 56, small.shape[1]), f32))
     small_grad[...] = jnp.transpose(jnp.concatenate(lines, axis=0))
+    out_sum[...] = sums.finish()
+    w_loads[2].wait()
+    for way in range(2):
+        near_y(way).wait_recv()
+    for k in range(2):
+        total = own_w[k].astype(f32) + near_in[0, k].astype(f32) + near_in[1, k].astype(f32)
+        expert_pair[k] = total.astype(bf16)
+    for way in range(2):
+        far_y(way).wait_send()
+        near_y(way).wait_send()
 
 
 def attend_back(
     lengths, mixed_grad, stream_qkv, mixed_stream, log_total, proj, first_all, table, block,
-    order_row, order_col, normed, wqkv, small, turn_grad,
+    order, normed, wqkv, small, turn_grad, out_part, expert_grads,
 ):
     rows, width = normed.shape
+    pair = (2,) + expert_grads.shape[1:]
+    half = (2, 2) + expert_grads.shape[2:]
     return pl.pallas_call(
         attend_back_kernel,
         out_shape=[
             jax.ShapeDtypeStruct((rows, 256), bf16),
             jax.ShapeDtypeStruct((GROUPS, 2, width // GROUPS, 128), bf16),
             jax.ShapeDtypeStruct((width, 128), f32),
+            jax.ShapeDtypeStruct(out_part.shape[1:], f32),
+            jax.ShapeDtypeStruct(pair, bf16),
         ],
-        in_specs=[pl.BlockSpec(memory_space=pltpu.SMEM)] + whole(14),
-        out_specs=whole(3),
+        in_specs=[pl.BlockSpec(memory_space=pltpu.SMEM)]
+        + whole(4)
+        + anywhere(1)
+        + whole(4)
+        + anywhere(1)
+        + whole(3)
+        + anywhere(2),
+        out_specs=whole(5),
         scratch_shapes=[
             pltpu.VMEM((8, 128), f32),
             pltpu.VMEM((rows, 128), bf16),
@@ -970,203 +1143,168 @@
             pltpu.VMEM((rows, 128), f32),
             pltpu.VMEM((rows, 128), f32),
             pltpu.VMEM((8, width), f32),
+            pltpu.VMEM(normed.shape, bf16),
+            pltpu.VMEM(proj.shape, f32),
+            pltpu.VMEM(out_part.shape, bf16),
+            *row_sum_scratch(out_part.shape[1], width),
+            pltpu.SemaphoreType.DMA((6,)),
+            pltpu.VMEM((2,) + half, bf16),
+            pltpu.VMEM((2,) + pair, bf16),
+            pltpu.VMEM((2,) + pair, bf16),
+            pltpu.VMEM(pair, bf16),
+            pltpu.SemaphoreType.DMA((4,)),
+            pltpu.SemaphoreType.DMA((4,)),
         ],
-        compiler_params=pltpu.CompilerParams(vmem_limit_bytes=56 << 20),
+        compiler_params=pltpu.CompilerParams(
+            collective_id=7, has_side_effects=True, vmem_limit_bytes=63 << 20
+        ),
         cost_estimate=cost_of(40),
         name="attend_back",
     )(
         lengths, mixed_grad, stream_qkv, mixed_stream, log_total, proj, first_all, table, block,
-        order_row, order_col, normed, wqkv, small, turn_grad,
+        order, normed, wqkv, small, turn_grad, out_part, expert_grads,
     )
 
 
 def experts_kernel(
-    rows_in, cotangent, hidden_in, routes, small, w,
-    cot_all, layer_out, copy_part, xs_out, us_out, inner_out, dgu_out,
-    xs, us, ys, weights, grads, acts, inner_s, dgu_s, ranks, x_buf, u_buf,
-    outs, far, near, leaving, landed, sum_send, sum_recv,
-    row_send, row_recv, sem, local_sem, out_sem,
+    rows_in, cot_in, tiny, small, w,
+    out_part, copy_part, xs_out, us_out, inner_out, dgu_out,
+    stage_x, stage_u, xs, us, ys, cs, weights, grads, inner_s, dgu_s, logits, picks, ranks, own,
+    in_sem, out_sem,
 ):
-    step = pl.program_id(0)
+    e = pl.program_id(0)
+    local = pl.num_programs(0)
     me = lax.axis_index("tensor")
-    blocks, held, width = xs.shape
-    local = held // CAP
-    hidden = inner_s.shape[1]
-    e = lax.rem(step, local)
+    blocks, _, width = xs.shape
+    hidden = inner_s.shape[2]
     here = pl.ds(pl.multiple_of(e * CAP, CAP), CAP)
-    slots = blocks * CAP
     group = blocks // 2
     tile = group * CAP
-    row_sems = row_send, row_recv
     long = ROW + 32
-
-    def fetch_rows(b, slot):
-        return pltpu.make_async_copy(rows_in.at[b], x_buf.at[slot], sem.at[0, slot])
-
-    def fetch_cot(b, slot):
-        return pltpu.make_async_copy(cot_all.at[b], u_buf.at[slot], sem.at[1, slot])
-
-    sums = RowSums(outs, far, near, leaving, landed, (sum_send, sum_recv))
-
-    def save_xs(b):
-        return pltpu.make_async_copy(xs.at[b], xs_out.at[b], out_sem.at[0, b])
-
-    def save_us(b):
-        return pltpu.make_async_copy(us.at[b], us_out.at[b], out_sem.at[1, b])
+    count = xs.shape[1] // CAP
+
+    def load_x(b):
+        return pltpu.make_async_copy(rows_in.at[b], stage_x.at[b], in_sem.at[0, b])
+
+    def load_u(b):
+        return pltpu.make_async_copy(cot_in.at[b], stage_u.at[b, 0:ROW], in_sem.at[1, b])
+
+    def save_slots(b):
+        return (
+            pltpu.make_async_copy(xs.at[b], xs_out.at[b], out_sem.at[0, b]),
+            pltpu.make_async_copy(us.at[b], us_out.at[b], out_sem.at[1, b]),
+        )
 
     def save_tile(k):
-        flat = pl.ds(pl.multiple_of(k * tile, tile), tile)
         return (
-            pltpu.make_async_copy(dgu_s.at[flat], dgu_out.at[flat], out_sem.at[2, k]),
-            pltpu.make_async_copy(inner_s.at[flat], inner_out.at[flat], out_sem.at[3, k]),
+            pltpu.make_async_copy(dgu_s.at[k], dgu_out.at[k], out_sem.at[2, k]),
+            pltpu.make_async_copy(inner_s.at[k], inner_out.at[k], out_sem.at[3, k]),
         )
 
-    def save_back(b):
-        flat = pl.ds(pl.multiple_of(b * long, 32), long)
-        return pltpu.make_async_copy(acts.at[flat], copy_part.at[b], out_sem.at[4, b])
+    def save_rows(b):
+        return (
+            pltpu.make_async_copy(stage_x.at[b], out_part.at[b], out_sem.at[4, b]),
+            pltpu.make_async_copy(stage_u.at[b, 0:long], copy_part.at[b], out_sem.at[5, b]),
+        )
+
+    def span(b):
+        return pl.ds(pl.multiple_of(b * ROW, ROW), ROW)
 
     def hits_of(b):
         slot = sublane((CAP, ROW))
-        return [ranks[b, i : i + 1, :] == slot for i in range(local)]
+        return [ranks[i : i + 1, span(b)] == slot for i in range(count)]
 
     def table_of(hits):
         return jnp.concatenate([jnp.where(hit, 1.0, 0.0).astype(bf16) for hit in hits], axis=0)
 
-    @pl.when(step == 0)
+    @pl.when(e == 0)
     def _():
-        _, near, _, partner, right, left = neighbours()
-        meet(others("tensor", blocks), [])
-        rows_begin(cotangent, cot_all, row_sems)
-        keep(cotangent, cot_all.at[me], local_sem.at[0])
-        fetch_rows(0, 0).start()
-        pick = (sublane((8, 32)) + me * local == lane((8, 32))) & (sublane((8, 32)) < local)
+        for b in range(blocks):
+            load_x(b).start()
+            load_u(b).start()
+        for b in range(blocks):
+            named = tiny[b, 80:96, :].astype(f32)
+            picks[:, b * ROW : b * ROW + 128] = named[0:8]
+            picks[:, b * ROW + 128 : (b + 1) * ROW] = named[8:16]
+        shape = (32, blocks * ROW)
+        expert = sublane(shape).astype(f32)
+        named = jnp.zeros(shape, f32)
+        for k in range(8):
+            named = jnp.where(picks[k : k + 1, :] == expert, 1.0, named)
+        pick = (sublane((8, 32)) + me * count == lane((8, 32))) & (sublane((8, 32)) < count)
         pick = jnp.where(pick, 1.0, 0.0)
         before = jnp.where(sublane((ROW, ROW)) < lane((ROW, ROW)), 1.0, 0.0).astype(bf16)
         router = small[8:40, :].astype(bf16)
-
-        @pl.loop(0, blocks)
-        def _(b):
-            slot = lax.rem(b, 2)
-
-            @pl.when(b + 1 < blocks)
-            def _():
-                fetch_rows(b + 1, 1 - slot).start()
-
-            fetch_rows(b, slot).wait()
-            x = x_buf[slot]
-            named = named_of(routes[b, 80:96, :])
-            gates = gates_of(named, dot(router, x, ((1,), (1,))))
-            own = lax.dot_general(
-                pick,
-                gates,
-                (((1,), (0,)), ((), ())),
-                precision=lax.Precision.HIGHEST,
-                preferred_element_type=f32,
-            )
-            place = jnp.where(named > 0.5, dot(named.astype(bf16), before), -1.0)
+        for b in range(blocks):
+            part = named[:, b * ROW : (b + 1) * ROW]
+            place = jnp.where(part > 0.5, dot(part.astype(bf16), before), -1.0)
             place = dot(pick.astype(bf16), place.astype(bf16))
-            ranks[b] = place.astype(jnp.int32)
-            hits = hits_of(b)
-            xs[b] = dot(table_of(hits), x).astype(bf16)
-            save_xs(b).start()
-            for i in range(local):
-                gate = jnp.sum(jnp.where(hits[i], own[i : i + 1], 0.0), axis=1, keepdims=True)
-                weights[b, pl.ds(i * CAP, CAP), :] = jnp.broadcast_to(gate, (CAP, 128))
-
-    @pl.when(step == 1)
-    def _():
-        rows_near(cotangent, cot_all, row_sems)
-
-    @pl.when(step == 3)
-    def _():
-        rows_far(cotangent, cot_all, row_sems)
-
-    @pl.when(step < local)
-    def _():
-        @pl.loop(0, 2)
-        def _(t):
-            part = pl.ds(t * group, group)
-            flat = pl.ds(pl.multiple_of(e * slots + t * tile, tile), tile)
-            x = xs[part, here, :].reshape(tile, width)
-            gate_act = dot(x, w[0, 0])
-            up_act = dot(x, w[0, 1])
-            acts[flat, 0:hidden] = gate_act.astype(bf16)
-            acts[flat, hidden : 2 * hidden] = up_act.astype(bf16)
-            inner = gate_act / (1.0 + jnp.exp(-gate_act)) * up_act
-            result = dot(inner.astype(bf16), w[0, 2], ((1,), (1,)))
-            gate = weights[part, here, :].reshape(tile, 128)[:, 0:1]
-            ys[part, here, :] = (gate * result).astype(bf16).reshape(group, CAP, width)
-
-    @pl.when(step == local)
-    def _():
-        @pl.loop(0, blocks)
-        def _(b):
-            outs[b] = dot(table_of(hits_of(b)), ys[b], ((0,), (0,))).astype(bf16)
-
-        rows_end(cotangent, cot_all, row_sems)
-        sums.begin(0)
-        sums.begin(1)
-        pltpu.make_async_copy(cotangent, cot_all.at[me], local_sem.at[0]).wait()
-        fetch_cot(0, 0).start()
-
-        @pl.loop(0, blocks)
-        def _(b):
-            slot = lax.rem(b, 2)
-
-            @pl.when(b + 1 < blocks)
-            def _():
-                fetch_cot(b + 1, 1 - slot).start()
-
-            table = table_of(hits_of(b))
-            fetch_cot(b, slot).wait()
-            us[b] = dot(table, u_buf[slot]).astype(bf16)
-            save_us(b).start()
-
-    @pl.when(step >= local)
-    def _():
-        @pl.loop(0, 2)
-        def _(t):
-            part = pl.ds(t * group, group)
-            flat = pl.ds(pl.multiple_of(e * slots + t * tile, tile), tile)
-            gate_act = acts[flat, 0:hidden].astype(f32)
-            up_act = acts[flat, hidden : 2 * hidden].astype(f32)
-            u = us[part, here, :].reshape(tile, width)
-            gate = weights[part, here, :].reshape(tile, 128)[:, 0:1]
-            pulled = dot(u, w[0, 2])
-            sig = 1.0 / (1.0 + jnp.exp(-gate_act))
-            silu = gate_act * sig
-            inner = silu * up_act
-            grad = jnp.sum(inner * pulled, axis=1, keepdims=True)
-            grads[part, here, :] = jnp.broadcast_to(grad, (tile, 128)).reshape(group, CAP, 128)
-            inner_s[flat, :] = (gate * inner).astype(bf16)
-            pulled = gate * pulled
-            dg = (pulled * up_act * (sig * (1.0 + gate_act * (1.0 - sig)))).astype(bf16)
-            du = (pulled * silu).astype(bf16)
-            dgu_s[flat, 0:hidden] = dg
-            dgu_s[flat, hidden : 2 * hidden] = du
-            for copy in save_tile(e * 2 + t):
-                copy.start()
-            copy_grad = dot(dg, w[0, 0], ((1,), (1,))) + dot(du, w[0, 1], ((1,), (1,)))
-            ys[part, here, :] = copy_grad.astype(bf16).reshape(group, CAP, width)
-
-    @pl.when(step == local)
-    def _():
-        sums.go_on(0)
-
-    @pl.when(step == local + 1)
-    def _():
-        sums.go_on(1)
-
-    @pl.when(step == 2 * local - 1)
-    def _():
-        sums.cross()
-
-        @pl.loop(0, blocks)
+            ranks[:, b * ROW : (b + 1) * ROW] = place.astype(jnp.int32)
+        for b in range(blocks):
+            load_x(b).wait()
+            logits[:, b * ROW : (b + 1) * ROW] = dot(router, stage_x[b], ((1,), (1,)))
+        gates = gates_of(named, logits[...])
+        own[...] = lax.dot_general(
+            pick,
+            gates,
+            (((1,), (0,)), ((), ())),
+            precision=lax.Precision.HIGHEST,
+            preferred_element_type=f32,
+        )
+        for b in range(blocks):
+            load_u(b).wait()
+
+        @pl.loop(0, blocks, unroll=2)
         def _(b):
             hits = hits_of(b)
-            row = sublane((32, ROW)) - me * local
+            table = table_of(hits)
+            xs[b] = dot(table, stage_x[b]).astype(bf16)
+            us[b] = dot(table, stage_u[b, 0:ROW]).astype(bf16)
+            for copy in save_slots(b):
+                copy.start()
+            for i in range(count):
+                gate = own[i : i + 1, span(b)]
+                gate = jnp.sum(jnp.where(hits[i], gate, 0.0), axis=1, keepdims=True)
+                weights[b, pl.ds(i * CAP, CAP), :] = jnp.broadcast_to(gate, (CAP, 128))
+
+    for t in range(2):
+        part = pl.ds(t * group, group)
+        x = xs[part, here, :].reshape(tile, width)
+        u = us[part, here, :].reshape(tile, width)
+        gate = weights[part, here, :].reshape(tile, 128)[:, 0:1]
+        gate_act = dot(x, w[0, 0])
+        up_act = dot(x, w[0, 1])
+        pulled = dot(u, w[0, 2])
+        sig = 1.0 / (1.0 + jnp.exp(-gate_act))
+        silu = gate_act * sig
+        inner = silu * up_act
+        result = dot(inner.astype(bf16), w[0, 2], ((1,), (1,)))
+        ys[part, here, :] = (gate * result).astype(bf16).reshape(group, CAP, width)
+        grad = jnp.sum(inner * pulled, axis=1, keepdims=True)
+        grads[part, here, :] = jnp.broadcast_to(grad, (tile, 128)).reshape(group, CAP, 128)
+        k = e * 2 + t
+        inner_s[k] = (gate * inner).astype(bf16)
+        pulled = gate * pulled
+        dg = (pulled * up_act * (sig * (1.0 + gate_act * (1.0 - sig)))).astype(bf16)
+        du = (pulled * silu).astype(bf16)
+        dgu_s[k, :, 0:hidden] = dg
+        dgu_s[k, :, hidden : 2 * hidden] = du
+        for copy in save_tile(k):
+            copy.start()
+        copy_grad = dot(dg, w[0, 0], ((1,), (1,))) + dot(du, w[0, 1], ((1,), (1,)))
+        cs[part, here, :] = copy_grad.astype(bf16).reshape(group, CAP, width)
+
+    @pl.when(e == local - 1)
+    def _():
+        @pl.loop(0, blocks, unroll=2)
+        def _(b):
+            hits = hits_of(b)
+            table = table_of(hits)
+            stage_x[b] = dot(table, ys[b], ((0,), (0,))).astype(bf16)
+            stage_u[b, 0:ROW] = dot(table, cs[b], ((0,), (0,))).astype(bf16)
+            row = sublane((32, ROW)) - me * count
             line = jnp.zeros((32, ROW), f32)
-            for i in range(local):
+            for i in range(count):
                 column = grads[b, pl.ds(i * CAP, CAP), :][:, 0:1]
                 total = jnp.sum(jnp.where(hits[i], column, 0.0), axis=0, keepdims=True)
                 line = jnp.where(row == i, total, line)
@@ -1174,71 +1312,59 @@
             both = jnp.concatenate(
                 [high, line - high, jnp.zeros((32, width - 2 * ROW), f32)], axis=1
             )
-            start = pl.multiple_of(b * long, 32)
-            acts[pl.ds(start, ROW), :] = dot(table_of(hits), ys[b], ((0,), (0,))).astype(bf16)
-            acts[pl.ds(pl.multiple_of(start + ROW, 32), 32), :] = both.astype(bf16)
-            save_back(b).start()
+            stage_u[b, ROW:long] = both.astype(bf16)
+            for copy in save_rows(b):
+                copy.start()
 
         for b in range(blocks):
-            save_xs(b).wait()
-            save_us(b).wait()
-            for copy in save_tile(b):
+            for copy in (*save_slots(b), *save_tile(b), *save_rows(b)):
                 copy.wait()
-            save_back(b).wait()
-        layer_out[...] = hidden_in[...] + sums.finish()
-
-
-def experts_part(rows_in, cotangent, hidden_in, routes, small, expert_full):
+
+
+def experts_part(rows_in, cot_in, tiny, small, expert_full):
     blocks, rows, width = rows_in.shape
     local, _, _, hidden = expert_full.shape
-    slots = blocks * CAP
     dma = pltpu.SemaphoreType.DMA
     like = jax.ShapeDtypeStruct
+    held = local * CAP
+    tile = blocks // 2 * CAP
     return pl.pallas_call(
         experts_kernel,
-        grid=(2 * local,),
+        grid=(local,),
         out_shape=[
             like((blocks, rows, width), bf16),
-            like((rows, width), f32),
             like((blocks, rows + 32, width), bf16),
-            like((blocks, local * CAP, width), bf16),
-            like((blocks, local * CAP, width), bf16),
-            like((local * slots, hidden), bf16),
-            like((local * slots, 2 * hidden), bf16),
+            like((blocks, held, width), bf16),
+            like((blocks, held, width), bf16),
+            like((2 * local, tile, hidden), bf16),
+            like((2 * local, tile, 2 * hidden), bf16),
         ],
         in_specs=anywhere(2)
-        + [pl.BlockSpec((rows, width), lambda s: (0, 0), pipeline_mode=pl.Buffered(1))]
         + whole(2)
-        + [pl.BlockSpec((1, 3, width, hidden), lambda s: (lax.rem(s, local), 0, 0, 0))],
-        out_specs=anywhere(1)
-        + [pl.BlockSpec((rows, width), lambda s: (0, 0), pipeline_mode=pl.Buffered(1))]
-        + anywhere(5),
+        + [pl.BlockSpec((1, 3, width, hidden), lambda s: (s, 0, 0, 0))],
+        out_specs=anywhere(6),
         scratch_shapes=[
-            pltpu.VMEM((blocks, local * CAP, width), bf16),
-            pltpu.VMEM((blocks, local * CAP, width), bf16),
-            pltpu.VMEM((blocks, local * CAP, width), bf16),
-            pltpu.VMEM((blocks, local * CAP, 128), f32),
-            pltpu.VMEM((blocks, local * CAP, 128), f32),
-            pltpu.VMEM((local * slots, 2 * hidden), bf16),
-            pltpu.VMEM((local * slots, hidden), bf16),
-            pltpu.VMEM((local * slots, 2 * hidden), bf16),
-            pltpu.VMEM((blocks, 8, ROW), jnp.int32),
-            pltpu.VMEM((2, rows, width), bf16),
-            pltpu.VMEM((2, rows, width), bf16),
             pltpu.VMEM((blocks, rows, width), bf16),
-            *row_sum_scratch(rows, width),
-            dma((9,)),
-            dma((9,)),
-            dma((2, 2)),
-            dma((1,)),
-            dma((5, blocks)),
+            pltpu.VMEM((blocks, rows + 32, width), bf16),
+            pltpu.VMEM((blocks, held, width), bf16),
+            pltpu.VMEM((blocks, held, width), bf16),
+            pltpu.VMEM((blocks, held, width), bf16),
+            pltpu.VMEM((blocks, held, width), bf16),
+            pltpu.VMEM((blocks, held, 128), f32),
+            pltpu.VMEM((blocks, held, 128), f32),
+            pltpu.VMEM((2 * local, tile, hidden), bf16),
+            pltpu.VMEM((2 * local, tile, 2 * hidden), bf16),
+            pltpu.VMEM((32, blocks * rows), f32),
+            pltpu.VMEM((8, blocks * rows), f32),
+            pltpu.VMEM((8, blocks * rows), jnp.int32),
+            pltpu.VMEM((8, blocks * rows), f32),
+            dma((2, blocks)),
+            dma((6, blocks)),
         ],
-        compiler_params=pltpu.CompilerParams(
-            collective_id=5, has_side_effects=True, vmem_limit_bytes=62 << 20
-        ),
-        cost_estimate=cost_of(65),
+        compiler_params=pltpu.CompilerParams(vmem_limit_bytes=63 << 20),
+        cost_estimate=cost_of(40),
         name="experts",
-    )(rows_in, cotangent, hidden_in, routes, small, expert_full)[1:]
+    )(rows_in, cot_in, tiny, small, expert_full)
 
 
 def weight_grads_kernel(
@@ -1288,7 +1414,6 @@
         meet([partner, here + right, here + left], [other["dp"]])
         load.wait()
         sums.begin(0)
-        sums.begin(1)
 
     both = dot(x[...].reshape(rows, -1), dgu[...], ((0,), (0,)))
     part = pl.ds(c * share, share)
@@ -1303,9 +1428,9 @@
     def _():
         sums.go_on(0)
 
-    @pl.when(step == 5)
+    @pl.when(step == 4)
     def _():
-        sums.go_on(1)
+        sums.begin(1)
 
     @pl.when((e > 0) & (c == parts - 1))
     def _():
@@ -1315,6 +1440,7 @@
     def _():
         add_core(e)
         sums.cross()
+        sums.go_on(1)
         back[...] = sums.finish()
         for k in range(made.shape[0]):
             for half in range(2):
@@ -1356,11 +1482,56 @@
             dma((local,)),
         ],
         compiler_params=pltpu.CompilerParams(
-            collective_id=6, has_side_effects=True, vmem_limit_bytes=62 << 20
+            collective_id=6, has_side_effects=True, vmem_limit_bytes=63 << 20
         ),
         cost_estimate=cost_of(45),
         name="weight_grads",
     )(xs, us, inner, dgu, copy_part)
+
+
+def finish_kernel(
+    hidden, out_sum, tokens_sum, wqkv_sum, wo_sum, small_sum, head_sum, expert_pair, expert_far,
+    layer_out, grad_tokens, attn_grad, ffn_grad, router_grad, query_grad, key_grad, value_grad,
+    output_grad, query_gains, key_gains, gate_grad, up_grad, down_grad,
+):
+    layer_out[...] = hidden[...] + out_sum[...]
+    grad_tokens[...] = tokens_sum[...]
+    small = small_sum[...]
+    columns = jnp.transpose(small)
+    attn_grad[...] = columns[40:41, :]
+    ffn_grad[...] = columns[0:1, :]
+    router_grad[...] = pltpu.roll(small, 120, 1)[:, 0:32]
+    query_grad[...] = wqkv_sum[:, 0:128]
+    key_grad[...] = wqkv_sum[:, 128:192]
+    value_grad[...] = pltpu.roll(wqkv_sum[:, 128:256], 64, 1)[:, 0:64]
+    output_grad[...] = wo_sum[...]
+    heads = jnp.transpose(head_sum[...])
+    query_gains[...] = heads[48:50, 0:4]
+    key_gains[...] = heads[50:51, 0:4]
+    _, side, _, _, _, _ = group_place()
+    for k, out in enumerate((gate_grad, up_grad, down_grad)):
+        out[...] = expert_pair[side, :, k].astype(f32) + expert_far[:, k].astype(f32)
+
+
+def finish(
+    hidden, out_sum, tokens_sum, wqkv_sum, wo_sum, small_sum, head_sum, expert_pair, expert_far
+):
+    rows = small_sum.shape[0]
+    shard = wo_sum.shape[0]
+    expert = (expert_far.shape[0],) + expert_far.shape[2:]
+    shapes = (
+        hidden.shape, hidden.shape, (1, rows), (1, rows), (rows, 32), (shard, 128), (shard, 64),
+        (shard, 64), (shard, 128), (2, 4), (1, 4), expert, expert, expert,
+    )
+    return pl.pallas_call(
+        finish_kernel,
+        out_shape=[jax.ShapeDtypeStruct(shape, f32) for shape in shapes],
+        in_specs=whole(9),
+        out_specs=whole(len(shapes)),
+        compiler_params=pltpu.CompilerParams(vmem_limit_bytes=63 << 20),
+        cost_estimate=cost_of(5),
+        name="finish",
+    )(hidden, out_sum, tokens_sum, wqkv_sum, wo_sum, small_sum, head_sum, expert_pair, expert_far)
 
 
 def per_device(
@@ -1388,7 +1559,7 @@
     own_experts = jnp.stack([w_gate, w_up, w_down.transpose(0, 2, 1)], axis=1)
     expert_full = lax.all_gather(own_experts, "dp", axis=2, tiled=True)
     tokens_all, qkv_cols, tiny_all, first_all, rest_all, small, routes_own = opening(
-        tokens, w_query, w_key, w_value, w_output, attn_gain[None], ffn_gain[None], router,
+        tokens, w_query, w_key, w_value, w_output.T, attn_gain[None], ffn_gain[None], router,
         query_gain, key_gain, routes.T,
     )
     first_all = first_all.reshape((GROUPS,) + first_all.shape[3:])
@@ -1399,10 +1570,11 @@
     starts = (np.arange(group_rows // ROW) * ROW)[:, None] * frequency
     table = np.stack([np.cos(within), np.sin(within)]).astype(np.float32)
     block = np.stack([np.cos(starts), np.sin(starts)]).astype(np.float32)
-    order_row, order_col = token_order, token_order.T
-    normed_all, proj, stream_qkv, mixed_stream, log_total, mixed, wqkv = attend(
+    (
+        normed_all, proj, stream_qkv, mixed_stream, log_total, mixed, wqkv, cot_all,
+    ) = attend(
         lengths[0], tokens_all.reshape(group_rows, width), small, first_all, table, block,
-        order_row, order_col,
+        token_order, cotangent,
     )
     mixed_own, hidden, normed2_all, done = middle(
         mixed.reshape(RANKS, rows, 128), rest_all, tokens, small
@@ -1410,42 +1582,47 @@
 
     qkv_cols, _ = lax.optimization_barrier((qkv_cols, done))
     wqkv_all = lax.all_gather(qkv_cols, "dp", axis=0, tiled=False)
-    layer_out, copy_part, xs, us, inner, dgu = experts_part(
-        normed2_all, cotangent, hidden, tiny_all, small, expert_full
-    )
-    back, expert_grads = weight_grads(xs, us, inner, dgu, copy_part)
-    groups = [[core + 2 * k for k in range(GROUPS // 2)] for core in range(2)]
-    expert_sums = lax.psum_scatter(
-        expert_grads, "dp", scatter_dimension=0, axis_index_groups=groups, tiled=False
-    ).astype(f32)
+    out_part, copy_part, xs, us, inner, dgu = experts_part(
+        normed2_all, cot_all, tiny_all, small, expert_full
+    )
+    back, expert_grads = weight_grads(
+        xs, us, inner.reshape(-1, inner.shape[2]), dgu.reshape(-1, dgu.shape[2]), copy_part
+    )
     hidden_grad, mixed_grad, wo_grad, turn_grad = turn(
         back, hidden, cotangent, routes_own, small, mixed_own, rest_all
     )
 
-    proj_grad, wqkv_grad, small_grad = attend_back(
+    proj_grad, wqkv_grad, small_grad, out_sum, expert_pair = attend_back(
         lengths[0], mixed_grad.reshape(group_rows, 128), stream_qkv, mixed_stream, log_total,
-        proj, first_all, table, block, order_row, order_col, normed_all, wqkv, small, turn_grad,
-    )
-    grad_tokens, wqkv_sum, wo_sum, small_sum, head_sum = closing(
+        proj, first_all, table, block, token_order, normed_all, wqkv, small, turn_grad, out_part,
+        expert_grads,
+    )
+    grad_tokens, wqkv_sum, wo_sum, small_sum, head_sum, expert_far = closing(
         proj_grad.reshape(RANKS, rows, 256), wo_grad.reshape((4, 2, 2) + wo_grad.shape[1:]),
         wqkv_grad.reshape((4, 2, 2) + wqkv_grad.shape[1:]), small_grad.reshape(4, 2, 2, -1, 128),
-        wqkv_all, tokens, small, hidden_grad,
+        wqkv_all, tokens, small, hidden_grad, expert_pair,
+    )
+    (
+        layer_out, grad_tokens, attn_grad, ffn_grad, router_grad, query_grad, key_grad, value_grad,
+        output_grad, query_gains, key_gains, gate_grad, up_grad, down_grad,
+    ) = finish(
+        hidden, out_sum, grad_tokens, wqkv_sum, wo_sum, small_sum, head_sum, expert_pair, expert_far
     )
     return (
         layer_out,
         grad_tokens,
-        small_sum[:, 40],
-        small_sum[:, 0],
-        small_sum[:, 8:40],
-        wqkv_sum[:, :128],
-        wqkv_sum[:, 128:192],
-        wqkv_sum[:, 192:256],
-        wo_sum.T,
-        head_sum[:4, 48:50].T,
-        head_sum[:4, 50:51].T,
-        expert_sums[:, 0],
-        expert_sums[:, 1],
-        expert_sums[:, 2].transpose(0, 2, 1),
+        attn_grad[0],
+        ffn_grad[0],
+        router_grad,
+        query_grad,
+        key_grad,
+        value_grad,
+        output_grad.T,
+        query_gains,
+        key_gains,
+        gate_grad,
+        up_grad,
+        down_grad.transpose(0, 2, 1),
     )
 
 

time: 423 us -> 390 us (0.922); the launches traced: 416 us -> 390 us
  local copies, waits for them, and re-layouts: 34.2 us -> 0 us
  Pallas kernels: 364 us -> 374 us
    pallas_call x1 -> x2, Pallas kernels: 78.8 us -> 39.8 us  [the longest x1 35.2 us: experts_part(): pl.pallas_call(experts_kernel, grid=(local,), out_shape=[like((blocks, ro...]
    unnamed x67 -> x0, local copies, waits for them, and re-layouts: 23.4 us -> none
    pallas_call x1, Pallas kernels: 29.9 us -> 50.8 us  [attend(): pl.pallas_call(attend_kernel, out_shape=[jax.ShapeDtypeStruct((rows, widt...]
    pallas_call x1, Pallas kernels: 40.6 us -> 57.3 us  [attend_back(): pl.pallas_call(attend_back_kernel, out_shape=[jax.ShapeDtypeStruct((rows,...]
    slice x5 -> x0, local copies, waits for them, and re-layouts: 7.24 us -> none  [the longest x1 1.53 us: per_device(): wqkv_sum[:, 192:256]]
    pallas_call x1, Pallas kernels: 56.5 us -> 62.3 us  [opening(): pl.pallas_call(opening_kernel, out_shape=[like((RANKS,) + tokens.shape, b...]
  transfers between devices with their start and end apart: 3 -> 2, of which waited for: 0 -> 0; matrix products, arithmetic and copies ran while one was open for 3% -> 0% of each run, Pallas kernels for 88% -> 83%
where the time goes in v4:
time: 390 us
  Pallas kernels  374 us (96%)
  between operations  14.1 us (4%)
    pallas_call x1, Pallas kernels, opening(): pl.pallas_call(opening_kernel, out_shape=[like((RANKS,) + tokens.shape, b...  62.3 us
    pallas_call x1, Pallas kernels, attend_back(): pl.pallas_call(attend_back_kernel, out_shape=[jax.ShapeDtypeStruct((rows,...  57.3 us
    pallas_call x1, Pallas kernels, middle(): pl.pallas_call(middle_kernel, out_shape=[jax.ShapeDtypeStruct(mixed.shape...  53.4 us
    pallas_call x1, Pallas kernels, attend(): pl.pallas_call(attend_kernel, out_shape=[jax.ShapeDtypeStruct((rows, widt...  50.8 us
    pallas_call x1, Pallas kernels, weight_grads(): pl.pallas_call(weight_grads_kernel, grid=(local, width // col), out_shape...  47.3 us
    pallas_call x1, Pallas kernels, closing(): pl.pallas_call(closing_kernel, out_shape=[jax.ShapeDtypeStruct(hidden_gra...  47.2 us
    pallas_call x1, Pallas kernels, experts_part(): pl.pallas_call(experts_kernel, grid=(local,), out_shape=[like((blocks, ro...  35.2 us
    pallas_call x1, Pallas kernels, turn(): pl.pallas_call(turn_kernel, out_shape=[jax.ShapeDtypeStruct((rows, width)...  15.5 us
  transfers between devices with their start and end apart: 2, of which 0 were waited for; matrix products, arithmetic and copies ran while one was open for 0% of the time, Pallas kernels for 83%

profile of v4, /device:TPU:0, one launch (start us, length us, event | category | flops | bytes accessed | tf_op | source)
XLA Modules:
  0.0 390.1 jit_solution(4932818392818494404)
XLA Ops:
  7.2 0.0 all-gather.4.cloned.1.call-start
  7.2 2.1 pad_maximum_fusion
  9.3 0.0 all-gather.4.cloned.1.call-update
  9.3 0.0 all-gather.6.cloned.1.call-start
  9.4 62.3 %opening.1 = (bf16[8,256,1024]{2,1,0:T(8,128)(2,1)}, bf16[8,128,128]{2,1,0:T(8,128)(2,1)}, bf16[8,96,128]{2,1,0:T(8,128)(2,1)}, bf16[4,2,2,144,128]{4,3,2,1,0:T(...) custom-call(bf16[256,1024]{1,0:T(8,128)(2,1)} %tokens.5, ...), custom_call_target="tpu_custom_call" | custom-call | flops 54999998464 | bytes 1048576 | tf_op jit(solution)/shard_map/opening/pallas_call | solution.py:336
  71.7 0.0 all-gather.6.cloned.1.call-update
  71.7 50.8 %attend.1 = (bf16[2048,1024]{1,0:T(8,128)(2,1)}, f32[2048,256]{1,0:T(8,128)}, bf16[2048,256]{1,0:T(8,128)(2,1)}, bf16[2048,128]{1,0:T(8,128)(2,1)}, f32[2048,128...) custom-call(s32[3]{0:T(128)} %bitcast.34, ...), custom_call_target="tpu_custom_call" | custom-call | flops 32999999488 | bytes 1048576 | tf_op jit(solution)/shard_map/attend/pallas_call | solution.py:856
  122.5 53.4 %middle.1 = (bf16[8,256,128]{2,1,0:T(8,128)(2,1)}, f32[256,1024]{1,0:T(8,128)}, bf16[8,256,1024]{2,1,0:T(8,128)(2,1)}, f32[8,128]{1,0:T(8,128)}) custom-call(bf16[8,256,128]{2,1,0:T(8,128)(2,1)} %bitcast.49, bf16[16,8,80,128]{3,2,1,0:T(8,128)(2,1)} %bitcast.38, bf16[256,1024]{1,0:T(8,128)(2,1)} %tokens.5, f32[40,1024]{1,0:T(8,128)} %get-tuple-element.70.small), custom_call_target="tpu_custom_call" | custom-call | flops 44000002048 | bytes 1048576 | tf_op jit(solution)/shard_map/middle/pallas_call | solution.py:406
  175.9 0.0 all-gather.4.cloned.1.call-done.w
  176.0 35.2 %experts.1 = (bf16[8,256,1024]{2,1,0:T(8,128)(2,1)}, bf16[8,288,1024]{2,1,0:T(8,128)(2,1)}, bf16[8,320,1024]{2,1,0:T(8,128)(2,1)}, bf16[8,320,1024]{2,1,0:T(8,12...) custom-call(bf16[8,256,1024]{2,1,0:T(8,128)(2,1)} %get-tuple-element.75.rows_in, ...), custom_call_target="tpu_custom_call" | custom-call | flops 44000002048 | bytes 1048576 | tf_op jit(solution)/shard_map/experts/pallas_call | solution.py:1331
  211.2 47.3 %weight_grads.1 = (f32[288,1024]{1,0:T(8,128)}, bf16[8,4,3,64,512]{4,3,2,1,0:T(8,128)(2,1)}) custom-call(bf16[8,320,1024]{2,1,0:T(8,128)(2,1)} %get-tuple-element.78.x, bf16[8,320,1024]{2,1,0:T(8,128)(2,1)} %get-tuple-element.79.u, bf16[2560,512]{1,0:T(8,128)(2,1)} %bitcast.40, bf16[2560,1024]{1,0:T(8,128)(2,1)} %bitcast.36, ...), custom_call_target="tpu_custom_call" | custom-call | flops 49500000256 | bytes 1048576 | tf_op jit(solution)/shard_map/weight_grads/pallas_call | solution.py:1459
  258.5 15.5 %turn.1 = (f32[256,1024]{1,0:T(8,128)}, bf16[8,256,128]{2,1,0:T(8,128)(2,1)}, bf16[16,8,64,128]{3,2,1,0:T(8,128)(2,1)}, f32[40,1024]{1,0:T(8,128)}) custom-call(f32[288,1024]{1,0:T(8,128)} %get-tuple-element.83.back, f32[256,1024]{1,0:T(8,128)} %get-tuple-element.74.hidden, bf16[256,1024]{1,0:T(8,128)(2,1)} %cotangent.3, ...), custom_call_target="tpu_custom_call" | custom-call | flops 16499999744 | bytes 1048576 | tf_op jit(solution)/shard_map/turn/pallas_call | solution.py:505
  274.0 57.3 %attend_back.1 = (bf16[2048,256]{1,0:T(8,128)(2,1)}, bf16[16,2,64,128]{3,2,1,0:T(8,128)(2,1)}, f32[1024,128]{1,0:T(8,128)}, f32[256,1024]{1,0:T(8,128)}, bf16[2,4,3,64,512]{4,3,2,1,0:T(8,128)(2,1)}) custom-call(s32[3]{0:T(128)} %bitcast.35, bf16[2048,128]{1,0:T(8,128)(2,1)} %bitcast.48, bf16[2048,256]{1,0:T(8,128)(2,1)} %get-tuple-element.87.stream_qkv, ...), custom_call_target="tpu_custom_call" | custom-call | flops 44000002048 | bytes 1048576 | tf_op jit(solution)/shard_map/attend_back/pallas_call | solution.py:1120
  331.4 0.0 all-gather.6.cloned.1.call-done
  331.4 47.2 %closing.1 = (f32[256,1024]{1,0:T(8,128)}, f32[64,256]{1,0:T(8,128)}, f32[64,128]{1,0:T(8,128)}, f32[8,128]{1,0:T(8,128)}, f32[8,128]{1,0:T(8,128)}, /*index=5*/bf16[4,3,64,512]{3,2,1,0:T(8,128)(2,1)}) custom-call(bf16[8,256,256]{2,1,0:T(8,128)(2,1)} %bitcast.42, bf16[4,2,2,8,64,128]{5,4,3,2,1,0:T(8,128)(2,1)} %bitcast.41, ...), custom_call_target="tpu_custom_call" | custom-call | flops 49500000256 | bytes 1048576 | tf_op jit(solution)/shard_map/closing/pallas_call | solution.py:645
  378.6 4.6 %finish.1 = (f32[256,1024]{1,0:T(8,128)}, f32[256,1024]{1,0:T(8,128)}, f32[1,8]{1,0:T(1,128)}, f32[1,8]{1,0:T(1,128)}, f32[8,32]{1,0:T(8,128)}, /*index=5*/f32[6...) custom-call(f32[256,1024]{1,0:T(8,128)} %get-tuple-element.74.hidden, ...), custom_call_target="tpu_custom_call" | custom-call | flops 5500000256 | bytes 1048576 | tf_op jit(solution)/shard_map/finish/pallas_call | solution.py:1526
Async XLA Ops:
  7.2 168.8 %all-gather.4.cloned.1.call-start = ((), (), s32[]{:S(2)}) async-start(), calls=%async_computation | async-start | bytes 13369344 | tf_op jit(solution)/shard_map/all_gather | solution.py:1560
  9.3 322.1 %all-gather.6.cloned.1.call-start = ((), (), s32[]{:S(2)}) async-start(), calls=%async_computation.1 | async-start | bytes 4456448 | tf_op jit(solution)/shard_map/all_gather | solution.py:1584
Sparse Core Ops, SparseCore 0:
  11.0 121.1 all-gather.3
  134.7 54.1 all-gather.5
